TPU v7x, 512 devices: a whole 4x8x8 slice. The times are simulated.
512 devices in a mesh: section: 8 (over y), row: 8 (over x, core), col: 8 (over z).
Axes of the slice: x: 4, y: 8, z: 8, core: 2. Of those that a mesh axis runs over, the one named last changes fastest.
Arguments:
- features: bfloat16 [12, 32, 96, 1024], P(None, 'row', None, 'col'), may hold values from -6 to 6
- conv_weight: bfloat16 [8, 3, 3, 3, 96, 96], P('section'), may hold values from -0.125 to 0.125
- norm_gain: float32 [8, 96], P('section'), may hold values from 0.1 to 1.9
- conv_bias: float32 [8, 96], P('section'), may hold values from -2 to 2
- cached: bfloat16 [8, 2, 32, 96, 1024], P('section', None, 'row', None, 'col'), may hold values from -4 to 4
Outputs:
- section_out: bfloat16 [8, 12, 32, 96, 1024], P('section', None, 'row', None, 'col')
All inputs are finite; a program needn't handle non-finite values.
Results may differ from a plain program's by a relative error of at most 0.013.
Values may be sent and summed in bfloat16 or wider, within the bound.
No kernel may reach another device: no remote copies, remote signals or barrier semaphores. Data moves between devices by JAX's collectives and lax.ppermute only.
A program may use at most 64 MiB of HBM per device.

v0:
```python
import jax
import jax.numpy as jnp
from jax import lax
from jax.sharding import PartitionSpec as P

GROUP_FR = 4


def extended_2(cells, sides, width):
    for axis, dim in sides:
        count = lax.axis_size(axis)
        ends = count - 1
        head = lax.slice_in_dim(cells, 0, width, axis=dim)
        tail = lax.slice_in_dim(cells, cells.shape[dim] - width, cells.shape[dim], axis=dim)
        cells = jnp.concatenate(
            [
                lax.ppermute(tail, axis, [(i, (i + 1) % count) for i in range(ends)]),
                cells,
                lax.ppermute(head, axis, [((i + 1) % count, i) for i in range(ends)]),
            ],
            axis=dim,
        )
    return cells


def from_behind(block, axis, distance):
    devices = range(lax.axis_size(axis))
    route = [(i - distance, i) for i in devices if i - distance in devices]
    return lax.ppermute(block, axis, route)


def prepare(inputs, gain):
    values = inputs.astype(jnp.float32)
    meansq = jnp.mean(values * values, axis=2, keepdims=True)
    normed = values * lax.rsqrt(meansq + 1e-06) * gain[None, None, :, None]
    return jax.nn.silu(normed).astype(jnp.bfloat16)


def convolve(extended, kernel):
    frames = extended.shape[0] - 2
    rows = extended.shape[1] - 2
    cols = extended.shape[3] - 2
    total = jnp.zeros((frames, rows, kernel.shape[4], cols), jnp.float32)
    for tap_time in range(3):
        for tap_row in range(3):
            for tap_col in range(3):
                window = extended[
                    tap_time : tap_time + frames,
                    tap_row : tap_row + rows,
                    :,
                    tap_col : tap_col + cols,
                ]
                total = total + jnp.einsum(
                    "fhcw,co->fhow",
                    window,
                    kernel[tap_time, tap_row, tap_col],
                    preferred_element_type=jnp.float32,
                )
    return total


def body(features, conv_weight, norm_gain, conv_bias, cached):
    sections = lax.axis_size("section")
    place = lax.axis_index("section")
    kernel = conv_weight[0]
    gain = norm_gain[0]
    offset_bias = conv_bias[0][None, None, :, None]
    frames_all = features.shape[0]
    step_frames = GROUP_FR
    count_steps = frames_all // step_frames
    rounds = count_steps + sections - 1
    stored_start = cached[0]
    shape_step = (step_frames,) + features.shape[1:]

    def advance(moment, carry):
        incoming, stored, saved = carry
        item = moment - place
        active = jnp.logical_and(item >= 0, item < count_steps)
        slot = jnp.clip(item, 0, count_steps - 1) * step_frames
        fresh = lax.dynamic_slice_in_dim(features, slot, step_frames, 0)
        inputs = jnp.where(place == 0, fresh, incoming)
        normed = prepare(inputs, gain)
        joined = jnp.concatenate([stored, normed], axis=0)
        extended = extended_2(joined, (("row", 1), ("col", 3)), 1)
        renewed = normed[-2:]

        def compute(source):
            return (inputs.astype(jnp.float32) + convolve(source, kernel) + offset_bias).astype(
                jnp.bfloat16
            )

        def skipped(source):
            return jnp.zeros(shape_step, jnp.bfloat16)

        output = lax.cond(active, compute, skipped, extended)
        stored = jnp.where(active, renewed, stored)
        previous = lax.dynamic_slice_in_dim(saved, slot, step_frames, 0)
        saved = lax.dynamic_update_slice_in_dim(saved, jnp.where(active, output, previous), slot, 0)
        incoming = from_behind(output, "section", 1)
        return (incoming, stored, saved)

    start = (
        jnp.zeros(shape_step, jnp.bfloat16),
        stored_start,
        jnp.zeros(features.shape, jnp.bfloat16),
    )
    final = lax.fori_loop(0, rounds, advance, start)
    return final[2][None]


def solution(mesh):
    return jax.shard_map(
        body,
        mesh=mesh,
        in_specs=(
            P(None, "row", None, "col"),
            P("section", None, None, None, None, None),
            P("section", None),
            P("section", None),
            P("section", None, "row", None, "col"),
        ),
        out_specs=P("section", None, "row", None, "col"),
        check_vma=False,
    )
```

profile of v0, /device:TPU:250, one launch (start us, length us, event | category | flops | bytes accessed | tf_op | source)
XLA Modules:
  0.0 659.6 jit_solution(18244247679520117159)
XLA Ops:
  4.6 654.9 %while.18 = (s32[]{:T(128)}, bf16[4,4,96,128]{3,2,1,0:T(8,128)(2,1)S(1)}, bf16[2,4,96,128]{2,1,3,0:T(4,128)(2,1)S(1)}, bf16[12,4,96,128]{3,2,1,0:T(8,128)(2,1)},...) while((s32[]{:T(128)}, ...), condition=%wide.region_4.5_spmd, body=%wide.region_0.4_spmd.sunk | while | flops 1037143040 | bytes 82682376 | solution.py:107
  16.2 3.8 collective-permute-done.1
  24.8 5.5 collective-permute-start.3
  38.8 8.6 %collective-permute-done.4 = bf16[4,4,96,128]{3,2,1,0:T(8,128)(2,1)S(1)} collective-permute-done((bf16[4,4,96,128]{3,2,1,0:T(8,128)(2,1)}, bf16[4,4,96,128]{3,2,1,0:T(8,128)(2,1)S(1)}, u32[]{:S(2)}, u32[]{:S(2)}) %collective-permute-start.4) | collective-permute-done | bytes 393248 | tf_op jit(solution)/shard_map/while/body/eval_jaxpr/ppermute | solution.py:29
  58.9 3.8 collective-permute-done.1
  67.4 5.1 collective-permute-start.3
  81.1 8.3 %collective-permute-done.4 = bf16[4,4,96,128]{3,2,1,0:T(8,128)(2,1)S(1)} collective-permute-done((bf16[4,4,96,128]{3,2,1,0:T(8,128)(2,1)}, bf16[4,4,96,128]{3,2,1,0:T(8,128)(2,1)S(1)}, u32[]{:S(2)}, u32[]{:S(2)}) %collective-permute-start.4) | collective-permute-done | bytes 393248 | tf_op jit(solution)/shard_map/while/body/eval_jaxpr/ppermute | solution.py:29
  100.9 3.8 collective-permute-done.1
  109.4 5.1 collective-permute-start.3
  123.1 7.2 %collective-permute-done.4 = bf16[4,4,96,128]{3,2,1,0:T(8,128)(2,1)S(1)} collective-permute-done((bf16[4,4,96,128]{3,2,1,0:T(8,128)(2,1)}, bf16[4,4,96,128]{3,2,1,0:T(8,128)(2,1)S(1)}, u32[]{:S(2)}, u32[]{:S(2)}) %collective-permute-start.4) | collective-permute-done | bytes 393248 | tf_op jit(solution)/shard_map/while/body/eval_jaxpr/ppermute | solution.py:29
  141.9 3.8 collective-permute-done.1
  150.4 5.1 collective-permute-start.3
  164.0 7.3 %collective-permute-done.4 = bf16[4,4,96,128]{3,2,1,0:T(8,128)(2,1)S(1)} collective-permute-done((bf16[4,4,96,128]{3,2,1,0:T(8,128)(2,1)}, bf16[4,4,96,128]{3,2,1,0:T(8,128)(2,1)S(1)}, u32[]{:S(2)}, u32[]{:S(2)}) %collective-permute-start.4) | collective-permute-done | bytes 393248 | tf_op jit(solution)/shard_map/while/body/eval_jaxpr/ppermute | solution.py:29
  191.4 5.1 collective-permute-start.3
  205.0 8.4 %collective-permute-done.4 = bf16[4,4,96,128]{3,2,1,0:T(8,128)(2,1)S(1)} collective-permute-done((bf16[4,4,96,128]{3,2,1,0:T(8,128)(2,1)}, bf16[4,4,96,128]{3,2,1,0:T(8,128)(2,1)S(1)}, u32[]{:S(2)}, u32[]{:S(2)}) %collective-permute-start.4) | collective-permute-done | bytes 393248 | tf_op jit(solution)/shard_map/while/body/eval_jaxpr/ppermute | solution.py:29
  225.0 3.8 collective-permute-done.1
  233.5 5.1 collective-permute-start.3
  247.2 8.4 %collective-permute-done.4 = bf16[4,4,96,128]{3,2,1,0:T(8,128)(2,1)S(1)} collective-permute-done((bf16[4,4,96,128]{3,2,1,0:T(8,128)(2,1)}, bf16[4,4,96,128]{3,2,1,0:T(8,128)(2,1)S(1)}, u32[]{:S(2)}, u32[]{:S(2)}) %collective-permute-start.4) | collective-permute-done | bytes 393248 | tf_op jit(solution)/shard_map/while/body/eval_jaxpr/ppermute | solution.py:29
  267.2 3.8 collective-permute-done.1
  275.7 5.1 collective-permute-start.3
  289.3 170.8 %collective-permute-done.4 = bf16[4,4,96,128]{3,2,1,0:T(8,128)(2,1)S(1)} collective-permute-done((bf16[4,4,96,128]{3,2,1,0:T(8,128)(2,1)}, bf16[4,4,96,128]{3,2,1,0:T(8,128)(2,1)S(1)}, u32[]{:S(2)}, u32[]{:S(2)}) %collective-permute-start.4) | collective-permute-done | bytes 393248 | tf_op jit(solution)/shard_map/while/body/eval_jaxpr/ppermute | solution.py:29
  471.7 3.8 collective-permute-done.1
  480.2 5.1 collective-permute-start.3
  489.7 25.5 %conditional.2 = (bf16[4,4,96,128]{3,2,1,0:T(8,128)(2,1)}) conditional(s32[]{:T(128)} %convert_element_type.58, () %tuple.55, (bf16[4,4,96,128]{2,1,3,0:T(4,128)(2,1)}, bf16[3,3,3,96,96]{3,4,2,1,0:T(8,128)(2,1)}, bf16[6,6,96,130]{2,1,3,0:T(8,128)(2,1)}, bf16[6,6,96,128]{2,1,3,0:T(8,128)(2,1)}, bf16[6,4,96,128]{2,1,3,0:T(4,128)(2,1)}, ...), branch_computations={%region_2.2_spmd, %region_3.3_spmd} | conditional | flops 1025114112 | bytes 62975552 | solution.py:95
  518.7 8.3 %collective-permute-done.4 = bf16[4,4,96,128]{3,2,1,0:T(8,128)(2,1)S(1)} collective-permute-done((bf16[4,4,96,128]{3,2,1,0:T(8,128)(2,1)}, bf16[4,4,96,128]{3,2,1,0:T(8,128)(2,1)S(1)}, u32[]{:S(2)}, u32[]{:S(2)}) %collective-permute-start.4) | collective-permute-done | bytes 393248 | tf_op jit(solution)/shard_map/while/body/eval_jaxpr/ppermute | solution.py:29
  538.6 3.8 collective-permute-done.1
  547.1 5.1 collective-permute-start.3
  556.6 25.5 %conditional.2 = (bf16[4,4,96,128]{3,2,1,0:T(8,128)(2,1)}) conditional(s32[]{:T(128)} %convert_element_type.58, () %tuple.55, (bf16[4,4,96,128]{2,1,3,0:T(4,128)(2,1)}, bf16[3,3,3,96,96]{3,4,2,1,0:T(8,128)(2,1)}, bf16[6,6,96,130]{2,1,3,0:T(8,128)(2,1)}, bf16[6,6,96,128]{2,1,3,0:T(8,128)(2,1)}, bf16[6,4,96,128]{2,1,3,0:T(4,128)(2,1)}, ...), branch_computations={%region_2.2_spmd, %region_3.3_spmd} | conditional | flops 1025114112 | bytes 62975552 | solution.py:95
  585.6 8.3 %collective-permute-done.4 = bf16[4,4,96,128]{3,2,1,0:T(8,128)(2,1)S(1)} collective-permute-done((bf16[4,4,96,128]{3,2,1,0:T(8,128)(2,1)}, bf16[4,4,96,128]{3,2,1,0:T(8,128)(2,1)S(1)}, u32[]{:S(2)}, u32[]{:S(2)}) %collective-permute-start.4) | collective-permute-done | bytes 393248 | tf_op jit(solution)/shard_map/while/body/eval_jaxpr/ppermute | solution.py:29
  614.0 5.1 collective-permute-start.3
  623.5 25.5 %conditional.2 = (bf16[4,4,96,128]{3,2,1,0:T(8,128)(2,1)}) conditional(s32[]{:T(128)} %convert_element_type.58, () %tuple.55, (bf16[4,4,96,128]{2,1,3,0:T(4,128)(2,1)}, bf16[3,3,3,96,96]{3,4,2,1,0:T(8,128)(2,1)}, bf16[6,6,96,130]{2,1,3,0:T(8,128)(2,1)}, bf16[6,6,96,128]{2,1,3,0:T(8,128)(2,1)}, bf16[6,4,96,128]{2,1,3,0:T(4,128)(2,1)}, ...), branch_computations={%region_2.2_spmd, %region_3.3_spmd} | conditional | flops 1025114112 | bytes 62975552 | solution.py:95
  652.5 7.1 %collective-permute-done.4 = bf16[4,4,96,128]{3,2,1,0:T(8,128)(2,1)S(1)} collective-permute-done((bf16[4,4,96,128]{3,2,1,0:T(8,128)(2,1)}, bf16[4,4,96,128]{3,2,1,0:T(8,128)(2,1)S(1)}, u32[]{:S(2)}, u32[]{:S(2)}) %collective-permute-start.4) | collective-permute-done | bytes 393248 | tf_op jit(solution)/shard_map/while/body/eval_jaxpr/ppermute | solution.py:29
  (369 shorter events, 338.3 us)
Async XLA Ops:
  9.0 7.2 %collective-permute-start = (bf16[6,1,96,128]{2,1,3,0:T(2,128)(2,1)S(1)}, bf16[6,1,96,128]{2,1,3,0:T(2,128)(2,1)S(1)}, u32[]{:S(2)}, u32[]{:S(2)}) collective-permute-start(bf16[6,1,96,128]{2,1,3,0:T(2,128)(2,1)S(1)} %get-tuple-element.376), channel_id=1, source_target_pairs={{8,0},{16,8},{24,16},{32,24},{40,32},{48,40},{56,48},{9,1},{17,9},... | collective-permute-start | bytes 442376 | tf_op jit(solution)/shard_map/while/body/eval_jaxpr/ppermute | solution.py:19
  11.0 9.1 %collective-permute-start.1 = (bf16[6,1,96,128]{2,1,3,0:T(2,128)(2,1)S(1)}, bf16[6,1,96,128]{2,1,3,0:T(2,128)(2,1)S(1)}, u32[]{:S(2)}, u32[]{:S(2)}) collective-permute-start(bf16[6,1,96,128]{2,1,3,0:T(2,128)(2,1)S(1)} %get-tuple-element.377), channel_id=1, source_target_pairs={{0,8},{8,16},{16,24},{24,32},{32,40},{40,48},{48,56},{1,9},{9,17},... | collective-permute-start | bytes 442376 | tf_op jit(solution)/shard_map/while/body/eval_jaxpr/ppermute | solution.py:17
  22.8 8.9 %collective-permute-start.2 = (bf16[6,6,96,1]{2,1,3,0:T(8,128)(2,1)S(1)}, bf16[6,6,96,1]{2,1,3,0:T(8,128)(2,1)S(1)}, u32[]{:S(2)}, u32[]{:S(2)}) collective-permute-start(bf16[6,6,96,1]{2,1,3,0:T(8,128)(2,1)S(1)} %get-tuple-element.378), channel_id=1, source_target_pairs={{1,0},{2,1},{3,2},{4,3},{5,4},{6,5},{7,6},{9,8},{10,9},{11,10},{12... | collective-permute-start | bytes 20744 | tf_op jit(solution)/shard_map/while/body/eval_jaxpr/ppermute | solution.py:19
  35.4 12.0 %collective-permute-start.4 = (bf16[4,4,96,128]{3,2,1,0:T(8,128)(2,1)}, bf16[4,4,96,128]{3,2,1,0:T(8,128)(2,1)S(1)}, u32[]{:S(2)}, u32[]{:S(2)}) collective-permute-start(bf16[4,4,96,128]{3,2,1,0:T(8,128)(2,1)} %get-tuple-element.428), channel_id=1, source_target_pairs={{0,64},{64,128},{128,192},{192,256},{256,320},{320,384},{384,448},... | collective-permute-start | bytes 1179656 | tf_op jit(solution)/shard_map/while/body/eval_jaxpr/ppermute | solution.py:29
  51.7 7.2 %collective-permute-start = (bf16[6,1,96,128]{2,1,3,0:T(2,128)(2,1)S(1)}, bf16[6,1,96,128]{2,1,3,0:T(2,128)(2,1)S(1)}, u32[]{:S(2)}, u32[]{:S(2)}) collective-permute-start(bf16[6,1,96,128]{2,1,3,0:T(2,128)(2,1)S(1)} %get-tuple-element.376), channel_id=1, source_target_pairs={{8,0},{16,8},{24,16},{32,24},{40,32},{48,40},{56,48},{9,1},{17,9},... | collective-permute-start | bytes 442376 | tf_op jit(solution)/shard_map/while/body/eval_jaxpr/ppermute | solution.py:19
  53.6 9.1 %collective-permute-start.1 = (bf16[6,1,96,128]{2,1,3,0:T(2,128)(2,1)S(1)}, bf16[6,1,96,128]{2,1,3,0:T(2,128)(2,1)S(1)}, u32[]{:S(2)}, u32[]{:S(2)}) collective-permute-start(bf16[6,1,96,128]{2,1,3,0:T(2,128)(2,1)S(1)} %get-tuple-element.377), channel_id=1, source_target_pairs={{0,8},{8,16},{16,24},{24,32},{32,40},{40,48},{48,56},{1,9},{9,17},... | collective-permute-start | bytes 442376 | tf_op jit(solution)/shard_map/while/body/eval_jaxpr/ppermute | solution.py:17
  65.5 8.6 %collective-permute-start.2 = (bf16[6,6,96,1]{2,1,3,0:T(8,128)(2,1)S(1)}, bf16[6,6,96,1]{2,1,3,0:T(8,128)(2,1)S(1)}, u32[]{:S(2)}, u32[]{:S(2)}) collective-permute-start(bf16[6,6,96,1]{2,1,3,0:T(8,128)(2,1)S(1)} %get-tuple-element.378), channel_id=1, source_target_pairs={{1,0},{2,1},{3,2},{4,3},{5,4},{6,5},{7,6},{9,8},{10,9},{11,10},{12... | collective-permute-start | bytes 20744 | tf_op jit(solution)/shard_map/while/body/eval_jaxpr/ppermute | solution.py:19
  77.7 11.6 %collective-permute-start.4 = (bf16[4,4,96,128]{3,2,1,0:T(8,128)(2,1)}, bf16[4,4,96,128]{3,2,1,0:T(8,128)(2,1)S(1)}, u32[]{:S(2)}, u32[]{:S(2)}) collective-permute-start(bf16[4,4,96,128]{3,2,1,0:T(8,128)(2,1)} %get-tuple-element.428), channel_id=1, source_target_pairs={{0,64},{64,128},{128,192},{192,256},{256,320},{320,384},{384,448},... | collective-permute-start | bytes 1179656 | tf_op jit(solution)/shard_map/while/body/eval_jaxpr/ppermute | solution.py:29
  95.6 9.1 %collective-permute-start.1 = (bf16[6,1,96,128]{2,1,3,0:T(2,128)(2,1)S(1)}, bf16[6,1,96,128]{2,1,3,0:T(2,128)(2,1)S(1)}, u32[]{:S(2)}, u32[]{:S(2)}) collective-permute-start(bf16[6,1,96,128]{2,1,3,0:T(2,128)(2,1)S(1)} %get-tuple-element.377), channel_id=1, source_target_pairs={{0,8},{8,16},{16,24},{24,32},{32,40},{40,48},{48,56},{1,9},{9,17},... | collective-permute-start | bytes 442376 | tf_op jit(solution)/shard_map/while/body/eval_jaxpr/ppermute | solution.py:17
  107.5 8.6 %collective-permute-start.2 = (bf16[6,6,96,1]{2,1,3,0:T(8,128)(2,1)S(1)}, bf16[6,6,96,1]{2,1,3,0:T(8,128)(2,1)S(1)}, u32[]{:S(2)}, u32[]{:S(2)}) collective-permute-start(bf16[6,6,96,1]{2,1,3,0:T(8,128)(2,1)S(1)} %get-tuple-element.378), channel_id=1, source_target_pairs={{1,0},{2,1},{3,2},{4,3},{5,4},{6,5},{7,6},{9,8},{10,9},{11,10},{12... | collective-permute-start | bytes 20744 | tf_op jit(solution)/shard_map/while/body/eval_jaxpr/ppermute | solution.py:19
  119.7 10.6 %collective-permute-start.4 = (bf16[4,4,96,128]{3,2,1,0:T(8,128)(2,1)}, bf16[4,4,96,128]{3,2,1,0:T(8,128)(2,1)S(1)}, u32[]{:S(2)}, u32[]{:S(2)}) collective-permute-start(bf16[4,4,96,128]{3,2,1,0:T(8,128)(2,1)} %get-tuple-element.428), channel_id=1, source_target_pairs={{0,64},{64,128},{128,192},{192,256},{256,320},{320,384},{384,448},... | collective-permute-start | bytes 1179656 | tf_op jit(solution)/shard_map/while/body/eval_jaxpr/ppermute | solution.py:29
  136.6 9.1 %collective-permute-start.1 = (bf16[6,1,96,128]{2,1,3,0:T(2,128)(2,1)S(1)}, bf16[6,1,96,128]{2,1,3,0:T(2,128)(2,1)S(1)}, u32[]{:S(2)}, u32[]{:S(2)}) collective-permute-start(bf16[6,1,96,128]{2,1,3,0:T(2,128)(2,1)S(1)} %get-tuple-element.377), channel_id=1, source_target_pairs={{0,8},{8,16},{16,24},{24,32},{32,40},{40,48},{48,56},{1,9},{9,17},... | collective-permute-start | bytes 442376 | tf_op jit(solution)/shard_map/while/body/eval_jaxpr/ppermute | solution.py:17
  148.5 8.6 %collective-permute-start.2 = (bf16[6,6,96,1]{2,1,3,0:T(8,128)(2,1)S(1)}, bf16[6,6,96,1]{2,1,3,0:T(8,128)(2,1)S(1)}, u32[]{:S(2)}, u32[]{:S(2)}) collective-permute-start(bf16[6,6,96,1]{2,1,3,0:T(8,128)(2,1)S(1)} %get-tuple-element.378), channel_id=1, source_target_pairs={{1,0},{2,1},{3,2},{4,3},{5,4},{6,5},{7,6},{9,8},{10,9},{11,10},{12... | collective-permute-start | bytes 20744 | tf_op jit(solution)/shard_map/while/body/eval_jaxpr/ppermute | solution.py:19
  160.7 10.6 %collective-permute-start.4 = (bf16[4,4,96,128]{3,2,1,0:T(8,128)(2,1)}, bf16[4,4,96,128]{3,2,1,0:T(8,128)(2,1)S(1)}, u32[]{:S(2)}, u32[]{:S(2)}) collective-permute-start(bf16[4,4,96,128]{3,2,1,0:T(8,128)(2,1)} %get-tuple-element.428), channel_id=1, source_target_pairs={{0,64},{64,128},{128,192},{192,256},{256,320},{320,384},{384,448},... | collective-permute-start | bytes 1179656 | tf_op jit(solution)/shard_map/while/body/eval_jaxpr/ppermute | solution.py:29
  177.6 9.1 %collective-permute-start.1 = (bf16[6,1,96,128]{2,1,3,0:T(2,128)(2,1)S(1)}, bf16[6,1,96,128]{2,1,3,0:T(2,128)(2,1)S(1)}, u32[]{:S(2)}, u32[]{:S(2)}) collective-permute-start(bf16[6,1,96,128]{2,1,3,0:T(2,128)(2,1)S(1)} %get-tuple-element.377), channel_id=1, source_target_pairs={{0,8},{8,16},{16,24},{24,32},{32,40},{40,48},{48,56},{1,9},{9,17},... | collective-permute-start | bytes 442376 | tf_op jit(solution)/shard_map/while/body/eval_jaxpr/ppermute | solution.py:17
  189.5 8.6 %collective-permute-start.2 = (bf16[6,6,96,1]{2,1,3,0:T(8,128)(2,1)S(1)}, bf16[6,6,96,1]{2,1,3,0:T(8,128)(2,1)S(1)}, u32[]{:S(2)}, u32[]{:S(2)}) collective-permute-start(bf16[6,6,96,1]{2,1,3,0:T(8,128)(2,1)S(1)} %get-tuple-element.378), channel_id=1, source_target_pairs={{1,0},{2,1},{3,2},{4,3},{5,4},{6,5},{7,6},{9,8},{10,9},{11,10},{12... | collective-permute-start | bytes 20744 | tf_op jit(solution)/shard_map/while/body/eval_jaxpr/ppermute | solution.py:19
  201.7 11.8 %collective-permute-start.4 = (bf16[4,4,96,128]{3,2,1,0:T(8,128)(2,1)}, bf16[4,4,96,128]{3,2,1,0:T(8,128)(2,1)S(1)}, u32[]{:S(2)}, u32[]{:S(2)}) collective-permute-start(bf16[4,4,96,128]{3,2,1,0:T(8,128)(2,1)} %get-tuple-element.428), channel_id=1, source_target_pairs={{0,64},{64,128},{128,192},{192,256},{256,320},{320,384},{384,448},... | collective-permute-start | bytes 1179656 | tf_op jit(solution)/shard_map/while/body/eval_jaxpr/ppermute | solution.py:29
  219.8 9.1 %collective-permute-start.1 = (bf16[6,1,96,128]{2,1,3,0:T(2,128)(2,1)S(1)}, bf16[6,1,96,128]{2,1,3,0:T(2,128)(2,1)S(1)}, u32[]{:S(2)}, u32[]{:S(2)}) collective-permute-start(bf16[6,1,96,128]{2,1,3,0:T(2,128)(2,1)S(1)} %get-tuple-element.377), channel_id=1, source_target_pairs={{0,8},{8,16},{16,24},{24,32},{32,40},{40,48},{48,56},{1,9},{9,17},... | collective-permute-start | bytes 442376 | tf_op jit(solution)/shard_map/while/body/eval_jaxpr/ppermute | solution.py:17
  231.6 8.6 %collective-permute-start.2 = (bf16[6,6,96,1]{2,1,3,0:T(8,128)(2,1)S(1)}, bf16[6,6,96,1]{2,1,3,0:T(8,128)(2,1)S(1)}, u32[]{:S(2)}, u32[]{:S(2)}) collective-permute-start(bf16[6,6,96,1]{2,1,3,0:T(8,128)(2,1)S(1)} %get-tuple-element.378), channel_id=1, source_target_pairs={{1,0},{2,1},{3,2},{4,3},{5,4},{6,5},{7,6},{9,8},{10,9},{11,10},{12... | collective-permute-start | bytes 20744 | tf_op jit(solution)/shard_map/while/body/eval_jaxpr/ppermute | solution.py:19
  243.8 11.8 %collective-permute-start.4 = (bf16[4,4,96,128]{3,2,1,0:T(8,128)(2,1)}, bf16[4,4,96,128]{3,2,1,0:T(8,128)(2,1)S(1)}, u32[]{:S(2)}, u32[]{:S(2)}) collective-permute-start(bf16[4,4,96,128]{3,2,1,0:T(8,128)(2,1)} %get-tuple-element.428), channel_id=1, source_target_pairs={{0,64},{64,128},{128,192},{192,256},{256,320},{320,384},{384,448},... | collective-permute-start | bytes 1179656 | tf_op jit(solution)/shard_map/while/body/eval_jaxpr/ppermute | solution.py:29
  261.9 9.1 %collective-permute-start.1 = (bf16[6,1,96,128]{2,1,3,0:T(2,128)(2,1)S(1)}, bf16[6,1,96,128]{2,1,3,0:T(2,128)(2,1)S(1)}, u32[]{:S(2)}, u32[]{:S(2)}) collective-permute-start(bf16[6,1,96,128]{2,1,3,0:T(2,128)(2,1)S(1)} %get-tuple-element.377), channel_id=1, source_target_pairs={{0,8},{8,16},{16,24},{24,32},{32,40},{40,48},{48,56},{1,9},{9,17},... | collective-permute-start | bytes 442376 | tf_op jit(solution)/shard_map/while/body/eval_jaxpr/ppermute | solution.py:17
  273.8 8.6 %collective-permute-start.2 = (bf16[6,6,96,1]{2,1,3,0:T(8,128)(2,1)S(1)}, bf16[6,6,96,1]{2,1,3,0:T(8,128)(2,1)S(1)}, u32[]{:S(2)}, u32[]{:S(2)}) collective-permute-start(bf16[6,6,96,1]{2,1,3,0:T(8,128)(2,1)S(1)} %get-tuple-element.378), channel_id=1, source_target_pairs={{1,0},{2,1},{3,2},{4,3},{5,4},{6,5},{7,6},{9,8},{10,9},{11,10},{12... | collective-permute-start | bytes 20744 | tf_op jit(solution)/shard_map/while/body/eval_jaxpr/ppermute | solution.py:19
  286.0 174.2 %collective-permute-start.4 = (bf16[4,4,96,128]{3,2,1,0:T(8,128)(2,1)}, bf16[4,4,96,128]{3,2,1,0:T(8,128)(2,1)S(1)}, u32[]{:S(2)}, u32[]{:S(2)}) collective-permute-start(bf16[4,4,96,128]{3,2,1,0:T(8,128)(2,1)} %get-tuple-element.428), channel_id=1, source_target_pairs={{0,64},{64,128},{128,192},{192,256},{256,320},{320,384},{384,448},... | collective-permute-start | bytes 1179656 | tf_op jit(solution)/shard_map/while/body/eval_jaxpr/ppermute | solution.py:29
  466.4 9.1 %collective-permute-start.1 = (bf16[6,1,96,128]{2,1,3,0:T(2,128)(2,1)S(1)}, bf16[6,1,96,128]{2,1,3,0:T(2,128)(2,1)S(1)}, u32[]{:S(2)}, u32[]{:S(2)}) collective-permute-start(bf16[6,1,96,128]{2,1,3,0:T(2,128)(2,1)S(1)} %get-tuple-element.377), channel_id=1, source_target_pairs={{0,8},{8,16},{16,24},{24,32},{32,40},{40,48},{48,56},{1,9},{9,17},... | collective-permute-start | bytes 442376 | tf_op jit(solution)/shard_map/while/body/eval_jaxpr/ppermute | solution.py:17
  478.3 8.6 %collective-permute-start.2 = (bf16[6,6,96,1]{2,1,3,0:T(8,128)(2,1)S(1)}, bf16[6,6,96,1]{2,1,3,0:T(8,128)(2,1)S(1)}, u32[]{:S(2)}, u32[]{:S(2)}) collective-permute-start(bf16[6,6,96,1]{2,1,3,0:T(8,128)(2,1)S(1)} %get-tuple-element.378), channel_id=1, source_target_pairs={{1,0},{2,1},{3,2},{4,3},{5,4},{6,5},{7,6},{9,8},{10,9},{11,10},{12... | collective-permute-start | bytes 20744 | tf_op jit(solution)/shard_map/while/body/eval_jaxpr/ppermute | solution.py:19
  515.2 11.8 %collective-permute-start.4 = (bf16[4,4,96,128]{3,2,1,0:T(8,128)(2,1)}, bf16[4,4,96,128]{3,2,1,0:T(8,128)(2,1)S(1)}, u32[]{:S(2)}, u32[]{:S(2)}) collective-permute-start(bf16[4,4,96,128]{3,2,1,0:T(8,128)(2,1)} %get-tuple-element.428), channel_id=1, source_target_pairs={{0,64},{64,128},{128,192},{192,256},{256,320},{320,384},{384,448},... | collective-permute-start | bytes 1179656 | tf_op jit(solution)/shard_map/while/body/eval_jaxpr/ppermute | solution.py:29
  533.3 9.1 %collective-permute-start.1 = (bf16[6,1,96,128]{2,1,3,0:T(2,128)(2,1)S(1)}, bf16[6,1,96,128]{2,1,3,0:T(2,128)(2,1)S(1)}, u32[]{:S(2)}, u32[]{:S(2)}) collective-permute-start(bf16[6,1,96,128]{2,1,3,0:T(2,128)(2,1)S(1)} %get-tuple-element.377), channel_id=1, source_target_pairs={{0,8},{8,16},{16,24},{24,32},{32,40},{40,48},{48,56},{1,9},{9,17},... | collective-permute-start | bytes 442376 | tf_op jit(solution)/shard_map/while/body/eval_jaxpr/ppermute | solution.py:17
  545.2 8.6 %collective-permute-start.2 = (bf16[6,6,96,1]{2,1,3,0:T(8,128)(2,1)S(1)}, bf16[6,6,96,1]{2,1,3,0:T(8,128)(2,1)S(1)}, u32[]{:S(2)}, u32[]{:S(2)}) collective-permute-start(bf16[6,6,96,1]{2,1,3,0:T(8,128)(2,1)S(1)} %get-tuple-element.378), channel_id=1, source_target_pairs={{1,0},{2,1},{3,2},{4,3},{5,4},{6,5},{7,6},{9,8},{10,9},{11,10},{12... | collective-permute-start | bytes 20744 | tf_op jit(solution)/shard_map/while/body/eval_jaxpr/ppermute | solution.py:19
  582.1 11.8 %collective-permute-start.4 = (bf16[4,4,96,128]{3,2,1,0:T(8,128)(2,1)}, bf16[4,4,96,128]{3,2,1,0:T(8,128)(2,1)S(1)}, u32[]{:S(2)}, u32[]{:S(2)}) collective-permute-start(bf16[4,4,96,128]{3,2,1,0:T(8,128)(2,1)} %get-tuple-element.428), channel_id=1, source_target_pairs={{0,64},{64,128},{128,192},{192,256},{256,320},{320,384},{384,448},... | collective-permute-start | bytes 1179656 | tf_op jit(solution)/shard_map/while/body/eval_jaxpr/ppermute | solution.py:29
  600.2 9.1 %collective-permute-start.1 = (bf16[6,1,96,128]{2,1,3,0:T(2,128)(2,1)S(1)}, bf16[6,1,96,128]{2,1,3,0:T(2,128)(2,1)S(1)}, u32[]{:S(2)}, u32[]{:S(2)}) collective-permute-start(bf16[6,1,96,128]{2,1,3,0:T(2,128)(2,1)S(1)} %get-tuple-element.377), channel_id=1, source_target_pairs={{0,8},{8,16},{16,24},{24,32},{32,40},{40,48},{48,56},{1,9},{9,17},... | collective-permute-start | bytes 442376 | tf_op jit(solution)/shard_map/while/body/eval_jaxpr/ppermute | solution.py:17
  612.1 8.6 %collective-permute-start.2 = (bf16[6,6,96,1]{2,1,3,0:T(8,128)(2,1)S(1)}, bf16[6,6,96,1]{2,1,3,0:T(8,128)(2,1)S(1)}, u32[]{:S(2)}, u32[]{:S(2)}) collective-permute-start(bf16[6,6,96,1]{2,1,3,0:T(8,128)(2,1)S(1)} %get-tuple-element.378), channel_id=1, source_target_pairs={{1,0},{2,1},{3,2},{4,3},{5,4},{6,5},{7,6},{9,8},{10,9},{11,10},{12... | collective-permute-start | bytes 20744 | tf_op jit(solution)/shard_map/while/body/eval_jaxpr/ppermute | solution.py:19
  649.0 10.6 %collective-permute-start.4 = (bf16[4,4,96,128]{3,2,1,0:T(8,128)(2,1)}, bf16[4,4,96,128]{3,2,1,0:T(8,128)(2,1)S(1)}, u32[]{:S(2)}, u32[]{:S(2)}) collective-permute-start(bf16[4,4,96,128]{3,2,1,0:T(8,128)(2,1)} %get-tuple-element.428), channel_id=1, source_target_pairs={{0,64},{64,128},{128,192},{192,256},{256,320},{320,384},{384,448},... | collective-permute-start | bytes 1179656 | tf_op jit(solution)/shard_map/while/body/eval_jaxpr/ppermute | solution.py:29
  (46 other events, 245.9 us)
where the time goes:
time: 663 us; the launch traced here: 660 us
  waiting for transfers between devices  310 us (47%)
  starting transfers between devices  127 us (19%)
  other arithmetic  107 us (16%)
  local copies, waits for them, and re-layouts  63.3 us (10%)
  matrix products  50.8 us (8%)
    ppermute x10, waiting for transfers between devices, from_behind(): return lax.ppermute(block, axis, route)  243 us
    ppermute x20, starting transfers between devices, extended_2(): lax.ppermute(tail, axis, [(i, (i + 1) % count) for i in range(ends)])  75.7 us
    dot_general x81, matrix products, convolve(): jnp.einsum('fhcw,co->fhow', window, kernel[tap_time, tap_row, tap_col], p...  50.8 us
    concatenate x20, other arithmetic, extended_2(): jnp.concatenate([lax.ppermute(tail, axis, [(i, (i + 1) % count) for i in...  44.4 us
    ppermute x20, starting transfers between devices, extended_2(): lax.ppermute(head, axis, [((i + 1) % count, i) for i in range(ends)])  38.3 us
    ppermute x20, waiting for transfers between devices, extended_2(): lax.ppermute(tail, axis, [(i, (i + 1) % count) for i in range(ends)])  38.2 us
    another operation x30, local copies, waits for them, and re-layouts  32.6 us
    ppermute x20, waiting for transfers between devices, extended_2(): lax.ppermute(head, axis, [((i + 1) % count, i) for i in range(ends)])  28.6 us
  transfers between devices with their start and end apart: 50, of which 30 were waited for; matrix products, arithmetic and copies ran while one was open for 5% of the time, Pallas kernels for 0%

commit v1 on v0

v1 whole, which is shorter than its diff:
```python
import jax
import jax.numpy as jnp
from jax import lax
from jax.experimental import pallas as pl
from jax.experimental.pallas import tpu as pltpu
from jax.sharding import PartitionSpec as P

C = 96
LAYERS = 8
FRAMES = 12
ROWS = 4
COLS = 128
OWN = 16
HALO = 8
WIN = OWN + 2 * HALO
LANES = 640
TAPS = 9 * C
WIDE = 896
VMEM = pl.BlockSpec(memory_space=pltpu.VMEM)
SMEM = pl.BlockSpec(memory_space=pltpu.SMEM)
F32 = jnp.float32
BF16 = jnp.bfloat16


def lanes_of(layer):
    used = (20 - 2 * layer) * WIN
    made = (18 - 2 * layer) * WIN
    return -(-used // 128) * 128, -(-made // 128) * 128


def shifted(block, offset):
    size = block.shape[-1]
    offset %= size
    return pltpu.roll(block, size - offset, 1) if offset else block


def edges_kernel(features, cached, right, left):
    lane = lax.broadcasted_iota(jnp.int32, (C, 128), 1)
    for group in range(4):
        ends = jnp.zeros((C, 128), F32)
        heads = jnp.zeros((C, 128), F32)
        for inner in range(4):
            frame = group * 4 + inner
            if frame >= FRAMES + 2:
                continue
            for row in range(ROWS):
                tile = (features[frame, row] if frame < FRAMES else cached[frame - FRAMES, row]).astype(F32)
                at = inner * 32 + row * 8
                here = jnp.logical_and(lane >= at, lane < at + 8)
                ends = jnp.where(here, shifted(tile, 120 - at), ends)
                heads = jnp.where(here, shifted(tile, -at), heads)
        right[group] = ends.astype(BF16)
        left[group] = heads.astype(BF16)


def windows_kernel(place, features, cached, before, after, own, spread):
    lane = lax.broadcasted_iota(jnp.int32, (C, 128), 1)
    section = place[0]

    def edge(block, frame, row, column):
        group, inner = divmod(frame, 4)
        at = inner * 32 + row * 8
        return shifted(block[group].astype(F32), at - row * WIN - column)

    def within(row, low, high):
        return jnp.logical_and(lane >= row * WIN + low, lane < row * WIN + high)

    for frame in range(FRAMES):
        total = jnp.zeros((C, 128), F32)
        for row in range(ROWS):
            tile = features[frame, row].astype(F32)
            amount = lax.rem(row * WIN + HALO - OWN * section + 256, 128)
            window = pltpu.roll(tile, amount, 1)
            first = jnp.logical_and(within(row, 0, HALO), section == 0)
            last = jnp.logical_and(within(row, WIN - HALO, WIN), section == LAYERS - 1)
            window = jnp.where(first, edge(before, frame, row, 0), window)
            window = jnp.where(last, edge(after, frame, row, WIN - HALO), window)
            total = jnp.where(within(row, 0, WIN), window, total)
        own[frame] = total.astype(BF16)
    for frame in range(2):
        for target in range(LAYERS):
            total = jnp.zeros((C, 128), F32)
            for row in range(ROWS):
                tile = cached[frame, row].astype(F32)
                window = shifted(tile, OWN * target - HALO - row * WIN)
                if target == 0:
                    window = jnp.where(within(row, 0, HALO), edge(before, FRAMES + frame, row, 0), window)
                if target == LAYERS - 1:
                    window = jnp.where(
                        within(row, WIN - HALO, WIN), edge(after, FRAMES + frame, row, WIN - HALO), window
                    )
                total = jnp.where(within(row, 0, WIN), window, total)
            spread[target, frame] = total.astype(BF16)


def blocks_kernel(f0, f1, f2, f3, f4, c0, c1, c2, c3, c4, weight, inside, out, act, taps, sums, here, ahead, held):
    for at, part in enumerate((f0, f1, f2, f3, f4)):
        act[:, :, at * 128 : (at + 1) * 128] = part[...]
    middle = lax.broadcasted_iota(jnp.int32, (C, 128), 1) % WIN
    middle = jnp.logical_and(middle >= HALO, middle < HALO + OWN)

    def spread_taps(values, start, base, count):
        for tap_row in range(3):
            for tap_col in range(3):
                block = shifted(values, base + tap_row * WIN + tap_col - 1)[:, :count]
                tap = tap_row * 3 + tap_col
                taps[tap * C : (tap + 1) * C, pl.ds(start, count)] = block.astype(BF16)

    for layer in range(LAYERS):
        used, made = lanes_of(layer)
        batch = {640: 3, 512: 4, 384: 4, 256: 6, 128: 12}[made]

        def column(at):
            parts = [weight[layer, 0:C, at + i : at + i + 1].astype(F32) for i in range(3)]
            return parts[0] + parts[1] + parts[2]

        gain = column(TAPS)
        bias = column(TAPS + 3)
        valid = inside[layer, :, 0:used]

        for frame in range(2):
            stored = jnp.concatenate([c[layer, frame] for c in (c0, c1, c2, c3, c4)], axis=1)
            spread_taps(stored.astype(F32), frame * made, layer * WIN, made)
        sums[0 : 2 * C, 0 : 2 * made] = jnp.dot(
            weight[layer, 0 : 2 * C, 0:TAPS], taps[:, 0 : 2 * made], preferred_element_type=F32
        )
        here[:, 0:made] = sums[0:C, 0:made] + sums[C : 2 * C, made : 2 * made] + bias
        ahead[:, 0:made] = sums[0:C, made : 2 * made] + bias

        def run(step, _, used=used, made=made, batch=batch, gain=gain, bias=bias, valid=valid, layer=layer):
            def prepare(inner, _):
                values = act[step * batch + inner, :, 0:used].astype(F32)
                meansq = jnp.sum(values * values, axis=0, keepdims=True) * (1.0 / C)
                scale = lax.rsqrt(meansq + 1e-06) * valid
                normed = values * scale * gain
                normed = (0.5 * normed) * (1.0 + jnp.tanh(0.5 * normed))
                spread_taps(normed, pl.multiple_of(inner * made, 128), 0, made)
                return 0

            lax.fori_loop(0, batch, prepare, 0)
            sums[:, 0 : batch * made] = jnp.dot(
                weight[layer, :, 0:TAPS], taps[:, 0 : batch * made], preferred_element_type=F32
            )

            def finish(inner, _):
                frame = step * batch + inner
                span = pl.ds(pl.multiple_of(inner * made, 128), made)
                inputs = shifted(act[frame, :, 0:used].astype(F32), WIN)[:, 0:made]
                total = inputs + here[:, 0:made] + sums[2 * C : 3 * C, span]
                here[:, 0:made] = ahead[:, 0:made] + sums[C : 2 * C, span]
                ahead[:, 0:made] = sums[0:C, span] + bias
                act[frame, :, 0:made] = total.astype(BF16)
                center = shifted(total, (7 - layer) * WIN)[:, 0:128]
                odd = lax.rem(frame, 2) == 1

                @pl.when(odd)
                def _():
                    both = jnp.where(middle, held[...], pltpu.roll(center, OWN, 1))
                    out[layer, frame // 2] = both.astype(BF16)

                @pl.when(jnp.logical_not(odd))
                def _():
                    held[...] = center

                return 0

            lax.fori_loop(0, batch, finish, 0)
            return 0

        lax.fori_loop(0, FRAMES // batch, run, 0)


def join_kernel(parts, out):
    lane = lax.broadcasted_iota(jnp.int32, (C, 128), 1)
    for frame in range(FRAMES):
        for row in range(ROWS):
            at = row * WIN + HALO + (OWN if frame % 2 else 0)
            total = jnp.zeros((C, 128), F32)
            for source in range(LAYERS):
                block = shifted(parts[source, frame // 2].astype(F32), at - source * OWN)
                mine = jnp.logical_and(lane >= source * OWN, lane < (source + 1) * OWN)
                total = jnp.where(mine, block, total)
            out[frame, row] = total.astype(BF16)


def call(kernel, shapes, scratch=(), limit=56, flops=0, moved=0, name=None):
    return pl.pallas_call(
        kernel,
        out_shape=[jax.ShapeDtypeStruct(s, BF16) for s in shapes],
        out_specs=[VMEM] * len(shapes),
        scratch_shapes=list(scratch),
        compiler_params=pltpu.CompilerParams(vmem_limit_bytes=limit << 20),
        cost_estimate=pl.CostEstimate(flops=flops, bytes_accessed=moved, transcendentals=0),
        name=name,
    )


def along(block, axis, distance):
    count = lax.axis_size(axis)
    route = [(i, i + distance) for i in range(count) if 0 <= i + distance < count]
    return lax.ppermute(block, axis, route)


def three_parts(values):
    high = values.astype(BF16)
    rest = values - high.astype(F32)
    mid = rest.astype(BF16)
    low = (rest - mid.astype(F32)).astype(BF16)
    return [high, mid, low]


def body(features, conv_weight, norm_gain, conv_bias, cached):
    section = lax.axis_index("section")
    row = lax.axis_index("row")
    col = lax.axis_index("col")
    cached = cached[0]

    matrix = jnp.transpose(conv_weight[0], (0, 4, 1, 2, 3)).reshape(3 * C, TAPS)
    extra = jnp.stack(three_parts(norm_gain[0]) + three_parts(conv_bias[0]), axis=1)
    extra = jnp.pad(extra, ((0, 2 * C), (0, WIDE - TAPS - 6)))
    matrix = jnp.concatenate([matrix, extra], axis=1)
    weights = lax.all_gather(matrix, "section")

    right, left = call(edges_kernel, [(4, C, 128)] * 2, name="edges")(features, cached)
    before = along(right, "col", 1)
    after = along(left, "col", -1)
    place = jnp.reshape(section, (1,)).astype(jnp.int32)
    own, spread = pl.pallas_call(
        windows_kernel,
        in_specs=[SMEM] + [VMEM] * 4,
        out_shape=[
            jax.ShapeDtypeStruct((FRAMES, C, 128), BF16),
            jax.ShapeDtypeStruct((LAYERS, 2, C, 128), BF16),
        ],
        out_specs=[VMEM] * 2,
        compiler_params=pltpu.CompilerParams(vmem_limit_bytes=32 << 20),
        name="windows",
    )(place, features, cached, before, after)
    stored = lax.all_to_all(spread, "section", 0, 0, tiled=True)
    steps = (2, 1, -1, -2)
    f = [along(own, "row", d) for d in steps]
    c = [along(stored, "row", d) for d in steps]
    f = [f[0], f[1], own, f[2], f[3]]
    c = [c[0], c[1], stored, c[2], c[3]]

    cell = jnp.arange(LANES, dtype=jnp.int32)[None, None, :]
    first = jnp.arange(LAYERS, dtype=jnp.int32)[:, None, None]
    at_row = row * ROWS - HALO + first + cell // WIN
    at_col = col * COLS + section * OWN - HALO + cell % WIN
    high = lax.axis_size("row") * ROWS
    wide = lax.axis_size("col") * COLS
    inside = (at_row >= 0) & (at_row < high) & (at_col >= 0) & (at_col < wide)
    inside = inside.astype(F32)

    (packed,) = call(
        blocks_kernel,
        [(LAYERS, FRAMES // 2, C, 128)],
        [
            pltpu.VMEM((FRAMES, C, LANES), BF16),
            pltpu.VMEM((TAPS, 2048), BF16),
            pltpu.VMEM((3 * C, 2048), F32),
            pltpu.VMEM((C, LANES), F32),
            pltpu.VMEM((C, LANES), F32),
            pltpu.VMEM((C, 128), F32),
        ],
        flops=18_000_000_000,
        moved=8_000_000,
        name="blocks",
    )(*f, *c, weights, inside)
    parts = lax.all_to_all(packed, "section", 0, 0, tiled=True)
    (joined,) = call(join_kernel, [(FRAMES, ROWS, C, COLS)], name="join")(parts)
    return joined[None]


def solution(mesh):
    return jax.shard_map(
        body,
        mesh=mesh,
        in_specs=(
            P(None, "row", None, "col"),
            P("section", None, None, None, None, None),
            P("section", None),
            P("section", None),
            P("section", None, "row", None, "col"),
        ),
        out_specs=P("section", None, "row", None, "col"),
        check_vma=False,
    )
```

time: 663 us -> 225 us (0.34)
  the two profiles are of different devices: /device:TPU:250 before, /device:TPU:199 now
where the time goes in v1:
time: 225 us; the launch traced here: 224 us
  Pallas kernels  100 us (44%)
  blocking collectives  36.3 us (16%)
  starting transfers between devices  33.8 us (15%)
  waiting for transfers between devices  33 us (15%)
  between operations  13.7 us (6%)
  local copies, waits for them, and re-layouts  4.19 us (2%)
  other arithmetic  2.96 us (1%)
    pallas_call x1, Pallas kernels, body(): call(blocks_kernel, [(LAYERS, FRAMES // 2, C, 128)], [pltpu.VMEM((FRAMES,...  90.4 us
    all_to_all x1, blocking collectives, body(): parts = lax.all_to_all(packed, 'section', 0, 0, tiled=True)  36.3 us
    ppermute x10, starting transfers between devices, along(): return lax.ppermute(block, axis, route)  27 us
    ppermute x10, waiting for transfers between devices, along(): return lax.ppermute(block, axis, route)  23.3 us
    all_to_all x1, waiting for transfers between devices, body(): stored = lax.all_to_all(spread, 'section', 0, 0, tiled=True)  9.65 us
    all_to_all x1, starting transfers between devices, body(): stored = lax.all_to_all(spread, 'section', 0, 0, tiled=True)  6.82 us
    pallas_call x1, Pallas kernels, body(): joined, = call(join_kernel, [(FRAMES, ROWS, C, COLS)], name='join')(parts)  4.78 us
  transfers between devices with their start and end apart: 12, of which 3 were waited for; matrix products, arithmetic and copies ran while one was open for 0% of the time, Pallas kernels for 2%

profile of v1, /device:TPU:199, one launch (start us, length us, event | category | flops | bytes accessed | tf_op | source)
XLA Modules:
  0.0 224.1 jit_solution(12857941220895323540)
XLA Ops:
  6.5 0.7 bitcast_convert_fusion
  7.2 0.7 subtract_convert_fusion
  7.9 0.1 copy.15
  8.0 2.3 %copy.14 = bf16[3,96,3,3,96]{4,3,2,1,0:T(4,128)(2,1)S(1)} copy(bf16[3,96,3,3,96]{1,4,3,2,0:T(8,128)(2,1)} %bitcast.35) | data formatting | bytes 995328 | tf_op jit(solution)/shard_map/transpose | solution.py:218
  10.3 0.6 reshape.273
  10.9 0.9 fusion.1
  11.8 2.8 %edges.1 = (bf16[4,96,128]{2,1,0:T(8,128)(2,1)}, bf16[4,96,128]{2,1,0:T(8,128)(2,1)}) custom-call(bf16[12,4,96,128]{3,2,1,0:T(8,128)(2,1)} %features.3, bf16[2,4,96,128]{3,2,1,0:T(8,128)(2,1)} %bitcast.33), custom_call_target="tpu_custom_call" | custom-call | tf_op jit(solution)/shard_map/edges/pallas_call | solution.py:224
  14.6 5.2 %collective-permute-start = (bf16[4,96,128]{2,1,0:T(8,128)(2,1)}, bf16[4,96,128]{2,1,0:T(8,128)(2,1)S(1)}, u32[]{:S(2)}, u32[]{:S(2)}) collective-permute-start(bf16[4,96,128]{2,1,0:T(8,128)(2,1)} %get-tuple-element.9), channel_id=1, source_target_pairs={{0,1},{1,2},{2,3},{3,4},{4,5},{5,6},{6,7},{8,9},{9,10},{10,11},{11... | collective-permute-start | bytes 294920 | tf_op jit(solution)/shard_map/ppermute | solution.py:201
  19.8 1.9 collective-permute-start.1
  21.8 4.8 %collective-permute-done.1.after = bf16[4,96,128]{2,1,0:T(8,128)(2,1)S(1)} collective-permute-done((bf16[4,96,128]{2,1,0:T(8,128)(2,1)}, bf16[4,96,128]{2,1,0:T(8,128)(2,1)S(1)}, u32[]{:S(2)}, u32[]{:S(2)}) %collective-permute-start.1) | collective-permute-done | bytes 98336 | tf_op jit(solution)/shard_map/ppermute | solution.py:201
  26.6 2.2 windows.1
  28.9 6.8 %all-to-all-start = ((bf16[8,2,96,128]{3,2,1,0:T(8,128)(2,1)}), bf16[8,2,96,128]{3,2,1,0:T(8,128)(2,1)S(1)}, u32[]{:S(2)}, u32[]{:S(2)}) async-start(bf16[8,2,96,128]{3,2,1,0:T(8,128)(2,1)} %get-tuple-element.12), calls=%async_computation | async-start | bytes 786432 | tf_op jit(solution)/shard_map/all_to_all | solution.py:239
  35.7 2.5 %collective-permute-start.5 = (bf16[12,96,128]{2,1,0:T(8,128)(2,1)S(1)}, bf16[12,96,128]{2,1,0:T(8,128)(2,1)S(1)}, u32[]{:S(2)}, u32[]{:S(2)}) collective-permute-start(bf16[12,96,128]{2,1,0:T(8,128)(2,1)S(1)} %get-tuple-element.11.f2), channel_id=1, source_target_pairs={{16,0},{24,8},{32,16},{40,24},{48,32},{56,40},{17,1},{25,9},{33,17... | collective-permute-start | bytes 884744 | tf_op jit(solution)/shard_map/ppermute | solution.py:201
  38.1 4.6 %collective-permute-start.4 = (bf16[12,96,128]{2,1,0:T(8,128)(2,1)S(1)}, bf16[12,96,128]{2,1,0:T(8,128)(2,1)S(1)}, u32[]{:S(2)}, u32[]{:S(2)}) collective-permute-start(bf16[12,96,128]{2,1,0:T(8,128)(2,1)S(1)} %get-tuple-element.11.f2), channel_id=1, source_target_pairs={{8,0},{16,8},{24,16},{32,24},{40,32},{48,40},{56,48},{9,1},{17,9},... | collective-permute-start | bytes 884744 | tf_op jit(solution)/shard_map/ppermute | solution.py:201
  42.7 1.3 collective-permute-start.3
  44.1 9.6 %all-to-all-done.c2 = bf16[8,2,96,128]{3,2,1,0:T(8,128)(2,1)S(1)} async-done(((bf16[8,2,96,128]{3,2,1,0:T(8,128)(2,1)}), bf16[8,2,96,128]{3,2,1,0:T(8,128)(2,1)S(1)}, u32[]{:S(2)}, u32[]{:S(2)}) %all-to-all-start) | async-done | bytes 393248 | tf_op jit(solution)/shard_map/all_to_all | solution.py:239
  53.7 2.5 %collective-permute-start.9 = (bf16[8,2,96,128]{3,2,1,0:T(8,128)(2,1)S(1)}, bf16[8,2,96,128]{3,2,1,0:T(8,128)(2,1)S(1)}, u32[]{:S(2)}, u32[]{:S(2)}) collective-permute-start(bf16[8,2,96,128]{3,2,1,0:T(8,128)(2,1)S(1)} %all-to-all-done.c2), channel_id=1, source_target_pairs={{16,0},{24,8},{32,16},{40,24},{48,32},{56,40},{17,1},{25,9},{33,17... | collective-permute-start | bytes 1179656 | tf_op jit(solution)/shard_map/ppermute | solution.py:201
  56.2 5.2 %collective-permute-start.8 = (bf16[8,2,96,128]{3,2,1,0:T(8,128)(2,1)S(1)}, bf16[8,2,96,128]{3,2,1,0:T(8,128)(2,1)S(1)}, u32[]{:S(2)}, u32[]{:S(2)}) collective-permute-start(bf16[8,2,96,128]{3,2,1,0:T(8,128)(2,1)S(1)} %all-to-all-done.c2), channel_id=1, source_target_pairs={{8,0},{16,8},{24,16},{32,24},{40,32},{48,40},{56,48},{9,1},{17,9},... | collective-permute-start | bytes 1179656 | tf_op jit(solution)/shard_map/ppermute | solution.py:201
  61.4 1.3 collective-permute-start.7
  62.7 1.3 collective-permute-start.6
  64.0 1.3 collective-permute-start.2
  65.3 0.7 and_convert_fusion.inside
  66.1 18.5 %collective-permute-done.2.f0 = bf16[12,96,128]{2,1,0:T(8,128)(2,1)S(1)} collective-permute-done((bf16[12,96,128]{2,1,0:T(8,128)(2,1)S(1)}, bf16[12,96,128]{2,1,0:T(8,128)(2,1)S(1)}, u32[]{:S(2)}, u32[]{:S(2)}) %collective-permute-start.2) | collective-permute-done | bytes 294944 | tf_op jit(solution)/shard_map/ppermute | solution.py:201
  84.6 0.0 all-gather.3.cloned.1.call-done
  84.7 0.6 copy-done.11
  85.2 0.2 copy-done.4
  85.4 0.1 copy-done.5
  85.5 0.1 copy-done.6
  85.6 0.2 copy-done.7
  85.8 90.4 %blocks.1 = bf16[8,6,96,128]{3,2,1,0:T(8,128)(2,1)} custom-call(bf16[12,96,128]{2,1,0:T(8,128)(2,1)} %copy-done.11, bf16[12,96,128]{2,1,0:T(8,128)(2,1)} %copy-done.10, bf16[12,96,128]{2,1,0:T(8,128)(2,1)} %copy-done.2, bf16[12,96,128]{2,1,0:T(8,128)(2,1)} %copy-done.9, bf16[12,96,128]{2,1,0:T(8,128)(2,1)} %copy-done.8, bf16[8,2,96,128]{3,2,1,0:T(8,128)(2,1)} %copy-done.7, ...), custom_call_target="tpu_custom_call" | custom-call | flops 17999998976 | bytes 8000000 | tf_op jit(solution)/shard_map/blocks/pallas_call | solution.py:255
  176.2 36.3 %all_to_all.10.parts = bf16[8,6,96,128]{3,2,1,0:T(8,128)(2,1)} all-to-all(bf16[8,6,96,128]{3,2,1,0:T(8,128)(2,1)} %blocks.1), channel_id=1, replica_groups=mesh['section'=8,'row'=8,'col'=8] {'section'}, dimensions={0} | all-to-all | bytes 2359296 | tf_op jit(solution)/shard_map/all_to_all | solution.py:270
  212.5 4.8 %join.1 = bf16[12,4,96,128]{3,2,1,0:T(8,128)(2,1)} custom-call(bf16[8,6,96,128]{3,2,1,0:T(8,128)(2,1)} %all_to_all.10.parts), custom_call_target="tpu_custom_call" | custom-call | tf_op jit(solution)/shard_map/join/pallas_call | solution.py:271
  (33 shorter events, 0.1 us)
Async XLA Ops:
  6.5 78.1 %all-gather.3.cloned.1.call-start = ((), (), s32[]{:S(2)}) async-start(), calls=%async_computation.2 | async-start | bytes 4644864 | tf_op jit(solution)/shard_map/all_gather | solution.py:222
  11.8 14.8 %copy-start = (bf16[12,4,96,128]{3,2,1,0:T(8,128)(2,1)S(1)}, bf16[12,4,96,128]{3,2,1,0:T(8,128)(2,1)}, u32[]{:S(2)}) copy-start(bf16[12,4,96,128]{3,2,1,0:T(8,128)(2,1)} %features.3) | copy-start | bytes 3538948
  11.8 14.8 %copy-start.1 = (bf16[1,2,4,96,128]{4,3,2,1,0:T(8,128)(2,1)S(1)}, bf16[1,2,4,96,128]{4,3,2,1,0:T(8,128)(2,1)}, u32[]{:S(2)}) copy-start(bf16[1,2,4,96,128]{4,3,2,1,0:T(8,128)(2,1)} %param.9) | copy-start | bytes 589828
  14.6 7.1 %collective-permute-start = (bf16[4,96,128]{2,1,0:T(8,128)(2,1)}, bf16[4,96,128]{2,1,0:T(8,128)(2,1)S(1)}, u32[]{:S(2)}, u32[]{:S(2)}) collective-permute-start(bf16[4,96,128]{2,1,0:T(8,128)(2,1)} %get-tuple-element.9), channel_id=1, source_target_pairs={{0,1},{1,2},{2,3},{3,4},{4,5},{5,6},{6,7},{8,9},{9,10},{10,11},{11... | collective-permute-start | bytes 294920 | tf_op jit(solution)/shard_map/ppermute | solution.py:201
  19.8 6.8 %collective-permute-start.1 = (bf16[4,96,128]{2,1,0:T(8,128)(2,1)}, bf16[4,96,128]{2,1,0:T(8,128)(2,1)S(1)}, u32[]{:S(2)}, u32[]{:S(2)}) collective-permute-start(bf16[4,96,128]{2,1,0:T(8,128)(2,1)} %get-tuple-element.10), channel_id=1, source_target_pairs={{1,0},{2,1},{3,2},{4,3},{5,4},{6,5},{7,6},{9,8},{10,9},{11,10},{12... | collective-permute-start | bytes 294920 | tf_op jit(solution)/shard_map/ppermute | solution.py:201
  28.9 55.8 %copy-start.2 = (bf16[12,96,128]{2,1,0:T(8,128)(2,1)}, bf16[12,96,128]{2,1,0:T(8,128)(2,1)S(1)}, u32[]{:S(2)}) copy-start(bf16[12,96,128]{2,1,0:T(8,128)(2,1)S(1)} %get-tuple-element.11.f2) | copy-start | bytes 884740
  28.9 24.9 %all-to-all-start = ((bf16[8,2,96,128]{3,2,1,0:T(8,128)(2,1)}), bf16[8,2,96,128]{3,2,1,0:T(8,128)(2,1)S(1)}, u32[]{:S(2)}, u32[]{:S(2)}) async-start(bf16[8,2,96,128]{3,2,1,0:T(8,128)(2,1)} %get-tuple-element.12), calls=%async_computation | async-start | bytes 786432 | tf_op jit(solution)/shard_map/all_to_all | solution.py:239
  35.7 25.7 %collective-permute-start.5 = (bf16[12,96,128]{2,1,0:T(8,128)(2,1)S(1)}, bf16[12,96,128]{2,1,0:T(8,128)(2,1)S(1)}, u32[]{:S(2)}, u32[]{:S(2)}) collective-permute-start(bf16[12,96,128]{2,1,0:T(8,128)(2,1)S(1)} %get-tuple-element.11.f2), channel_id=1, source_target_pairs={{16,0},{24,8},{32,16},{40,24},{48,32},{56,40},{17,1},{25,9},{33,17... | collective-permute-start | bytes 884744 | tf_op jit(solution)/shard_map/ppermute | solution.py:201
  38.1 24.5 %collective-permute-start.4 = (bf16[12,96,128]{2,1,0:T(8,128)(2,1)S(1)}, bf16[12,96,128]{2,1,0:T(8,128)(2,1)S(1)}, u32[]{:S(2)}, u32[]{:S(2)}) collective-permute-start(bf16[12,96,128]{2,1,0:T(8,128)(2,1)S(1)} %get-tuple-element.11.f2), channel_id=1, source_target_pairs={{8,0},{16,8},{24,16},{32,24},{40,32},{48,40},{56,48},{9,1},{17,9},... | collective-permute-start | bytes 884744 | tf_op jit(solution)/shard_map/ppermute | solution.py:201
  42.7 21.3 %collective-permute-start.3 = (bf16[12,96,128]{2,1,0:T(8,128)(2,1)S(1)}, bf16[12,96,128]{2,1,0:T(8,128)(2,1)S(1)}, u32[]{:S(2)}, u32[]{:S(2)}) collective-permute-start(bf16[12,96,128]{2,1,0:T(8,128)(2,1)S(1)} %get-tuple-element.11.f2), channel_id=1, source_target_pairs={{0,8},{8,16},{16,24},{24,32},{32,40},{40,48},{48,56},{1,9},{9,17},... | collective-permute-start | bytes 884744 | tf_op jit(solution)/shard_map/ppermute | solution.py:201
  53.7 30.9 %copy-start.3 = (bf16[8,2,96,128]{3,2,1,0:T(8,128)(2,1)}, bf16[8,2,96,128]{3,2,1,0:T(8,128)(2,1)S(1)}, u32[]{:S(2)}) copy-start(bf16[8,2,96,128]{3,2,1,0:T(8,128)(2,1)S(1)} %all-to-all-done.c2) | copy-start | bytes 1179652
  53.7 30.8 %collective-permute-start.9 = (bf16[8,2,96,128]{3,2,1,0:T(8,128)(2,1)S(1)}, bf16[8,2,96,128]{3,2,1,0:T(8,128)(2,1)S(1)}, u32[]{:S(2)}, u32[]{:S(2)}) collective-permute-start(bf16[8,2,96,128]{3,2,1,0:T(8,128)(2,1)S(1)} %all-to-all-done.c2), channel_id=1, source_target_pairs={{16,0},{24,8},{32,16},{40,24},{48,32},{56,40},{17,1},{25,9},{33,17... | collective-permute-start | bytes 1179656 | tf_op jit(solution)/shard_map/ppermute | solution.py:201
  56.2 28.3 %collective-permute-start.8 = (bf16[8,2,96,128]{3,2,1,0:T(8,128)(2,1)S(1)}, bf16[8,2,96,128]{3,2,1,0:T(8,128)(2,1)S(1)}, u32[]{:S(2)}, u32[]{:S(2)}) collective-permute-start(bf16[8,2,96,128]{3,2,1,0:T(8,128)(2,1)S(1)} %all-to-all-done.c2), channel_id=1, source_target_pairs={{8,0},{16,8},{24,16},{32,24},{40,32},{48,40},{56,48},{9,1},{17,9},... | collective-permute-start | bytes 1179656 | tf_op jit(solution)/shard_map/ppermute | solution.py:201
  61.4 23.3 %copy-start.8 = (bf16[12,96,128]{2,1,0:T(8,128)(2,1)}, bf16[12,96,128]{2,1,0:T(8,128)(2,1)S(1)}, u32[]{:S(2)}) copy-start(bf16[12,96,128]{2,1,0:T(8,128)(2,1)S(1)} %collective-permute-done.5.f4) | copy-start | bytes 884740
  61.4 23.2 %collective-permute-start.7 = (bf16[8,2,96,128]{3,2,1,0:T(8,128)(2,1)S(1)}, bf16[8,2,96,128]{3,2,1,0:T(8,128)(2,1)S(1)}, u32[]{:S(2)}, u32[]{:S(2)}) collective-permute-start(bf16[8,2,96,128]{3,2,1,0:T(8,128)(2,1)S(1)} %all-to-all-done.c2), channel_id=1, source_target_pairs={{0,8},{8,16},{16,24},{24,32},{32,40},{40,48},{48,56},{1,9},{9,17},... | collective-permute-start | bytes 1179656 | tf_op jit(solution)/shard_map/ppermute | solution.py:201
  62.7 22.0 %copy-start.9 = (bf16[12,96,128]{2,1,0:T(8,128)(2,1)}, bf16[12,96,128]{2,1,0:T(8,128)(2,1)S(1)}, u32[]{:S(2)}) copy-start(bf16[12,96,128]{2,1,0:T(8,128)(2,1)S(1)} %collective-permute-done.4.f3) | copy-start | bytes 884740
  62.7 21.9 %collective-permute-start.6 = (bf16[8,2,96,128]{3,2,1,0:T(8,128)(2,1)S(1)}, bf16[8,2,96,128]{3,2,1,0:T(8,128)(2,1)S(1)}, u32[]{:S(2)}, u32[]{:S(2)}) collective-permute-start(bf16[8,2,96,128]{3,2,1,0:T(8,128)(2,1)S(1)} %all-to-all-done.c2), channel_id=1, source_target_pairs={{0,16},{8,24},{16,32},{24,40},{32,48},{40,56},{1,17},{9,25},{17,33... | collective-permute-start | bytes 1179656 | tf_op jit(solution)/shard_map/ppermute | solution.py:201
  64.0 20.6 %copy-start.10 = (bf16[12,96,128]{2,1,0:T(8,128)(2,1)}, bf16[12,96,128]{2,1,0:T(8,128)(2,1)S(1)}, u32[]{:S(2)}) copy-start(bf16[12,96,128]{2,1,0:T(8,128)(2,1)S(1)} %collective-permute-done.3.f1) | copy-start | bytes 884740
  64.0 20.5 %collective-permute-start.2 = (bf16[12,96,128]{2,1,0:T(8,128)(2,1)S(1)}, bf16[12,96,128]{2,1,0:T(8,128)(2,1)S(1)}, u32[]{:S(2)}, u32[]{:S(2)}) collective-permute-start(bf16[12,96,128]{2,1,0:T(8,128)(2,1)S(1)} %get-tuple-element.11.f2), channel_id=1, source_target_pairs={{0,16},{8,24},{16,32},{24,40},{32,48},{40,56},{1,17},{9,25},{17,33... | collective-permute-start | bytes 884744 | tf_op jit(solution)/shard_map/ppermute | solution.py:201
  84.5 0.7 copy-start.11
  84.5 0.9 copy-start.4
  84.5 1.0 copy-start.5
  84.6 1.1 copy-start.6
  84.6 1.2 copy-start.7
Sparse Core Ops, SparseCore 0:
  11.9 67.3 all-gather.2

commit v2 on v0

v2 whole, which is shorter than its diff:
```python
import jax
import jax.numpy as jnp
from jax import lax
from jax.experimental import pallas as pl
from jax.experimental.pallas import tpu as pltpu
from jax.sharding import PartitionSpec as P

C = 96
LAYERS = 8
FRAMES = 12
ROWS = 4
COLS = 128
OWN = 16
HALO = 8
WIN = OWN + 2 * HALO
GROUPS = 3
GROUP = 4
HIGH = ROWS + 2 * HALO
TAPS = 9 * C
WIDE = 896
VMEM = pl.BlockSpec(memory_space=pltpu.VMEM)
SMEM = pl.BlockSpec(memory_space=pltpu.SMEM)
F32 = jnp.float32
BF16 = jnp.bfloat16


def shifted(block, offset):
    size = block.shape[-1]
    offset %= size
    return pltpu.roll(block, size - offset, 1) if offset else block


def weights_kernel(place, taps, gain, bias, out, whole):
    for time in range(3):
        whole[time * C : (time + 1) * C, 0:TAPS] = taps[time].T
    values = jnp.concatenate([gain[...], bias[...], jnp.zeros((6, C), F32)], axis=0).T
    high = values.astype(BF16)
    rest = values - high.astype(F32)
    mid = rest.astype(BF16)
    low = (rest - mid.astype(F32)).astype(BF16)
    whole[0:C, TAPS:WIDE] = jnp.concatenate([high, mid, low, jnp.zeros((C, 8), BF16)], axis=1)
    whole[C : 3 * C, TAPS:WIDE] = jnp.zeros((2 * C, WIDE - TAPS), BF16)
    out[...] = whole[pl.ds(pl.multiple_of(place[1] * HALF, 16), HALF), :]


def windows_kernel(place, features, cached, own, spread):
    lane = lax.broadcasted_iota(jnp.int32, (C, 128), 1)
    section = place[0]

    def joined(pieces):
        total = pieces[0]
        for slot in (1, 2, 3):
            total = jnp.where(lane >= slot * WIN, pieces[slot], total)
        return total

    for group in range(GROUPS):
        for row in range(ROWS):
            pieces = []
            for slot in range(GROUP):
                amount = lax.rem(slot * WIN + HALO - OWN * section + 256, 128)
                pieces.append(pltpu.roll(features[group * GROUP + slot, row], amount, 1))
            own[group, row] = joined(pieces)
    for target in range(LAYERS):
        for pair in range(ROWS // 2):
            pieces = []
            for slot in range(4):
                tile = cached[slot % 2, 2 * pair + slot // 2]
                pieces.append(shifted(tile, OWN * target - HALO - slot * WIN))
            spread[target, pair] = joined(pieces)


STARTS = [sum(HIGH - 2 * i - 2 for i in range(layer)) for layer in range(LAYERS + 1)]
HALF = 3 * C // 2


def blocks_kernel(
    f0, f1, f2, f3, f4, c0, c1, c2, c3, c4, inside, gathered,
    out, act, taps0, taps1, taps2, sums0, sums1, sums2, early, gains, biases, weight, spare0, spare1, arrived,
):
    taps, sums, spare = (taps0, taps1, taps2), (sums0, sums1, sums2), (spare0, spare1)
    lane = lax.broadcasted_iota(jnp.int32, (C, 128), 1)
    middle = jnp.logical_and(lane % WIN >= HALO, lane % WIN < HALO + OWN)

    def tile(row):
        return pl.ds(row * 128 if isinstance(row, int) else pl.multiple_of(row * 128, 128), 128)

    def put(target, row, values):
        target[0:C, tile(row)] = pltpu.roll(values, 1, 1)
        target[C : 2 * C, tile(row)] = values
        target[2 * C : 3 * C, tile(row)] = pltpu.roll(values, 127, 1)

    def prepare(layer, group, row, stored):
        values = stored.astype(F32)
        meansq = jnp.sum(values * values, axis=0, keepdims=True) * (1.0 / C)
        scale = lax.rsqrt(meansq + 1e-06) * inside[row]
        half = values * scale * gains[layer]
        put(taps[group], row, (half * (1.0 + jnp.tanh(half))).astype(BF16))

    def multiply(layer, source, row, count, height, target, column):
        parts = [source[:, pl.ds((row + b) * 128, count * 128)] for b in range(3)]
        target[0:height, pl.ds(column * 128, count * 128)] = jnp.dot(
            weight[layer, 0:height, 0:TAPS], jnp.concatenate(parts, axis=0), preferred_element_type=F32
        )

    def finish(layer, group, row):
        now = tile(row - (layer + 1))
        cur = sums[group]
        if group:
            old, before = sums[group - 1], now
        else:
            old, before = early, tile(row - (layer + 1) + STARTS[layer])
        one = jnp.where(lane >= 3 * WIN, old[C : 2 * C, before], cur[C : 2 * C, now])
        two = jnp.where(lane >= 2 * WIN, old[0:C, before], cur[0:C, now])
        total = act[group, row].astype(F32) + biases[layer] + cur[2 * C : 3 * C, now]
        total = total + pltpu.roll(one, WIN, 1) + pltpu.roll(two, 2 * WIN, 1)
        stored = total.astype(BF16)
        act[group, row] = stored
        if layer + 1 < LAYERS:
            prepare(layer + 1, group, row, stored)

    def emit(layer, group):
        for pair in range(ROWS // 2):
            even = act[group, HALO + 2 * pair]
            odd = pltpu.roll(act[group, HALO + 2 * pair + 1], OWN, 1)
            out[layer, group * 2 + pair] = jnp.where(middle, even, odd)

    def loop(count, step, unroll=1):
        def run(index, _):
            step(index)
            return 0

        lax.fori_loop(0, count, run, 0, unroll=unroll)

    copies = [
        pltpu.make_async_copy(gathered.at[layer], weight.at[layer], arrived.at[layer]) for layer in range(LAYERS)
    ]
    for copy in copies:
        copy.start()
    for at, part in enumerate((f0, f1, f2, f3, f4)):
        act[:, at * ROWS : (at + 1) * ROWS] = part[...]
    for layer in range(LAYERS):
        copies[layer].wait()

        def column(at, layer=layer):
            parts = [weight[layer, 0:C, at + 8 * i : at + 8 * i + 1].astype(F32) for i in range(3)]
            return jnp.broadcast_to(parts[0] + parts[1] + parts[2], (C, 128))

        gains[layer] = 0.5 * column(TAPS)
        biases[layer] = column(TAPS + 1)
        if layer == 0:
            for group in range(GROUPS):
                loop(HIGH, lambda row, group=group: prepare(0, group, row, act[group, row]), 4)

    for layer in range(LAYERS):
        source = spare[layer % 2]
        for row in range(layer, HIGH - layer):
            stored = (c0, c1, c2, c3, c4)[row // ROWS][layer, row % ROWS // 2]
            put(source, row, stored if row % 2 else pltpu.roll(stored, 64, 1))
        multiply(layer, source, layer, HIGH - 2 * layer - 2, 2 * C, early, STARTS[layer])

    behind = None
    for layer in range(LAYERS):
        rows = HIGH - 2 * layer - 2
        for group in range(GROUPS):

            multiply(layer, taps[group], layer, rows, 3 * C, sums[group], 0)
            if behind is not None:
                for row in range(behind[0] + 1, HIGH - behind[0] - 1):
                    finish(*behind, row)
                emit(*behind)
            behind = (layer, group)
    loop(ROWS, lambda index: finish(*behind, LAYERS + index))
    emit(*behind)


def join_kernel(parts, out):
    lane = lax.broadcasted_iota(jnp.int32, (C, 128), 1)
    for at in range(FRAMES // 2):
        tiles = [shifted(parts[source, at], HALO) for source in range(LAYERS)]
        for bit in (1, 2, 4):
            low = (lane // OWN) % (2 * bit) < bit
            for first in range(LAYERS):
                if first & bit:
                    continue
                one, two = tiles[first], tiles[first + bit]
                tiles[first] = jnp.where(low, one, shifted(two, -OWN * bit))
                tiles[first + bit] = jnp.where(low, shifted(one, OWN * bit), two)
        for k in range(LAYERS):
            out[at // 2 * GROUP + k // 2, at % 2 * 2 + k % 2] = tiles[k]


def along(block, axes, distance):
    count = lax.axis_size(axes)
    route = [(i, i + distance) for i in range(count) if 0 <= i + distance < count]
    return lax.ppermute(block, axes, route)


def mended(block):
    sections, cols = lax.axis_size("section"), lax.axis_size("col")
    last = (sections - 1) * cols
    route = [(i, i + 1) for i in range(cols - 1)] + [(last + i + 1, last + i) for i in range(cols - 1)]
    beyond = lax.ppermute(block, ("section", "col"), route)
    section = lax.axis_index("section")
    column = jnp.arange(128, dtype=jnp.int32) % WIN
    ends = (section == 0) & (column < HALO) | (section == sections - 1) & (column >= WIN - HALO)
    return jnp.where(ends, beyond, block)


def vmem(size):
    return pltpu.CompilerParams(vmem_limit_bytes=size << 20)


def body(features, conv_weight, norm_gain, conv_bias, cached):
    section = lax.axis_index("section")
    row = lax.axis_index(("x", "core"))
    col = lax.axis_index("col")
    place = jnp.stack([section, lax.axis_index("core")]).astype(jnp.int32)

    mine = pl.pallas_call(
        weights_kernel,
        in_specs=[SMEM] + [VMEM] * 3,
        out_shape=jax.ShapeDtypeStruct((HALF, WIDE), BF16),
        out_specs=VMEM,
        scratch_shapes=[pltpu.VMEM((3 * C, WIDE), BF16)],
        compiler_params=vmem(32),
        name="weights",
    )(place, conv_weight.reshape(3, TAPS, C), norm_gain, conv_bias)
    gathered = lax.all_gather(mine, ("section", "core")).reshape(LAYERS, 3 * C, WIDE)

    own, spread = pl.pallas_call(
        windows_kernel,
        in_specs=[SMEM] + [VMEM] * 2,
        out_shape=[
            jax.ShapeDtypeStruct((GROUPS, ROWS, C, 128), BF16),
            jax.ShapeDtypeStruct((LAYERS, 2, C, 128), BF16),
        ],
        out_specs=[VMEM] * 2,
        compiler_params=vmem(32),
        name="windows",
    )(place, features, cached[0])
    stored = mended(lax.all_to_all(spread, "section", 0, 0, tiled=True))
    own = mended(own)
    steps = (2, 1, -1, -2)
    f = [along(own, ("x", "core"), d) for d in steps]
    c = [along(stored[0 : LAYERS // 2] if abs(d) == 2 else stored, ("x", "core"), d) for d in steps]
    f = [f[0], f[1], own, f[2], f[3]]
    c = [c[0], c[1], stored, c[2], c[3]]

    at_row = row * ROWS - HALO + jnp.arange(HIGH, dtype=jnp.int32)[:, None, None]
    at_col = col * COLS + section * OWN - HALO + jnp.arange(128, dtype=jnp.int32)[None, None, :] % WIN
    high = lax.axis_size(("x", "core")) * ROWS
    wide = lax.axis_size("col") * COLS
    inside = (at_row >= 0) & (at_row < high) & (at_col >= 0) & (at_col < wide)
    inside = inside.astype(F32)

    packed = pl.pallas_call(
        blocks_kernel,
        in_specs=[VMEM] * 11 + [pl.BlockSpec(memory_space=pl.ANY)],
        out_shape=jax.ShapeDtypeStruct((LAYERS, FRAMES // 2, C, 128), BF16),
        out_specs=VMEM,
        scratch_shapes=[
            pltpu.VMEM((GROUPS, HIGH, C, 128), BF16),
            *[pltpu.VMEM((3 * C, HIGH * 128), BF16)] * GROUPS,
            *[pltpu.VMEM((3 * C, (HIGH - 2) * 128), F32)] * GROUPS,
            pltpu.VMEM((2 * C, STARTS[LAYERS] * 128), F32),
            pltpu.VMEM((LAYERS, C, 128), F32),
            pltpu.VMEM((LAYERS, C, 128), F32),
            pltpu.VMEM((LAYERS, 3 * C, WIDE), BF16),
            *[pltpu.VMEM((3 * C, HIGH * 128), BF16)] * 2,
            pltpu.SemaphoreType.DMA((LAYERS,)),
        ],
        compiler_params=vmem(56),
        cost_estimate=pl.CostEstimate(flops=18_000_000_000, bytes_accessed=8_000_000, transcendentals=0),
        name="blocks",
    )(*f, *c, inside, gathered)
    parts = lax.all_to_all(packed, "section", 0, 0, tiled=True)
    joined = pl.pallas_call(
        join_kernel,
        in_specs=[VMEM],
        out_shape=jax.ShapeDtypeStruct((FRAMES, ROWS, C, COLS), BF16),
        out_specs=VMEM,
        compiler_params=vmem(32),
        name="join",
    )(parts)
    return joined[None]


def solution(mesh):
    sections, rows, cols = (mesh.shape[name] for name in ("section", "row", "col"))
    cores = jax.sharding.Mesh(mesh.devices.reshape(sections, rows // 2, 2, cols), ("section", "x", "core", "col"))
    return jax.shard_map(
        body,
        mesh=cores,
        in_specs=(
            P(None, ("x", "core"), None, "col"),
            P("section", None, None, None, None, None),
            P("section", None),
            P("section", None),
            P("section", None, ("x", "core"), None, "col"),
        ),
        out_specs=P("section", None, ("x", "core"), None, "col"),
        check_vma=False,
    )
```

time: 663 us -> 158 us (0.24)
  the two profiles are of different devices: /device:TPU:250 before, /device:TPU:199 now
where the time goes in v2:
time: 158 us; the launch traced here: 157 us
  Pallas kernels  45.2 us (29%)
  starting transfers between devices  39 us (25%)
  blocking collectives  35 us (22%)
  waiting for transfers between devices  19.2 us (12%)
  between operations  13.7 us (9%)
  local copies, waits for them, and re-layouts  4.32 us (3%)
    pallas_call x1, Pallas kernels, body(): pl.pallas_call(blocks_kernel, in_specs=[VMEM] * 11 + [pl.BlockSpec(memory...  38.5 us
    all_to_all x1, blocking collectives, body(): parts = lax.all_to_all(packed, 'section', 0, 0, tiled=True)  35 us
    ppermute x8, starting transfers between devices, along(): return lax.ppermute(block, axes, route)  21 us
    ppermute x2, starting transfers between devices, mended(): beyond = lax.ppermute(block, ('section', 'col'), route)  11.1 us
    ppermute x8, waiting for transfers between devices, along(): return lax.ppermute(block, axes, route)  9.73 us
    all_to_all x1, waiting for transfers between devices, body(): stored = mended(lax.all_to_all(spread, 'section', 0, 0, tiled=True))  9.4 us
    all_to_all x1, starting transfers between devices, body(): stored = mended(lax.all_to_all(spread, 'section', 0, 0, tiled=True))  6.82 us
    unnamed x30, local copies, waits for them, and re-layouts  4.31 us
  transfers between devices with their start and end apart: 12, of which 3 were waited for; matrix products, arithmetic and copies ran while one was open for 1% of the time, Pallas kernels for 1%

profile of v2, /device:TPU:199, one launch (start us, length us, event | category | flops | bytes accessed | tf_op | source)
XLA Modules:
  0.0 157.2 jit_solution(6996344000272518389)
XLA Ops:
  6.5 0.1 pad_add_fusion.place
  6.6 1.2 copy-done.1
  7.8 0.7 copy-done.3
  8.4 0.7 copy-done.4
  9.1 1.7 %weights.1 = bf16[144,896]{1,0:T(8,128)(2,1)} custom-call(s32[2]{0:T(128)S(1)} %pad_add_fusion.place, bf16[3,864,96]{2,1,0:T(8,128)(2,1)S(1)} %bitcast.6, f32[1,96]{1,0:T(1,128)S(1)} %copy-done.3, f32[1,96]{1,0:T(1,128)S(1)} %copy-done.4), custom_call_target="tpu_custom_call" | custom-call | tf_op jit(solution)/shard_map/weights/pallas_call | solution.py:219
  10.8 0.0 all-gather.3.cloned.1.call-update
  10.8 0.0 copy-start.2
  10.8 0.9 copy-done.2
  11.8 2.1 %windows.1 = (bf16[3,4,96,128]{3,2,1,0:T(8,128)(2,1)S(1)}, bf16[8,2,96,128]{3,2,1,0:T(8,128)(2,1)}) custom-call(s32[2]{0:T(128)S(1)} %pad_add_fusion.place, bf16[12,4,96,128]{3,2,1,0:T(8,128)(2,1)S(1)} %copy-done, bf16[2,4,96,128]{3,2,1,0:T(8,128)(2,1)S(1)} %bitcast.7), custom_call_target="tpu_custom_call" | custom-call | tf_op jit(solution)/shard_map/windows/pallas_call | solution.py:230
  13.8 6.8 %all-to-all-start = ((bf16[8,2,96,128]{3,2,1,0:T(8,128)(2,1)}), bf16[8,2,96,128]{3,2,1,0:T(8,128)(2,1)S(1)}, u32[]{:S(2)}, u32[]{:S(2)}) async-start(bf16[8,2,96,128]{3,2,1,0:T(8,128)(2,1)} %get-tuple-element.8), calls=%async_computation | async-start | bytes 786432 | tf_op jit(solution)/shard_map/all_to_all | solution.py:241
  20.6 5.2 %collective-permute-start = (bf16[3,4,96,128]{3,2,1,0:T(8,128)(2,1)S(1)}, bf16[3,4,96,128]{3,2,1,0:T(8,128)(2,1)S(1)}, u32[]{:S(2)}, u32[]{:S(2)}) collective-permute-start(bf16[3,4,96,128]{3,2,1,0:T(8,128)(2,1)S(1)} %get-tuple-element.7), channel_id=1, source_target_pairs={{0,1},{1,2},{2,3},{3,4},{4,5},{5,6},{6,7},{449,448},{450,449},{451... | collective-permute-start | bytes 884744 | tf_op jit(solution)/shard_map/ppermute | solution.py:202
  25.8 9.4 %all-to-all-done = bf16[8,2,96,128]{3,2,1,0:T(8,128)(2,1)S(1)} async-done(((bf16[8,2,96,128]{3,2,1,0:T(8,128)(2,1)}), bf16[8,2,96,128]{3,2,1,0:T(8,128)(2,1)S(1)}, u32[]{:S(2)}, u32[]{:S(2)}) %all-to-all-start) | async-done | bytes 393248 | tf_op jit(solution)/shard_map/all_to_all | solution.py:241
  35.3 5.9 %collective-permute-start.5 = (bf16[8,2,96,128]{3,2,1,0:T(8,128)(2,1)S(1)}, bf16[8,2,96,128]{3,2,1,0:T(8,128)(2,1)S(1)}, u32[]{:S(2)}, u32[]{:S(2)}) collective-permute-start(bf16[8,2,96,128]{3,2,1,0:T(8,128)(2,1)S(1)} %all-to-all-done), channel_id=1, source_target_pairs={{0,1},{1,2},{2,3},{3,4},{4,5},{5,6},{6,7},{449,448},{450,449},{451... | collective-permute-start | bytes 1179656 | tf_op jit(solution)/shard_map/ppermute | solution.py:202
  41.2 0.0 collective-permute-done
  41.3 2.4 %collective-permute-start.4 = (bf16[3,4,96,128]{3,2,1,0:T(8,128)(2,1)S(1)}, bf16[3,4,96,128]{3,2,1,0:T(8,128)(2,1)S(1)}, u32[]{:S(2)}, u32[]{:S(2)}) collective-permute-start(bf16[3,4,96,128]{3,2,1,0:T(8,128)(2,1)S(1)} %broadcast_select_fusion.1.f2), channel_id=1, source_target_pairs={{16,0},{24,8},{32,16},{40,24},{48,32},{56,40},{17,1},{25,9},{33,17... | collective-permute-start | bytes 884744 | tf_op jit(solution)/shard_map/ppermute | solution.py:195
  43.7 4.6 %collective-permute-start.3 = (bf16[3,4,96,128]{3,2,1,0:T(8,128)(2,1)S(1)}, bf16[3,4,96,128]{3,2,1,0:T(8,128)(2,1)S(1)}, u32[]{:S(2)}, u32[]{:S(2)}) collective-permute-start(bf16[3,4,96,128]{3,2,1,0:T(8,128)(2,1)S(1)} %broadcast_select_fusion.1.f2), channel_id=1, source_target_pairs={{8,0},{16,8},{24,16},{32,24},{40,32},{48,40},{56,48},{9,1},{17,9},... | collective-permute-start | bytes 884744 | tf_op jit(solution)/shard_map/ppermute | solution.py:195
  48.4 1.3 collective-permute-start.2
  49.7 3.1 %collective-permute-start.8 = (bf16[8,2,96,128]{3,2,1,0:T(8,128)(2,1)S(1)}, bf16[8,2,96,128]{3,2,1,0:T(8,128)(2,1)S(1)}, u32[]{:S(2)}, u32[]{:S(2)}) collective-permute-start(bf16[8,2,96,128]{3,2,1,0:T(8,128)(2,1)S(1)} %broadcast_select_fusion.c2), channel_id=1, source_target_pairs={{8,0},{16,8},{24,16},{32,24},{40,32},{48,40},{56,48},{9,1},{17,9},... | collective-permute-start | bytes 1179656 | tf_op jit(solution)/shard_map/ppermute | solution.py:195
  52.8 1.3 collective-permute-start.7
  54.1 1.3 collective-permute-start.1
  55.5 5.7 %collective-permute-start.9 = (bf16[4,2,96,128]{3,2,1,0:T(8,128)(2,1)S(1)}, bf16[4,2,96,128]{3,2,1,0:T(8,128)(2,1)S(1)}, u32[]{:S(2)}, u32[]{:S(2)}) collective-permute-start(bf16[4,2,96,128]{3,2,1,0:T(8,128)(2,1)S(1)} %slice.5), channel_id=1, source_target_pairs={{16,0},{24,8},{32,16},{40,24},{48,32},{56,40},{17,1},{25,9},{33,17... | collective-permute-start | bytes 589832 | tf_op jit(solution)/shard_map/ppermute | solution.py:195
  61.2 1.3 collective-permute-start.6
  62.5 0.7 and_convert_fusion.inside
  63.2 7.4 %collective-permute-done.1.f0 = bf16[3,4,96,128]{3,2,1,0:T(8,128)(2,1)S(1)} collective-permute-done((bf16[3,4,96,128]{3,2,1,0:T(8,128)(2,1)S(1)}, bf16[3,4,96,128]{3,2,1,0:T(8,128)(2,1)S(1)}, u32[]{:S(2)}, u32[]{:S(2)}) %collective-permute-start.1) | collective-permute-done | bytes 294944 | tf_op jit(solution)/shard_map/ppermute | solution.py:195
  70.6 2.3 %collective-permute-done.6.c0 = bf16[4,2,96,128]{3,2,1,0:T(8,128)(2,1)S(1)} collective-permute-done((bf16[4,2,96,128]{3,2,1,0:T(8,128)(2,1)S(1)}, bf16[4,2,96,128]{3,2,1,0:T(8,128)(2,1)S(1)}, u32[]{:S(2)}, u32[]{:S(2)}) %collective-permute-start.6) | collective-permute-done | bytes 196640 | tf_op jit(solution)/shard_map/ppermute | solution.py:195
  73.0 0.0 all-gather.3.cloned.1.call-done
  73.1 0.6 copy-done.14
  73.6 0.2 copy-done.7
  73.8 0.2 copy-done.8
  73.9 38.5 %blocks.1 = bf16[8,6,96,128]{3,2,1,0:T(8,128)(2,1)} custom-call(bf16[3,4,96,128]{3,2,1,0:T(8,128)(2,1)} %copy-done.12, bf16[3,4,96,128]{3,2,1,0:T(8,128)(2,1)} %copy-done.11, bf16[3,4,96,128]{3,2,1,0:T(8,128)(2,1)} %copy-done.6, bf16[3,4,96,128]{3,2,1,0:T(8,128)(2,1)} %copy-done.10, bf16[3,4,96,128]{3,2,1,0:T(8,128)(2,1)} %copy-done.9, ...), custom_call_target="tpu_custom_call" | custom-call | flops 17999998976 | bytes 8000000 | tf_op jit(solution)/shard_map/blocks/pallas_call | solution.py:256
  112.5 35.0 %all_to_all.10.parts = bf16[8,6,96,128]{3,2,1,0:T(8,128)(2,1)S(1)} all-to-all(bf16[8,6,96,128]{3,2,1,0:T(8,128)(2,1)} %blocks.1), channel_id=1, replica_groups=mesh['section'=8,'x'=4,'core'=2,'col'=8] {'section'}, dimensions={0} | all-to-all | bytes 2359296 | tf_op jit(solution)/shard_map/all_to_all | solution.py:276
  147.5 2.9 %join.1 = bf16[12,4,96,128]{3,2,1,0:T(8,128)(2,1)} custom-call(bf16[8,6,96,128]{3,2,1,0:T(8,128)(2,1)S(1)} %all_to_all.10.parts), custom_call_target="tpu_custom_call" | custom-call | tf_op jit(solution)/shard_map/join/pallas_call | solution.py:277
  (36 shorter events, 0.2 us)
Async XLA Ops:
  6.5 4.3 %copy-start = (bf16[12,4,96,128]{3,2,1,0:T(8,128)(2,1)S(1)}, bf16[12,4,96,128]{3,2,1,0:T(8,128)(2,1)}, u32[]{:S(2)}) copy-start(bf16[12,4,96,128]{3,2,1,0:T(8,128)(2,1)} %features.1) | copy-start | bytes 3538948
  6.5 66.5 %all-gather.3.cloned.1.call-start = ((), (), s32[]{:S(2)}) async-start(), calls=%async_computation.2 | async-start | bytes 4386816 | tf_op jit(solution)/shard_map/all_gather | solution.py:228
  6.6 1.2 copy-start.1
  7.8 0.7 copy-start.3
  8.4 0.7 copy-start.4
  10.8 0.9 copy-start.2
  13.8 21.4 %all-to-all-start = ((bf16[8,2,96,128]{3,2,1,0:T(8,128)(2,1)}), bf16[8,2,96,128]{3,2,1,0:T(8,128)(2,1)S(1)}, u32[]{:S(2)}, u32[]{:S(2)}) async-start(bf16[8,2,96,128]{3,2,1,0:T(8,128)(2,1)} %get-tuple-element.8), calls=%async_computation | async-start | bytes 786432 | tf_op jit(solution)/shard_map/all_to_all | solution.py:241
  20.6 20.6 %collective-permute-start = (bf16[3,4,96,128]{3,2,1,0:T(8,128)(2,1)S(1)}, bf16[3,4,96,128]{3,2,1,0:T(8,128)(2,1)S(1)}, u32[]{:S(2)}, u32[]{:S(2)}) collective-permute-start(bf16[3,4,96,128]{3,2,1,0:T(8,128)(2,1)S(1)} %get-tuple-element.7), channel_id=1, source_target_pairs={{0,1},{1,2},{2,3},{3,4},{4,5},{5,6},{6,7},{449,448},{450,449},{451... | collective-permute-start | bytes 884744 | tf_op jit(solution)/shard_map/ppermute | solution.py:202
  35.3 14.4 %collective-permute-start.5 = (bf16[8,2,96,128]{3,2,1,0:T(8,128)(2,1)S(1)}, bf16[8,2,96,128]{3,2,1,0:T(8,128)(2,1)S(1)}, u32[]{:S(2)}, u32[]{:S(2)}) collective-permute-start(bf16[8,2,96,128]{3,2,1,0:T(8,128)(2,1)S(1)} %all-to-all-done), channel_id=1, source_target_pairs={{0,1},{1,2},{2,3},{3,4},{4,5},{5,6},{6,7},{449,448},{450,449},{451... | collective-permute-start | bytes 1179656 | tf_op jit(solution)/shard_map/ppermute | solution.py:202
  41.2 31.8 %copy-start.6 = (bf16[3,4,96,128]{3,2,1,0:T(8,128)(2,1)}, bf16[3,4,96,128]{3,2,1,0:T(8,128)(2,1)S(1)}, u32[]{:S(2)}) copy-start(bf16[3,4,96,128]{3,2,1,0:T(8,128)(2,1)S(1)} %broadcast_select_fusion.1.f2) | copy-start | bytes 884740
  41.3 12.9 %collective-permute-start.4 = (bf16[3,4,96,128]{3,2,1,0:T(8,128)(2,1)S(1)}, bf16[3,4,96,128]{3,2,1,0:T(8,128)(2,1)S(1)}, u32[]{:S(2)}, u32[]{:S(2)}) collective-permute-start(bf16[3,4,96,128]{3,2,1,0:T(8,128)(2,1)S(1)} %broadcast_select_fusion.1.f2), channel_id=1, source_target_pairs={{16,0},{24,8},{32,16},{40,24},{48,32},{56,40},{17,1},{25,9},{33,17... | collective-permute-start | bytes 884744 | tf_op jit(solution)/shard_map/ppermute | solution.py:195
  43.7 11.8 %collective-permute-start.3 = (bf16[3,4,96,128]{3,2,1,0:T(8,128)(2,1)S(1)}, bf16[3,4,96,128]{3,2,1,0:T(8,128)(2,1)S(1)}, u32[]{:S(2)}, u32[]{:S(2)}) collective-permute-start(bf16[3,4,96,128]{3,2,1,0:T(8,128)(2,1)S(1)} %broadcast_select_fusion.1.f2), channel_id=1, source_target_pairs={{8,0},{16,8},{24,16},{32,24},{40,32},{48,40},{56,48},{9,1},{17,9},... | collective-permute-start | bytes 884744 | tf_op jit(solution)/shard_map/ppermute | solution.py:195
  48.4 12.9 %collective-permute-start.2 = (bf16[3,4,96,128]{3,2,1,0:T(8,128)(2,1)S(1)}, bf16[3,4,96,128]{3,2,1,0:T(8,128)(2,1)S(1)}, u32[]{:S(2)}, u32[]{:S(2)}) collective-permute-start(bf16[3,4,96,128]{3,2,1,0:T(8,128)(2,1)S(1)} %broadcast_select_fusion.1.f2), channel_id=1, source_target_pairs={{0,8},{8,16},{16,24},{24,32},{32,40},{40,48},{48,56},{1,9},{9,17},... | collective-permute-start | bytes 884744 | tf_op jit(solution)/shard_map/ppermute | solution.py:195
  49.7 23.3 %copy-start.5 = (bf16[8,2,96,128]{3,2,1,0:T(8,128)(2,1)}, bf16[8,2,96,128]{3,2,1,0:T(8,128)(2,1)S(1)}, u32[]{:S(2)}) copy-start(bf16[8,2,96,128]{3,2,1,0:T(8,128)(2,1)S(1)} %broadcast_select_fusion.c2) | copy-start | bytes 1179652
  49.7 23.2 %collective-permute-start.8 = (bf16[8,2,96,128]{3,2,1,0:T(8,128)(2,1)S(1)}, bf16[8,2,96,128]{3,2,1,0:T(8,128)(2,1)S(1)}, u32[]{:S(2)}, u32[]{:S(2)}) collective-permute-start(bf16[8,2,96,128]{3,2,1,0:T(8,128)(2,1)S(1)} %broadcast_select_fusion.c2), channel_id=1, source_target_pairs={{8,0},{16,8},{24,16},{32,24},{40,32},{48,40},{56,48},{9,1},{17,9},... | collective-permute-start | bytes 1179656 | tf_op jit(solution)/shard_map/ppermute | solution.py:195
  52.8 20.2 %collective-permute-start.7 = (bf16[8,2,96,128]{3,2,1,0:T(8,128)(2,1)S(1)}, bf16[8,2,96,128]{3,2,1,0:T(8,128)(2,1)S(1)}, u32[]{:S(2)}, u32[]{:S(2)}) collective-permute-start(bf16[8,2,96,128]{3,2,1,0:T(8,128)(2,1)S(1)} %broadcast_select_fusion.c2), channel_id=1, source_target_pairs={{0,8},{8,16},{16,24},{24,32},{32,40},{40,48},{48,56},{1,9},{9,17},... | collective-permute-start | bytes 1179656 | tf_op jit(solution)/shard_map/ppermute | solution.py:195
  54.1 18.9 %copy-start.9 = (bf16[3,4,96,128]{3,2,1,0:T(8,128)(2,1)}, bf16[3,4,96,128]{3,2,1,0:T(8,128)(2,1)S(1)}, u32[]{:S(2)}) copy-start(bf16[3,4,96,128]{3,2,1,0:T(8,128)(2,1)S(1)} %collective-permute-done.4.f4) | copy-start | bytes 884740
  54.1 16.5 %collective-permute-start.1 = (bf16[3,4,96,128]{3,2,1,0:T(8,128)(2,1)S(1)}, bf16[3,4,96,128]{3,2,1,0:T(8,128)(2,1)S(1)}, u32[]{:S(2)}, u32[]{:S(2)}) collective-permute-start(bf16[3,4,96,128]{3,2,1,0:T(8,128)(2,1)S(1)} %broadcast_select_fusion.1.f2), channel_id=1, source_target_pairs={{0,16},{8,24},{16,32},{24,40},{32,48},{40,56},{1,17},{9,25},{17,33... | collective-permute-start | bytes 884744 | tf_op jit(solution)/shard_map/ppermute | solution.py:195
  55.5 17.6 %copy-start.10 = (bf16[3,4,96,128]{3,2,1,0:T(8,128)(2,1)}, bf16[3,4,96,128]{3,2,1,0:T(8,128)(2,1)S(1)}, u32[]{:S(2)}) copy-start(bf16[3,4,96,128]{3,2,1,0:T(8,128)(2,1)S(1)} %collective-permute-done.3.f3) | copy-start | bytes 884740
  55.5 15.1 %collective-permute-start.9 = (bf16[4,2,96,128]{3,2,1,0:T(8,128)(2,1)S(1)}, bf16[4,2,96,128]{3,2,1,0:T(8,128)(2,1)S(1)}, u32[]{:S(2)}, u32[]{:S(2)}) collective-permute-start(bf16[4,2,96,128]{3,2,1,0:T(8,128)(2,1)S(1)} %slice.5), channel_id=1, source_target_pairs={{16,0},{24,8},{32,16},{40,24},{48,32},{56,40},{17,1},{25,9},{33,17... | collective-permute-start | bytes 589832 | tf_op jit(solution)/shard_map/ppermute | solution.py:195
  61.2 11.8 %copy-start.11 = (bf16[3,4,96,128]{3,2,1,0:T(8,128)(2,1)}, bf16[3,4,96,128]{3,2,1,0:T(8,128)(2,1)S(1)}, u32[]{:S(2)}) copy-start(bf16[3,4,96,128]{3,2,1,0:T(8,128)(2,1)S(1)} %collective-permute-done.2.f1) | copy-start | bytes 884740
  61.2 11.7 %collective-permute-start.6 = (bf16[4,2,96,128]{3,2,1,0:T(8,128)(2,1)S(1)}, bf16[4,2,96,128]{3,2,1,0:T(8,128)(2,1)S(1)}, u32[]{:S(2)}, u32[]{:S(2)}) collective-permute-start(bf16[4,2,96,128]{3,2,1,0:T(8,128)(2,1)S(1)} %slice.5), channel_id=1, source_target_pairs={{0,16},{8,24},{16,32},{24,40},{32,48},{40,56},{1,17},{9,25},{17,33... | collective-permute-start | bytes 589832 | tf_op jit(solution)/shard_map/ppermute | solution.py:195
  70.6 2.4 %copy-start.12 = (bf16[3,4,96,128]{3,2,1,0:T(8,128)(2,1)}, bf16[3,4,96,128]{3,2,1,0:T(8,128)(2,1)S(1)}, u32[]{:S(2)}) copy-start(bf16[3,4,96,128]{3,2,1,0:T(8,128)(2,1)S(1)} %collective-permute-done.1.f0) | copy-start | bytes 884740
  70.6 2.4 %copy-start.13 = (bf16[4,2,96,128]{3,2,1,0:T(8,128)(2,1)}, bf16[4,2,96,128]{3,2,1,0:T(8,128)(2,1)S(1)}, u32[]{:S(2)}) copy-start(bf16[4,2,96,128]{3,2,1,0:T(8,128)(2,1)S(1)} %collective-permute-done.9.c4) | copy-start | bytes 589828
  72.9 0.7 copy-start.14
  72.9 0.8 copy-start.7
  73.0 1.0 copy-start.8
Sparse Core Ops, SparseCore 0:
  10.9 49.0 all-gather.2

commit v3 on v2

--- a/solution.py
+++ b/solution.py
@@ -30,7 +30,13 @@
     return pltpu.roll(block, size - offset, 1) if offset else block
 
 
-def weights_kernel(place, taps, gain, bias, out, whole):
+def weights_kernel(place, taps_at, gain_at, bias_at, out, taps, gain, bias, whole, arrived):
+    pairs = ((taps_at, taps), (gain_at, gain), (bias_at, bias))
+    copies = [pltpu.make_async_copy(*pair, arrived.at[at]) for at, pair in enumerate(pairs)]
+    for copy in copies:
+        copy.start()
+    for copy in copies:
+        copy.wait()
     for time in range(3):
         whole[time * C : (time + 1) * C, 0:TAPS] = taps[time].T
     values = jnp.concatenate([gain[...], bias[...], jnp.zeros((6, C), F32)], axis=0).T
@@ -43,9 +49,31 @@
     out[...] = whole[pl.ds(pl.multiple_of(place[1] * HALF, 16), HALF), :]
 
 
-def windows_kernel(place, features, cached, own, spread):
+def edges_kernel(features, cached, right, left):
+    lane = lax.broadcasted_iota(jnp.int32, (C, 128), 1)
+    for group in range(4):
+        ends = heads = jnp.zeros((C, 128), BF16)
+        for inner in range(4):
+            frame = group * 4 + inner
+            if frame >= FRAMES + 2:
+                continue
+            for row in range(ROWS):
+                tile = features[frame, row] if frame < FRAMES else cached[frame - FRAMES, row]
+                at = inner * 32 + row * HALO
+                here = jnp.logical_and(lane >= at, lane < at + HALO)
+                ends = jnp.where(here, shifted(tile, 120 - at), ends)
+                heads = jnp.where(here, shifted(tile, -at), heads)
+        right[group] = ends
+        left[group] = heads
+
+
+def windows_kernel(place, features, cached, before, after, own, spread):
     lane = lax.broadcasted_iota(jnp.int32, (C, 128), 1)
     section = place[0]
+
+    def edge(block, frame, row, slot, column):
+        at = frame % 4 * 32 + row * HALO
+        return shifted(block[frame // 4], at - slot * WIN - column)
 
     def joined(pieces):
         total = pieces[0]
@@ -53,6 +81,27 @@
             total = jnp.where(lane >= slot * WIN, pieces[slot], total)
         return total
 
+    def mended(total, block, cells, column):
+        for slot, (frame, row) in enumerate(cells):
+            at = slot * WIN + column
+            here = jnp.logical_and(lane >= at, lane < at + HALO)
+            total = jnp.where(here, edge(block, frame, row, slot, column), total)
+        return total
+
+    for target in range(LAYERS):
+        for pair in range(ROWS // 2):
+            cells = [(slot % 2, 2 * pair + slot // 2) for slot in range(4)]
+            pieces = [
+                shifted(cached[frame, row], OWN * target - HALO - slot * WIN)
+                for slot, (frame, row) in enumerate(cells)
+            ]
+            total = joined(pieces)
+            cells = [(FRAMES + frame, row) for frame, row in cells]
+            if target == 0:
+                total = mended(total, before, cells, 0)
+            if target == LAYERS - 1:
+                total = mended(total, after, cells, WIN - HALO)
+            spread[target, pair] = total
     for group in range(GROUPS):
         for row in range(ROWS):
             pieces = []
@@ -60,15 +109,23 @@
                 amount = lax.rem(slot * WIN + HALO - OWN * section + 256, 128)
                 pieces.append(pltpu.roll(features[group * GROUP + slot, row], amount, 1))
             own[group, row] = joined(pieces)
-    for target in range(LAYERS):
-        for pair in range(ROWS // 2):
-            pieces = []
-            for slot in range(4):
-                tile = cached[slot % 2, 2 * pair + slot // 2]
-                pieces.append(shifted(tile, OWN * target - HALO - slot * WIN))
-            spread[target, pair] = joined(pieces)
-
-
+
+    @pl.when(section == 0)
+    def _():
+        for group in range(GROUPS):
+            for row in range(ROWS):
+                cells = [(group * GROUP + slot, row) for slot in range(GROUP)]
+                own[group, row] = mended(own[group, row], before, cells, 0)
+
+    @pl.when(section == LAYERS - 1)
+    def _():
+        for group in range(GROUPS):
+            for row in range(ROWS):
+                cells = [(group * GROUP + slot, row) for slot in range(GROUP)]
+                own[group, row] = mended(own[group, row], after, cells, WIN - HALO)
+
+
+ODD = HIGH // 2
 STARTS = [sum(HIGH - 2 * i - 2 for i in range(layer)) for layer in range(LAYERS + 1)]
 HALF = 3 * C // 2
 
@@ -106,11 +163,14 @@
         now = tile(row - (layer + 1))
         cur = sums[group]
         if group:
-            old, before = sums[group - 1], now
+            old_one, old_two = sums[group - 1][C : 2 * C, now], sums[group - 1][0:C, now]
         else:
-            old, before = early, tile(row - (layer + 1) + STARTS[layer])
-        one = jnp.where(lane >= 3 * WIN, old[C : 2 * C, before], cur[C : 2 * C, now])
-        two = jnp.where(lane >= 2 * WIN, old[0:C, before], cur[0:C, now])
+            pair = tile((row - (layer + 1) + STARTS[layer]) // 2)
+            old_one, old_two = early[C : 2 * C, pair], early[0:C, pair]
+            if (row - layer) % 2:
+                old_one, old_two = pltpu.roll(old_one, 64, 1), pltpu.roll(old_two, 64, 1)
+        one = jnp.where(lane >= 3 * WIN, old_one, cur[C : 2 * C, now])
+        two = jnp.where(lane >= 2 * WIN, old_two, cur[0:C, now])
         total = act[group, row].astype(F32) + biases[layer] + cur[2 * C : 3 * C, now]
         total = total + pltpu.roll(one, WIN, 1) + pltpu.roll(two, 2 * WIN, 1)
         stored = total.astype(BF16)
@@ -147,16 +207,23 @@
 
         gains[layer] = 0.5 * column(TAPS)
         biases[layer] = column(TAPS + 1)
-        if layer == 0:
-            for group in range(GROUPS):
-                loop(HIGH, lambda row, group=group: prepare(0, group, row, act[group, row]), 4)
+    def mixed(one, two):
+        return pltpu.roll(jnp.where(lane >= 64, one, two), 64, 1)
 
     for layer in range(LAYERS):
-        source = spare[layer % 2]
-        for row in range(layer, HIGH - layer):
-            stored = (c0, c1, c2, c3, c4)[row // ROWS][layer, row % ROWS // 2]
-            put(source, row, stored if row % 2 else pltpu.roll(stored, 64, 1))
-        multiply(layer, source, layer, HIGH - 2 * layer - 2, 2 * C, early, STARTS[layer])
+        source, pairs = spare[layer % 2], HIGH // 2 - layer - 1
+        for at in range(2 * pairs + 1):
+            low = (layer + at) // 2
+            stored = (c0, c1, c2, c3, c4)[low // 2][layer, low % 2]
+            if (layer + at) % 2:
+                stored = mixed(stored, (c0, c1, c2, c3, c4)[(low + 1) // 2][layer, (low + 1) % 2])
+            put(source, at // 2 + at % 2 * ODD, stored)
+        parts = [source[:, at * 128 : (at + pairs) * 128] for at in (0, ODD, 1)]
+        early[:, STARTS[layer] * 64 : STARTS[layer + 1] * 64] = jnp.dot(
+            weight[layer, 0 : 2 * C, 0:TAPS], jnp.concatenate(parts, axis=0), preferred_element_type=F32
+        )
+    for row in range(HIGH):
+        prepare(0, 0, row, act[0, row])
 
     behind = None
     for layer in range(LAYERS):
@@ -164,6 +231,9 @@
         for group in range(GROUPS):
 
             multiply(layer, taps[group], layer, rows, 3 * C, sums[group], 0)
+            if layer == 0 and group + 1 < GROUPS:
+                for row in range(HIGH):
+                    prepare(0, group + 1, row, act[group + 1, row])
             if behind is not None:
                 for row in range(behind[0] + 1, HIGH - behind[0] - 1):
                     finish(*behind, row)
@@ -195,17 +265,6 @@
     return lax.ppermute(block, axes, route)
 
 
-def mended(block):
-    sections, cols = lax.axis_size("section"), lax.axis_size("col")
-    last = (sections - 1) * cols
-    route = [(i, i + 1) for i in range(cols - 1)] + [(last + i + 1, last + i) for i in range(cols - 1)]
-    beyond = lax.ppermute(block, ("section", "col"), route)
-    section = lax.axis_index("section")
-    column = jnp.arange(128, dtype=jnp.int32) % WIN
-    ends = (section == 0) & (column < HALO) | (section == sections - 1) & (column >= WIN - HALO)
-    return jnp.where(ends, beyond, block)
-
-
 def vmem(size):
     return pltpu.CompilerParams(vmem_limit_bytes=size << 20)
 
@@ -218,18 +277,34 @@
 
     mine = pl.pallas_call(
         weights_kernel,
-        in_specs=[SMEM] + [VMEM] * 3,
+        in_specs=[SMEM] + [pl.BlockSpec(memory_space=pltpu.HBM)] * 3,
         out_shape=jax.ShapeDtypeStruct((HALF, WIDE), BF16),
         out_specs=VMEM,
-        scratch_shapes=[pltpu.VMEM((3 * C, WIDE), BF16)],
+        scratch_shapes=[
+            pltpu.VMEM((3, TAPS, C), BF16),
+            pltpu.VMEM((1, C), F32),
+            pltpu.VMEM((1, C), F32),
+            pltpu.VMEM((3 * C, WIDE), BF16),
+            pltpu.SemaphoreType.DMA((3,)),
+        ],
         compiler_params=vmem(32),
         name="weights",
     )(place, conv_weight.reshape(3, TAPS, C), norm_gain, conv_bias)
     gathered = lax.all_gather(mine, ("section", "core")).reshape(LAYERS, 3 * C, WIDE)
 
+    right, left = pl.pallas_call(
+        edges_kernel,
+        in_specs=[VMEM] * 2,
+        out_shape=[jax.ShapeDtypeStruct((4, C, 128), BF16)] * 2,
+        out_specs=[VMEM] * 2,
+        compiler_params=vmem(32),
+        name="edges",
+    )(features, cached[0])
+    before = along(right, "col", 1)
+    after = along(left, "col", -1)
     own, spread = pl.pallas_call(
         windows_kernel,
-        in_specs=[SMEM] + [VMEM] * 2,
+        in_specs=[SMEM] + [VMEM] * 4,
         out_shape=[
             jax.ShapeDtypeStruct((GROUPS, ROWS, C, 128), BF16),
             jax.ShapeDtypeStruct((LAYERS, 2, C, 128), BF16),
@@ -237,14 +312,14 @@
         out_specs=[VMEM] * 2,
         compiler_params=vmem(32),
         name="windows",
-    )(place, features, cached[0])
-    stored = mended(lax.all_to_all(spread, "section", 0, 0, tiled=True))
-    own = mended(own)
-    steps = (2, 1, -1, -2)
+    )(place, features, cached[0], before, after)
+    stored = lax.all_to_all(spread, "section", 0, 0, tiled=True)
+    steps = (1, -1, 2, -2)
     f = [along(own, ("x", "core"), d) for d in steps]
+    stored, *f = lax.optimization_barrier((stored, *f))
     c = [along(stored[0 : LAYERS // 2] if abs(d) == 2 else stored, ("x", "core"), d) for d in steps]
-    f = [f[0], f[1], own, f[2], f[3]]
-    c = [c[0], c[1], stored, c[2], c[3]]
+    f = [f[2], f[0], own, f[1], f[3]]
+    c = [c[2], c[0], stored, c[1], c[3]]
 
     at_row = row * ROWS - HALO + jnp.arange(HIGH, dtype=jnp.int32)[:, None, None]
     at_col = col * COLS + section * OWN - HALO + jnp.arange(128, dtype=jnp.int32)[None, None, :] % WIN
@@ -262,7 +337,7 @@
             pltpu.VMEM((GROUPS, HIGH, C, 128), BF16),
             *[pltpu.VMEM((3 * C, HIGH * 128), BF16)] * GROUPS,
             *[pltpu.VMEM((3 * C, (HIGH - 2) * 128), F32)] * GROUPS,
-            pltpu.VMEM((2 * C, STARTS[LAYERS] * 128), F32),
+            pltpu.VMEM((2 * C, STARTS[LAYERS] * 64), F32),
             pltpu.VMEM((LAYERS, C, 128), F32),
             pltpu.VMEM((LAYERS, C, 128), F32),
             pltpu.VMEM((LAYERS, 3 * C, WIDE), BF16),

time: 158 us -> 154 us (0.975)
  the two profiles are of different devices: /device:TPU:199 before, /device:TPU:196 now
where the time goes in v3:
time: 154 us
  Pallas kernels  44.6 us (29%)
  blocking collectives  37.1 us (24%)
  starting transfers between devices  34.9 us (23%)
  waiting for transfers between devices  18.5 us (12%)
  between operations  13.7 us (9%)
  local copies, waits for them, and re-layouts  4.32 us (3%)
    all_to_all x1, blocking collectives, body(): parts = lax.all_to_all(packed, 'section', 0, 0, tiled=True)  37.1 us
    pallas_call x1, Pallas kernels, body(): pl.pallas_call(blocks_kernel, in_specs=[VMEM] * 11 + [pl.BlockSpec(memory...  36.8 us
    ppermute x10, starting transfers between devices, along(): return lax.ppermute(block, axes, route)  27.9 us
    ppermute x10, waiting for transfers between devices, along(): return lax.ppermute(block, axes, route)  16.6 us
    all_to_all x1, starting transfers between devices, body(): stored = lax.all_to_all(spread, 'section', 0, 0, tiled=True)  6.98 us
    unnamed x30, local copies, waits for them, and re-layouts  4.31 us
  transfers between devices with their start and end apart: 12, of which 8 were waited for; matrix products, arithmetic and copies ran while one was open for 0% of the time, Pallas kernels for 2%

profile of v3, /device:TPU:196, one launch (start us, length us, event | category | flops | bytes accessed | tf_op | source)
XLA Modules:
  0.0 153.8 jit_solution(5278873389021569421)
XLA Ops:
  6.6 1.2 copy-done.2
  7.8 0.7 copy-done.3
  8.4 0.7 copy-done.4
  9.1 1.9 %weights.1 = bf16[144,896]{1,0:T(8,128)(2,1)} custom-call(s32[2]{0:T(128)S(1)} %pad_add_fusion.place, bf16[3,864,96]{2,1,0:T(8,128)(2,1)S(1)} %bitcast.8, f32[1,96]{1,0:T(1,128)S(1)} %copy-done.3, f32[1,96]{1,0:T(1,128)S(1)} %copy-done.4), custom_call_target="tpu_custom_call" | custom-call | tf_op jit(solution)/shard_map/weights/pallas_call | solution.py:278
  11.1 0.9 copy-done.1
  12.0 0.7 edges.1
  12.8 5.5 %collective-permute-start = (bf16[4,96,128]{2,1,0:T(8,128)(2,1)S(1)}, bf16[4,96,128]{2,1,0:T(8,128)(2,1)S(1)}, u32[]{:S(2)}, u32[]{:S(2)}) collective-permute-start(bf16[4,96,128]{2,1,0:T(8,128)(2,1)S(1)} %get-tuple-element.14), channel_id=1, source_target_pairs={{0,1},{1,2},{2,3},{3,4},{4,5},{5,6},{6,7},{8,9},{9,10},{10,11},{11... | collective-permute-start | bytes 294920 | tf_op jit(solution)/shard_map/ppermute | solution.py:265
  18.2 1.9 %collective-permute-start.1 = (bf16[4,96,128]{2,1,0:T(8,128)(2,1)S(1)}, bf16[4,96,128]{2,1,0:T(8,128)(2,1)S(1)}, u32[]{:S(2)}, u32[]{:S(2)}) collective-permute-start(bf16[4,96,128]{2,1,0:T(8,128)(2,1)S(1)} %get-tuple-element.15), channel_id=1, source_target_pairs={{1,0},{2,1},{3,2},{4,3},{5,4},{6,5},{7,6},{9,8},{10,9},{11,10},{12... | collective-permute-start | bytes 294920 | tf_op jit(solution)/shard_map/ppermute | solution.py:265
  20.2 0.3 collective-permute-done.before
  20.4 5.5 %collective-permute-done.1.after = bf16[4,96,128]{2,1,0:T(8,128)(2,1)S(1)} collective-permute-done((bf16[4,96,128]{2,1,0:T(8,128)(2,1)S(1)}, bf16[4,96,128]{2,1,0:T(8,128)(2,1)S(1)}, u32[]{:S(2)}, u32[]{:S(2)}) %collective-permute-start.1) | collective-permute-done | bytes 98336 | tf_op jit(solution)/shard_map/ppermute | solution.py:265
  26.0 2.2 %windows.1 = (bf16[3,4,96,128]{3,2,1,0:T(8,128)(2,1)S(1)}, bf16[8,2,96,128]{3,2,1,0:T(8,128)(2,1)}) custom-call(s32[2]{0:T(128)S(1)} %pad_add_fusion.place, bf16[12,4,96,128]{3,2,1,0:T(8,128)(2,1)S(1)} %copy-done, bf16[2,4,96,128]{3,2,1,0:T(8,128)(2,1)S(1)} %bitcast.7, bf16[4,96,128]{2,1,0:T(8,128)(2,1)S(1)} %collective-permute-done.before, ...), custom_call_target="tpu_custom_call" | custom-call | tf_op jit(solution)/shard_map/windows/pallas_call | solution.py:305
  28.2 7.0 %all-to-all-start = ((bf16[8,2,96,128]{3,2,1,0:T(8,128)(2,1)}), bf16[8,2,96,128]{3,2,1,0:T(8,128)(2,1)S(1)}, u32[]{:S(2)}, u32[]{:S(2)}) async-start(bf16[8,2,96,128]{3,2,1,0:T(8,128)(2,1)} %get-tuple-element.16), calls=%async_computation | async-start | bytes 786432 | tf_op jit(solution)/shard_map/all_to_all | solution.py:316
  35.2 2.4 %collective-permute-start.5 = (bf16[3,4,96,128]{3,2,1,0:T(8,128)(2,1)S(1)}, bf16[3,4,96,128]{3,2,1,0:T(8,128)(2,1)S(1)}, u32[]{:S(2)}, u32[]{:S(2)}) collective-permute-start(bf16[3,4,96,128]{3,2,1,0:T(8,128)(2,1)S(1)} %get-tuple-element.17.f2), channel_id=1, source_target_pairs={{16,0},{24,8},{32,16},{40,24},{48,32},{56,40},{17,1},{25,9},{33,17... | collective-permute-start | bytes 884744 | tf_op jit(solution)/shard_map/ppermute | solution.py:265
  37.6 3.4 %collective-permute-start.4 = (bf16[3,4,96,128]{3,2,1,0:T(8,128)(2,1)S(1)}, bf16[3,4,96,128]{3,2,1,0:T(8,128)(2,1)S(1)}, u32[]{:S(2)}, u32[]{:S(2)}) collective-permute-start(bf16[3,4,96,128]{3,2,1,0:T(8,128)(2,1)S(1)} %get-tuple-element.17.f2), channel_id=1, source_target_pairs={{0,16},{8,24},{16,32},{24,40},{32,48},{40,56},{1,17},{9,25},{17,33... | collective-permute-start | bytes 884744 | tf_op jit(solution)/shard_map/ppermute | solution.py:265
  41.0 1.9 %collective-permute-start.3 = (bf16[3,4,96,128]{3,2,1,0:T(8,128)(2,1)S(1)}, bf16[3,4,96,128]{3,2,1,0:T(8,128)(2,1)S(1)}, u32[]{:S(2)}, u32[]{:S(2)}) collective-permute-start(bf16[3,4,96,128]{3,2,1,0:T(8,128)(2,1)S(1)} %get-tuple-element.17.f2), channel_id=1, source_target_pairs={{8,0},{16,8},{24,16},{32,24},{40,32},{48,40},{56,48},{9,1},{17,9},... | collective-permute-start | bytes 884744 | tf_op jit(solution)/shard_map/ppermute | solution.py:265
  43.0 2.4 %collective-permute-start.2 = (bf16[3,4,96,128]{3,2,1,0:T(8,128)(2,1)S(1)}, bf16[3,4,96,128]{3,2,1,0:T(8,128)(2,1)S(1)}, u32[]{:S(2)}, u32[]{:S(2)}) collective-permute-start(bf16[3,4,96,128]{3,2,1,0:T(8,128)(2,1)S(1)} %get-tuple-element.17.f2), channel_id=1, source_target_pairs={{0,8},{8,16},{16,24},{24,32},{32,40},{40,48},{48,56},{1,9},{9,17},... | collective-permute-start | bytes 884744 | tf_op jit(solution)/shard_map/ppermute | solution.py:265
  45.4 0.9 collective-permute-done.4.f0
  46.3 0.9 collective-permute-done.3.f3
  47.2 3.8 %collective-permute-done.2.f1 = bf16[3,4,96,128]{3,2,1,0:T(8,128)(2,1)S(1)} collective-permute-done((bf16[3,4,96,128]{3,2,1,0:T(8,128)(2,1)S(1)}, bf16[3,4,96,128]{3,2,1,0:T(8,128)(2,1)S(1)}, u32[]{:S(2)}, u32[]{:S(2)}) %collective-permute-start.2) | collective-permute-done | bytes 294944 | tf_op jit(solution)/shard_map/ppermute | solution.py:265
  51.0 1.9 %all-to-all-done.c2 = bf16[8,2,96,128]{3,2,1,0:T(8,128)(2,1)S(1)} async-done(((bf16[8,2,96,128]{3,2,1,0:T(8,128)(2,1)}), bf16[8,2,96,128]{3,2,1,0:T(8,128)(2,1)S(1)}, u32[]{:S(2)}, u32[]{:S(2)}) %all-to-all-start) | async-done | bytes 393248 | tf_op jit(solution)/shard_map/all_to_all | solution.py:316
  52.9 1.9 %collective-permute-start.8 = (bf16[8,2,96,128]{3,2,1,0:T(8,128)(2,1)S(1)}, bf16[8,2,96,128]{3,2,1,0:T(8,128)(2,1)S(1)}, u32[]{:S(2)}, u32[]{:S(2)}) collective-permute-start(bf16[8,2,96,128]{3,2,1,0:T(8,128)(2,1)S(1)} %all-to-all-done.c2), channel_id=1, source_target_pairs={{8,0},{16,8},{24,16},{32,24},{40,32},{48,40},{56,48},{9,1},{17,9},... | collective-permute-start | bytes 1179656 | tf_op jit(solution)/shard_map/ppermute | solution.py:265
  54.8 2.4 %collective-permute-start.7 = (bf16[8,2,96,128]{3,2,1,0:T(8,128)(2,1)S(1)}, bf16[8,2,96,128]{3,2,1,0:T(8,128)(2,1)S(1)}, u32[]{:S(2)}, u32[]{:S(2)}) collective-permute-start(bf16[8,2,96,128]{3,2,1,0:T(8,128)(2,1)S(1)} %all-to-all-done.c2), channel_id=1, source_target_pairs={{0,8},{8,16},{16,24},{24,32},{32,40},{40,48},{48,56},{1,9},{9,17},... | collective-permute-start | bytes 1179656 | tf_op jit(solution)/shard_map/ppermute | solution.py:265
  57.3 2.4 %collective-permute-start.9 = (bf16[4,2,96,128]{3,2,1,0:T(8,128)(2,1)S(1)}, bf16[4,2,96,128]{3,2,1,0:T(8,128)(2,1)S(1)}, u32[]{:S(2)}, u32[]{:S(2)}) collective-permute-start(bf16[4,2,96,128]{3,2,1,0:T(8,128)(2,1)S(1)} %slice.4), channel_id=1, source_target_pairs={{16,0},{24,8},{32,16},{40,24},{48,32},{56,40},{17,1},{25,9},{33,17... | collective-permute-start | bytes 589832 | tf_op jit(solution)/shard_map/ppermute | solution.py:265
  59.7 3.6 %collective-permute-start.6 = (bf16[4,2,96,128]{3,2,1,0:T(8,128)(2,1)S(1)}, bf16[4,2,96,128]{3,2,1,0:T(8,128)(2,1)S(1)}, u32[]{:S(2)}, u32[]{:S(2)}) collective-permute-start(bf16[4,2,96,128]{3,2,1,0:T(8,128)(2,1)S(1)} %slice.4), channel_id=1, source_target_pairs={{0,16},{8,24},{16,32},{24,40},{32,48},{40,56},{1,17},{9,25},{17,33... | collective-permute-start | bytes 589832 | tf_op jit(solution)/shard_map/ppermute | solution.py:265
  63.3 0.7 and_convert_fusion.inside
  64.0 2.8 %collective-permute-done.9.c4 = bf16[4,2,96,128]{3,2,1,0:T(8,128)(2,1)S(1)} collective-permute-done((bf16[4,2,96,128]{3,2,1,0:T(8,128)(2,1)S(1)}, bf16[4,2,96,128]{3,2,1,0:T(8,128)(2,1)S(1)}, u32[]{:S(2)}, u32[]{:S(2)}) %collective-permute-start.9) | collective-permute-done | bytes 196640 | tf_op jit(solution)/shard_map/ppermute | solution.py:265
  66.8 2.4 %collective-permute-done.6.c0 = bf16[4,2,96,128]{3,2,1,0:T(8,128)(2,1)S(1)} collective-permute-done((bf16[4,2,96,128]{3,2,1,0:T(8,128)(2,1)S(1)}, bf16[4,2,96,128]{3,2,1,0:T(8,128)(2,1)S(1)}, u32[]{:S(2)}, u32[]{:S(2)}) %collective-permute-start.6) | collective-permute-done | bytes 196640 | tf_op jit(solution)/shard_map/ppermute | solution.py:265
  69.4 0.6 copy-done.14
  69.9 0.2 copy-done.7
  70.2 36.8 %blocks.1 = bf16[8,6,96,128]{3,2,1,0:T(8,128)(2,1)} custom-call(bf16[3,4,96,128]{3,2,1,0:T(8,128)(2,1)} %copy-done.10, bf16[3,4,96,128]{3,2,1,0:T(8,128)(2,1)} %copy-done.12, bf16[3,4,96,128]{3,2,1,0:T(8,128)(2,1)} %copy-done.5, bf16[3,4,96,128]{3,2,1,0:T(8,128)(2,1)} %copy-done.11, bf16[3,4,96,128]{3,2,1,0:T(8,128)(2,1)} %copy-done.9, ...), custom_call_target="tpu_custom_call" | custom-call | flops 17999998976 | bytes 8000000 | tf_op jit(solution)/shard_map/blocks/pallas_call | solution.py:331
  107.1 37.1 %all_to_all.10.parts = bf16[8,6,96,128]{3,2,1,0:T(8,128)(2,1)S(1)} all-to-all(bf16[8,6,96,128]{3,2,1,0:T(8,128)(2,1)} %blocks.1), channel_id=1, replica_groups=mesh['section'=8,'x'=4,'core'=2,'col'=8] {'section'}, dimensions={0} | all-to-all | bytes 2359296 | tf_op jit(solution)/shard_map/all_to_all | solution.py:351
  144.1 2.9 %join.1 = bf16[12,4,96,128]{3,2,1,0:T(8,128)(2,1)} custom-call(bf16[8,6,96,128]{3,2,1,0:T(8,128)(2,1)S(1)} %all_to_all.10.parts), custom_call_target="tpu_custom_call" | custom-call | tf_op jit(solution)/shard_map/join/pallas_call | solution.py:352
  (34 shorter events, 0.3 us)
Async XLA Ops:
  6.5 4.5 %copy-start = (bf16[12,4,96,128]{3,2,1,0:T(8,128)(2,1)S(1)}, bf16[12,4,96,128]{3,2,1,0:T(8,128)(2,1)}, u32[]{:S(2)}) copy-start(bf16[12,4,96,128]{3,2,1,0:T(8,128)(2,1)} %features.3) | copy-start | bytes 3538948
  6.5 62.8 %all-gather.3.cloned.1.call-start = ((), (), s32[]{:S(2)}) async-start(), calls=%async_computation.2 | async-start | bytes 4386816 | tf_op jit(solution)/shard_map/all_gather | solution.py:293
  6.6 1.2 copy-start.2
  7.8 0.7 copy-start.3
  8.4 0.7 copy-start.4
  11.1 0.9 copy-start.1
  12.8 7.7 %collective-permute-start = (bf16[4,96,128]{2,1,0:T(8,128)(2,1)S(1)}, bf16[4,96,128]{2,1,0:T(8,128)(2,1)S(1)}, u32[]{:S(2)}, u32[]{:S(2)}) collective-permute-start(bf16[4,96,128]{2,1,0:T(8,128)(2,1)S(1)} %get-tuple-element.14), channel_id=1, source_target_pairs={{0,1},{1,2},{2,3},{3,4},{4,5},{5,6},{6,7},{8,9},{9,10},{10,11},{11... | collective-permute-start | bytes 294920 | tf_op jit(solution)/shard_map/ppermute | solution.py:265
  18.2 7.7 %collective-permute-start.1 = (bf16[4,96,128]{2,1,0:T(8,128)(2,1)S(1)}, bf16[4,96,128]{2,1,0:T(8,128)(2,1)S(1)}, u32[]{:S(2)}, u32[]{:S(2)}) collective-permute-start(bf16[4,96,128]{2,1,0:T(8,128)(2,1)S(1)} %get-tuple-element.15), channel_id=1, source_target_pairs={{1,0},{2,1},{3,2},{4,3},{5,4},{6,5},{7,6},{9,8},{10,9},{11,10},{12... | collective-permute-start | bytes 294920 | tf_op jit(solution)/shard_map/ppermute | solution.py:265
  28.2 41.1 %copy-start.5 = (bf16[3,4,96,128]{3,2,1,0:T(8,128)(2,1)}, bf16[3,4,96,128]{3,2,1,0:T(8,128)(2,1)S(1)}, u32[]{:S(2)}) copy-start(bf16[3,4,96,128]{3,2,1,0:T(8,128)(2,1)S(1)} %get-tuple-element.17.f2) | copy-start | bytes 884740
  28.2 24.7 %all-to-all-start = ((bf16[8,2,96,128]{3,2,1,0:T(8,128)(2,1)}), bf16[8,2,96,128]{3,2,1,0:T(8,128)(2,1)S(1)}, u32[]{:S(2)}, u32[]{:S(2)}) async-start(bf16[8,2,96,128]{3,2,1,0:T(8,128)(2,1)} %get-tuple-element.16), calls=%async_computation | async-start | bytes 786432 | tf_op jit(solution)/shard_map/all_to_all | solution.py:316
  35.2 10.2 %collective-permute-start.5 = (bf16[3,4,96,128]{3,2,1,0:T(8,128)(2,1)S(1)}, bf16[3,4,96,128]{3,2,1,0:T(8,128)(2,1)S(1)}, u32[]{:S(2)}, u32[]{:S(2)}) collective-permute-start(bf16[3,4,96,128]{3,2,1,0:T(8,128)(2,1)S(1)} %get-tuple-element.17.f2), channel_id=1, source_target_pairs={{16,0},{24,8},{32,16},{40,24},{48,32},{56,40},{17,1},{25,9},{33,17... | collective-permute-start | bytes 884744 | tf_op jit(solution)/shard_map/ppermute | solution.py:265
  37.6 8.7 %collective-permute-start.4 = (bf16[3,4,96,128]{3,2,1,0:T(8,128)(2,1)S(1)}, bf16[3,4,96,128]{3,2,1,0:T(8,128)(2,1)S(1)}, u32[]{:S(2)}, u32[]{:S(2)}) collective-permute-start(bf16[3,4,96,128]{3,2,1,0:T(8,128)(2,1)S(1)} %get-tuple-element.17.f2), channel_id=1, source_target_pairs={{0,16},{8,24},{16,32},{24,40},{32,48},{40,56},{1,17},{9,25},{17,33... | collective-permute-start | bytes 884744 | tf_op jit(solution)/shard_map/ppermute | solution.py:265
  41.0 6.1 %collective-permute-start.3 = (bf16[3,4,96,128]{3,2,1,0:T(8,128)(2,1)S(1)}, bf16[3,4,96,128]{3,2,1,0:T(8,128)(2,1)S(1)}, u32[]{:S(2)}, u32[]{:S(2)}) collective-permute-start(bf16[3,4,96,128]{3,2,1,0:T(8,128)(2,1)S(1)} %get-tuple-element.17.f2), channel_id=1, source_target_pairs={{8,0},{16,8},{24,16},{32,24},{40,32},{48,40},{56,48},{9,1},{17,9},... | collective-permute-start | bytes 884744 | tf_op jit(solution)/shard_map/ppermute | solution.py:265
  43.0 8.0 %collective-permute-start.2 = (bf16[3,4,96,128]{3,2,1,0:T(8,128)(2,1)S(1)}, bf16[3,4,96,128]{3,2,1,0:T(8,128)(2,1)S(1)}, u32[]{:S(2)}, u32[]{:S(2)}) collective-permute-start(bf16[3,4,96,128]{3,2,1,0:T(8,128)(2,1)S(1)} %get-tuple-element.17.f2), channel_id=1, source_target_pairs={{0,8},{8,16},{16,24},{24,32},{32,40},{40,48},{48,56},{1,9},{9,17},... | collective-permute-start | bytes 884744 | tf_op jit(solution)/shard_map/ppermute | solution.py:265
  45.4 23.9 %copy-start.9 = (bf16[3,4,96,128]{3,2,1,0:T(8,128)(2,1)}, bf16[3,4,96,128]{3,2,1,0:T(8,128)(2,1)S(1)}, u32[]{:S(2)}) copy-start(bf16[3,4,96,128]{3,2,1,0:T(8,128)(2,1)S(1)} %collective-permute-done.5.f4) | copy-start | bytes 884740
  46.3 23.0 %copy-start.10 = (bf16[3,4,96,128]{3,2,1,0:T(8,128)(2,1)}, bf16[3,4,96,128]{3,2,1,0:T(8,128)(2,1)S(1)}, u32[]{:S(2)}) copy-start(bf16[3,4,96,128]{3,2,1,0:T(8,128)(2,1)S(1)} %collective-permute-done.4.f0) | copy-start | bytes 884740
  47.2 22.1 %copy-start.11 = (bf16[3,4,96,128]{3,2,1,0:T(8,128)(2,1)}, bf16[3,4,96,128]{3,2,1,0:T(8,128)(2,1)S(1)}, u32[]{:S(2)}) copy-start(bf16[3,4,96,128]{3,2,1,0:T(8,128)(2,1)S(1)} %collective-permute-done.3.f3) | copy-start | bytes 884740
  51.0 18.3 %copy-start.12 = (bf16[3,4,96,128]{3,2,1,0:T(8,128)(2,1)}, bf16[3,4,96,128]{3,2,1,0:T(8,128)(2,1)S(1)}, u32[]{:S(2)}) copy-start(bf16[3,4,96,128]{3,2,1,0:T(8,128)(2,1)S(1)} %collective-permute-done.2.f1) | copy-start | bytes 884740
  52.9 16.5 %copy-start.6 = (bf16[8,2,96,128]{3,2,1,0:T(8,128)(2,1)}, bf16[8,2,96,128]{3,2,1,0:T(8,128)(2,1)S(1)}, u32[]{:S(2)}) copy-start(bf16[8,2,96,128]{3,2,1,0:T(8,128)(2,1)S(1)} %all-to-all-done.c2) | copy-start | bytes 1179652
  52.9 16.4 %collective-permute-start.8 = (bf16[8,2,96,128]{3,2,1,0:T(8,128)(2,1)S(1)}, bf16[8,2,96,128]{3,2,1,0:T(8,128)(2,1)S(1)}, u32[]{:S(2)}, u32[]{:S(2)}) collective-permute-start(bf16[8,2,96,128]{3,2,1,0:T(8,128)(2,1)S(1)} %all-to-all-done.c2), channel_id=1, source_target_pairs={{8,0},{16,8},{24,16},{32,24},{40,32},{48,40},{56,48},{9,1},{17,9},... | collective-permute-start | bytes 1179656 | tf_op jit(solution)/shard_map/ppermute | solution.py:265
  54.8 14.5 %collective-permute-start.7 = (bf16[8,2,96,128]{3,2,1,0:T(8,128)(2,1)S(1)}, bf16[8,2,96,128]{3,2,1,0:T(8,128)(2,1)S(1)}, u32[]{:S(2)}, u32[]{:S(2)}) collective-permute-start(bf16[8,2,96,128]{3,2,1,0:T(8,128)(2,1)S(1)} %all-to-all-done.c2), channel_id=1, source_target_pairs={{0,8},{8,16},{16,24},{24,32},{32,40},{40,48},{48,56},{1,9},{9,17},... | collective-permute-start | bytes 1179656 | tf_op jit(solution)/shard_map/ppermute | solution.py:265
  57.3 9.5 %collective-permute-start.9 = (bf16[4,2,96,128]{3,2,1,0:T(8,128)(2,1)S(1)}, bf16[4,2,96,128]{3,2,1,0:T(8,128)(2,1)S(1)}, u32[]{:S(2)}, u32[]{:S(2)}) collective-permute-start(bf16[4,2,96,128]{3,2,1,0:T(8,128)(2,1)S(1)} %slice.4), channel_id=1, source_target_pairs={{16,0},{24,8},{32,16},{40,24},{48,32},{56,40},{17,1},{25,9},{33,17... | collective-permute-start | bytes 589832 | tf_op jit(solution)/shard_map/ppermute | solution.py:265
  59.7 9.6 %collective-permute-start.6 = (bf16[4,2,96,128]{3,2,1,0:T(8,128)(2,1)S(1)}, bf16[4,2,96,128]{3,2,1,0:T(8,128)(2,1)S(1)}, u32[]{:S(2)}, u32[]{:S(2)}) collective-permute-start(bf16[4,2,96,128]{3,2,1,0:T(8,128)(2,1)S(1)} %slice.4), channel_id=1, source_target_pairs={{0,16},{8,24},{16,32},{24,40},{32,48},{40,56},{1,17},{9,25},{17,33... | collective-permute-start | bytes 589832 | tf_op jit(solution)/shard_map/ppermute | solution.py:265
  66.8 2.6 %copy-start.13 = (bf16[4,2,96,128]{3,2,1,0:T(8,128)(2,1)}, bf16[4,2,96,128]{3,2,1,0:T(8,128)(2,1)S(1)}, u32[]{:S(2)}) copy-start(bf16[4,2,96,128]{3,2,1,0:T(8,128)(2,1)S(1)} %collective-permute-done.9.c4) | copy-start | bytes 589828
  69.2 0.7 copy-start.14
  69.2 0.8 copy-start.7
  69.3 1.0 copy-start.8
Sparse Core Ops, SparseCore 0:
  11.2 53.1 all-gather.2

commit v4 on v2

--- a/solution.py
+++ b/solution.py
@@ -30,10 +30,10 @@
     return pltpu.roll(block, size - offset, 1) if offset else block
 
 
-def weights_kernel(place, taps, gain, bias, out, whole):
+def weights_kernel(place, taps, small, out, whole):
     for time in range(3):
         whole[time * C : (time + 1) * C, 0:TAPS] = taps[time].T
-    values = jnp.concatenate([gain[...], bias[...], jnp.zeros((6, C), F32)], axis=0).T
+    values = small[...].T
     high = values.astype(BF16)
     rest = values - high.astype(F32)
     mid = rest.astype(BF16)
@@ -43,7 +43,15 @@
     out[...] = whole[pl.ds(pl.multiple_of(place[1] * HALF, 16), HALF), :]
 
 
-def windows_kernel(place, features, cached, own, spread):
+def gathered_ends(tiles, column):
+    lane = lax.broadcasted_iota(jnp.int32, (C, 128), 1)
+    total = shifted(tiles[0], column)
+    for at in (1, 2, 3):
+        total = jnp.where(lane % WIN >= at * HALO, shifted(tiles[at], column - at * HALO), total)
+    return total
+
+
+def windows_kernel(place, features, cached, own, spread, ends):
     lane = lax.broadcasted_iota(jnp.int32, (C, 128), 1)
     section = place[0]
 
@@ -53,6 +61,13 @@
             total = jnp.where(lane >= slot * WIN, pieces[slot], total)
         return total
 
+    for target in range(LAYERS):
+        for pair in range(ROWS // 2):
+            pieces = []
+            for slot in range(4):
+                tile = cached[slot % 2, 2 * pair + slot // 2]
+                pieces.append(shifted(tile, OWN * target - HALO - slot * WIN))
+            spread[target, pair] = joined(pieces)
     for group in range(GROUPS):
         for row in range(ROWS):
             pieces = []
@@ -60,15 +75,53 @@
                 amount = lax.rem(slot * WIN + HALO - OWN * section + 256, 128)
                 pieces.append(pltpu.roll(features[group * GROUP + slot, row], amount, 1))
             own[group, row] = joined(pieces)
-    for target in range(LAYERS):
-        for pair in range(ROWS // 2):
-            pieces = []
-            for slot in range(4):
-                tile = cached[slot % 2, 2 * pair + slot // 2]
-                pieces.append(shifted(tile, OWN * target - HALO - slot * WIN))
-            spread[target, pair] = joined(pieces)
-
-
+
+    @pl.when(section == 0)
+    def _():
+        for group in range(GROUPS):
+            ends[group] = gathered_ends([own[group, row] for row in range(ROWS)], 0)
+
+    @pl.when(section != 0)
+    def _():
+        for group in range(GROUPS):
+            ends[group] = gathered_ends([own[group, row] for row in range(ROWS)], WIN - HALO)
+
+
+def ends_kernel(place, block, ends):
+    section = place[0]
+
+    @pl.when(section == 0)
+    def _():
+        for at in range(4):
+            ends[at] = gathered_ends([block[at * 4 + i] for i in range(4)], 0)
+
+    @pl.when(section != 0)
+    def _():
+        for at in range(4):
+            ends[at] = gathered_ends([block[at * 4 + i] for i in range(4)], WIN - HALO)
+
+
+def mend_kernel(place, block, beyond, out, *first):
+    lane = lax.broadcasted_iota(jnp.int32, (C, 128), 1) % WIN
+    section = place[0]
+    out[...] = block[...]
+
+    @pl.when(section == 0)
+    def _():
+        for at in range(block.shape[0]):
+            out[at] = jnp.where(lane < HALO, shifted(beyond[at // 4], at % 4 * HALO), block[at])
+
+    @pl.when(section == LAYERS - 1)
+    def _():
+        for at in range(block.shape[0]):
+            piece = shifted(beyond[at // 4], at % 4 * HALO - (WIN - HALO))
+            out[at] = jnp.where(lane >= WIN - HALO, piece, block[at])
+
+    for half in first:
+        half[...] = out[0 : half.shape[0]]
+
+
+ODD = HIGH // 2
 STARTS = [sum(HIGH - 2 * i - 2 for i in range(layer)) for layer in range(LAYERS + 1)]
 HALF = 3 * C // 2
 
@@ -106,11 +159,14 @@
         now = tile(row - (layer + 1))
         cur = sums[group]
         if group:
-            old, before = sums[group - 1], now
+            old_one, old_two = sums[group - 1][C : 2 * C, now], sums[group - 1][0:C, now]
         else:
-            old, before = early, tile(row - (layer + 1) + STARTS[layer])
-        one = jnp.where(lane >= 3 * WIN, old[C : 2 * C, before], cur[C : 2 * C, now])
-        two = jnp.where(lane >= 2 * WIN, old[0:C, before], cur[0:C, now])
+            pair = tile((row - (layer + 1) + STARTS[layer]) // 2)
+            old_one, old_two = early[C : 2 * C, pair], early[0:C, pair]
+            if (row - layer) % 2:
+                old_one, old_two = pltpu.roll(old_one, 64, 1), pltpu.roll(old_two, 64, 1)
+        one = jnp.where(lane >= 3 * WIN, old_one, cur[C : 2 * C, now])
+        two = jnp.where(lane >= 2 * WIN, old_two, cur[0:C, now])
         total = act[group, row].astype(F32) + biases[layer] + cur[2 * C : 3 * C, now]
         total = total + pltpu.roll(one, WIN, 1) + pltpu.roll(two, 2 * WIN, 1)
         stored = total.astype(BF16)
@@ -147,16 +203,23 @@
 
         gains[layer] = 0.5 * column(TAPS)
         biases[layer] = column(TAPS + 1)
-        if layer == 0:
-            for group in range(GROUPS):
-                loop(HIGH, lambda row, group=group: prepare(0, group, row, act[group, row]), 4)
+    def mixed(one, two):
+        return pltpu.roll(jnp.where(lane >= 64, one, two), 64, 1)
 
     for layer in range(LAYERS):
-        source = spare[layer % 2]
-        for row in range(layer, HIGH - layer):
-            stored = (c0, c1, c2, c3, c4)[row // ROWS][layer, row % ROWS // 2]
-            put(source, row, stored if row % 2 else pltpu.roll(stored, 64, 1))
-        multiply(layer, source, layer, HIGH - 2 * layer - 2, 2 * C, early, STARTS[layer])
+        source, pairs = spare[layer % 2], HIGH // 2 - layer - 1
+        for at in range(2 * pairs + 1):
+            low = (layer + at) // 2
+            stored = (c0, c1, c2, c3, c4)[low // 2][layer, low % 2]
+            if (layer + at) % 2:
+                stored = mixed(stored, (c0, c1, c2, c3, c4)[(low + 1) // 2][layer, (low + 1) % 2])
+            put(source, at // 2 + at % 2 * ODD, stored)
+        parts = [source[:, at * 128 : (at + pairs) * 128] for at in (0, ODD, 1)]
+        early[:, STARTS[layer] * 64 : STARTS[layer + 1] * 64] = jnp.dot(
+            weight[layer, 0 : 2 * C, 0:TAPS], jnp.concatenate(parts, axis=0), preferred_element_type=F32
+        )
+    for row in range(HIGH):
+        prepare(0, 0, row, act[0, row])
 
     behind = None
     for layer in range(LAYERS):
@@ -164,6 +227,9 @@
         for group in range(GROUPS):
 
             multiply(layer, taps[group], layer, rows, 3 * C, sums[group], 0)
+            if layer == 0 and group + 1 < GROUPS:
+                for row in range(HIGH):
+                    prepare(0, group + 1, row, act[group + 1, row])
             if behind is not None:
                 for row in range(behind[0] + 1, HIGH - behind[0] - 1):
                     finish(*behind, row)
@@ -195,15 +261,22 @@
     return lax.ppermute(block, axes, route)
 
 
-def mended(block):
+def mended(place, block, ends, halved=False):
     sections, cols = lax.axis_size("section"), lax.axis_size("col")
     last = (sections - 1) * cols
     route = [(i, i + 1) for i in range(cols - 1)] + [(last + i + 1, last + i) for i in range(cols - 1)]
-    beyond = lax.ppermute(block, ("section", "col"), route)
-    section = lax.axis_index("section")
-    column = jnp.arange(128, dtype=jnp.int32) % WIN
-    ends = (section == 0) & (column < HALO) | (section == sections - 1) & (column >= WIN - HALO)
-    return jnp.where(ends, beyond, block)
+    beyond = lax.ppermute(ends, ("section", "col"), route)
+    tiles = block.reshape(-1, C, 128)
+    counts = [tiles.shape[0], tiles.shape[0] // 2][: 1 + halved]
+    whole, *first = pl.pallas_call(
+        mend_kernel,
+        in_specs=[SMEM] + [VMEM] * 2,
+        out_shape=[jax.ShapeDtypeStruct((count, C, 128), BF16) for count in counts],
+        out_specs=[VMEM] * len(counts),
+        compiler_params=vmem(32),
+        name="mend",
+    )(place, tiles, beyond)
+    return whole.reshape(block.shape), *(half.reshape(-1, *block.shape[1:]) for half in first)
 
 
 def vmem(size):
@@ -216,35 +289,47 @@
     col = lax.axis_index("col")
     place = jnp.stack([section, lax.axis_index("core")]).astype(jnp.int32)
 
+    small = jnp.concatenate([norm_gain, conv_bias, jnp.zeros((6, C), F32)], axis=0)
     mine = pl.pallas_call(
         weights_kernel,
-        in_specs=[SMEM] + [VMEM] * 3,
+        in_specs=[SMEM] + [VMEM] * 2,
         out_shape=jax.ShapeDtypeStruct((HALF, WIDE), BF16),
         out_specs=VMEM,
         scratch_shapes=[pltpu.VMEM((3 * C, WIDE), BF16)],
         compiler_params=vmem(32),
         name="weights",
-    )(place, conv_weight.reshape(3, TAPS, C), norm_gain, conv_bias)
+    )(place, conv_weight.reshape(3, TAPS, C), small)
     gathered = lax.all_gather(mine, ("section", "core")).reshape(LAYERS, 3 * C, WIDE)
 
-    own, spread = pl.pallas_call(
+    own, spread, ends = pl.pallas_call(
         windows_kernel,
         in_specs=[SMEM] + [VMEM] * 2,
         out_shape=[
             jax.ShapeDtypeStruct((GROUPS, ROWS, C, 128), BF16),
             jax.ShapeDtypeStruct((LAYERS, 2, C, 128), BF16),
+            jax.ShapeDtypeStruct((GROUPS, C, 128), BF16),
         ],
-        out_specs=[VMEM] * 2,
+        out_specs=[VMEM] * 3,
         compiler_params=vmem(32),
         name="windows",
     )(place, features, cached[0])
-    stored = mended(lax.all_to_all(spread, "section", 0, 0, tiled=True))
-    own = mended(own)
-    steps = (2, 1, -1, -2)
+    stored = lax.all_to_all(spread, "section", 0, 0, tiled=True)
+    (own,) = mended(place, own, ends)
+    steps = (1, -1, 2, -2)
     f = [along(own, ("x", "core"), d) for d in steps]
-    c = [along(stored[0 : LAYERS // 2] if abs(d) == 2 else stored, ("x", "core"), d) for d in steps]
-    f = [f[0], f[1], own, f[2], f[3]]
-    c = [c[0], c[1], stored, c[2], c[3]]
+    stored, *f = lax.optimization_barrier((stored, *f))
+    f = [f[2], f[0], own, f[1], f[3]]
+    ends = pl.pallas_call(
+        ends_kernel,
+        in_specs=[SMEM, VMEM],
+        out_shape=jax.ShapeDtypeStruct((LAYERS // 2, C, 128), BF16),
+        out_specs=VMEM,
+        compiler_params=vmem(32),
+        name="ends",
+    )(place, stored.reshape(2 * LAYERS, C, 128))
+    stored, first = mended(place, stored, ends, True)
+    c = [along(first if abs(d) == 2 else stored, ("x", "core"), d) for d in steps]
+    c = [c[2], c[0], stored, c[1], c[3]]
 
     at_row = row * ROWS - HALO + jnp.arange(HIGH, dtype=jnp.int32)[:, None, None]
     at_col = col * COLS + section * OWN - HALO + jnp.arange(128, dtype=jnp.int32)[None, None, :] % WIN
@@ -262,7 +347,7 @@
             pltpu.VMEM((GROUPS, HIGH, C, 128), BF16),
             *[pltpu.VMEM((3 * C, HIGH * 128), BF16)] * GROUPS,
             *[pltpu.VMEM((3 * C, (HIGH - 2) * 128), F32)] * GROUPS,
-            pltpu.VMEM((2 * C, STARTS[LAYERS] * 128), F32),
+            pltpu.VMEM((2 * C, STARTS[LAYERS] * 64), F32),
             pltpu.VMEM((LAYERS, C, 128), F32),
             pltpu.VMEM((LAYERS, C, 128), F32),
             pltpu.VMEM((LAYERS, 3 * C, WIDE), BF16),

time: 158 us -> 155 us (0.981)
  the two profiles are of different devices: /device:TPU:199 before, /device:TPU:196 now
where the time goes in v4:
time: 155 us; the launch traced here: 154 us
  Pallas kernels  45.7 us (29%)
  starting transfers between devices  38.6 us (25%)
  blocking collectives  36.6 us (24%)
  waiting for transfers between devices  15 us (10%)
  between operations  13.7 us (9%)
  local copies, waits for them, and re-layouts  2.99 us (2%)
  other arithmetic  1.61 us (1%)
    pallas_call x1, Pallas kernels, body(): pl.pallas_call(blocks_kernel, in_specs=[VMEM] * 11 + [pl.BlockSpec(memory...  36.9 us
    all_to_all x1, blocking collectives, body(): parts = lax.all_to_all(packed, 'section', 0, 0, tiled=True)  36.6 us
    ppermute x8, starting transfers between devices, along(): return lax.ppermute(block, axes, route)  20.5 us
    ppermute x2, starting transfers between devices, mended(): beyond = lax.ppermute(ends, ('section', 'col'), route)  11 us
    ppermute x8, waiting for transfers between devices, along(): return lax.ppermute(block, axes, route)  10.9 us
    all_to_all x1, starting transfers between devices, body(): stored = lax.all_to_all(spread, 'section', 0, 0, tiled=True)  7.11 us
    ppermute x2, waiting for transfers between devices, mended(): beyond = lax.ppermute(ends, ('section', 'col'), route)  4.14 us
  transfers between devices with their start and end apart: 12, of which 7 were waited for; matrix products, arithmetic and copies ran while one was open for 0% of the time, Pallas kernels for 3%

profile of v4, /device:TPU:196, one launch (start us, length us, event | category | flops | bytes accessed | tf_op | source)
XLA Modules:
  0.0 154.2 jit_solution(9516464381871562729)
XLA Ops:
  6.7 0.8 maximum_maximum_fusion.small
  7.5 1.1 copy-done.1
  8.6 1.7 %weights.1 = bf16[144,896]{1,0:T(8,128)(2,1)} custom-call(s32[2]{0:T(128)S(1)} %pad_add_fusion.place, bf16[3,864,96]{2,1,0:T(8,128)(2,1)S(1)} %bitcast.13, f32[8,96]{1,0:T(8,128)S(1)} %maximum_maximum_fusion.small), custom_call_target="tpu_custom_call" | custom-call | tf_op jit(solution)/shard_map/weights/pallas_call | solution.py:293
  10.4 0.9 copy-done.3
  11.3 2.2 %windows.1 = (bf16[3,4,96,128]{3,2,1,0:T(8,128)(2,1)S(1)}, bf16[8,2,96,128]{3,2,1,0:T(8,128)(2,1)}, bf16[3,96,128]{2,1,0:T(8,128)(2,1)S(1)}) custom-call(s32[2]{0:T(128)S(1)} %pad_add_fusion.place, bf16[12,4,96,128]{3,2,1,0:T(8,128)(2,1)S(1)} %copy-done, bf16[2,4,96,128]{3,2,1,0:T(8,128)(2,1)S(1)} %bitcast.20), custom_call_target="tpu_custom_call" | custom-call | tf_op jit(solution)/shard_map/windows/pallas_call | solution.py:304
  13.5 7.1 %all-to-all-start = ((bf16[8,2,96,128]{3,2,1,0:T(8,128)(2,1)}), bf16[8,2,96,128]{3,2,1,0:T(8,128)(2,1)S(1)}, u32[]{:S(2)}, u32[]{:S(2)}) async-start(bf16[8,2,96,128]{3,2,1,0:T(8,128)(2,1)} %get-tuple-element.15), calls=%async_computation | async-start | bytes 786432 | tf_op jit(solution)/shard_map/all_to_all | solution.py:316
  20.6 5.5 %collective-permute-start = (bf16[3,96,128]{2,1,0:T(8,128)(2,1)S(1)}, bf16[3,96,128]{2,1,0:T(8,128)(2,1)S(1)}, u32[]{:S(2)}, u32[]{:S(2)}) collective-permute-start(bf16[3,96,128]{2,1,0:T(8,128)(2,1)S(1)} %get-tuple-element.17), channel_id=1, source_target_pairs={{0,1},{1,2},{2,3},{3,4},{4,5},{5,6},{6,7},{449,448},{450,449},{451... | collective-permute-start | bytes 221192 | tf_op jit(solution)/shard_map/ppermute | solution.py:268
  26.0 2.0 %collective-permute-done.beyond = bf16[3,96,128]{2,1,0:T(8,128)(2,1)S(1)} collective-permute-done((bf16[3,96,128]{2,1,0:T(8,128)(2,1)S(1)}, bf16[3,96,128]{2,1,0:T(8,128)(2,1)S(1)}, u32[]{:S(2)}, u32[]{:S(2)}) %collective-permute-start) | collective-permute-done | bytes 73760 | tf_op jit(solution)/shard_map/ppermute | solution.py:268
  28.0 0.7 mend.2
  28.7 2.4 %collective-permute-start.4 = (bf16[3,4,96,128]{3,2,1,0:T(8,128)(2,1)S(1)}, bf16[3,4,96,128]{3,2,1,0:T(8,128)(2,1)S(1)}, u32[]{:S(2)}, u32[]{:S(2)}) collective-permute-start(bf16[3,4,96,128]{3,2,1,0:T(8,128)(2,1)S(1)} %bitcast.14), channel_id=1, source_target_pairs={{16,0},{24,8},{32,16},{40,24},{48,32},{56,40},{17,1},{25,9},{33,17... | collective-permute-start | bytes 884744 | tf_op jit(solution)/shard_map/ppermute | solution.py:261
  31.2 3.4 %collective-permute-start.3 = (bf16[3,4,96,128]{3,2,1,0:T(8,128)(2,1)S(1)}, bf16[3,4,96,128]{3,2,1,0:T(8,128)(2,1)S(1)}, u32[]{:S(2)}, u32[]{:S(2)}) collective-permute-start(bf16[3,4,96,128]{3,2,1,0:T(8,128)(2,1)S(1)} %bitcast.15), channel_id=1, source_target_pairs={{0,16},{8,24},{16,32},{24,40},{32,48},{40,56},{1,17},{9,25},{17,33... | collective-permute-start | bytes 884744 | tf_op jit(solution)/shard_map/ppermute | solution.py:261
  34.6 1.9 %collective-permute-start.2 = (bf16[3,4,96,128]{3,2,1,0:T(8,128)(2,1)S(1)}, bf16[3,4,96,128]{3,2,1,0:T(8,128)(2,1)S(1)}, u32[]{:S(2)}, u32[]{:S(2)}) collective-permute-start(bf16[3,4,96,128]{3,2,1,0:T(8,128)(2,1)S(1)} %bitcast.16), channel_id=1, source_target_pairs={{8,0},{16,8},{24,16},{32,24},{40,32},{48,40},{56,48},{9,1},{17,9},... | collective-permute-start | bytes 884744 | tf_op jit(solution)/shard_map/ppermute | solution.py:261
  36.5 2.4 %collective-permute-start.1 = (bf16[3,4,96,128]{3,2,1,0:T(8,128)(2,1)S(1)}, bf16[3,4,96,128]{3,2,1,0:T(8,128)(2,1)S(1)}, u32[]{:S(2)}, u32[]{:S(2)}) collective-permute-start(bf16[3,4,96,128]{3,2,1,0:T(8,128)(2,1)S(1)} %bitcast.17), channel_id=1, source_target_pairs={{0,8},{8,16},{16,24},{24,32},{32,40},{40,48},{48,56},{1,9},{9,17},... | collective-permute-start | bytes 884744 | tf_op jit(solution)/shard_map/ppermute | solution.py:261
  38.9 1.4 collective-permute-done.3.f0
  40.4 0.3 collective-permute-done.2.f3
  40.7 3.8 %collective-permute-done.1.f1 = bf16[3,4,96,128]{3,2,1,0:T(8,128)(2,1)S(1)} collective-permute-done((bf16[3,4,96,128]{3,2,1,0:T(8,128)(2,1)S(1)}, bf16[3,4,96,128]{3,2,1,0:T(8,128)(2,1)S(1)}, u32[]{:S(2)}, u32[]{:S(2)}) %collective-permute-start.1) | collective-permute-done | bytes 294944 | tf_op jit(solution)/shard_map/ppermute | solution.py:261
  44.6 0.7 ends.1
  45.3 5.5 %collective-permute-start.5 = (bf16[4,96,128]{2,1,0:T(8,128)(2,1)S(1)}, bf16[4,96,128]{2,1,0:T(8,128)(2,1)S(1)}, u32[]{:S(2)}, u32[]{:S(2)}) collective-permute-start(bf16[4,96,128]{2,1,0:T(8,128)(2,1)S(1)} %ends.1), channel_id=1, source_target_pairs={{0,1},{1,2},{2,3},{3,4},{4,5},{5,6},{6,7},{449,448},{450,449},{451... | collective-permute-start | bytes 294920 | tf_op jit(solution)/shard_map/ppermute | solution.py:268
  50.8 2.2 %collective-permute-done.5.beyond = bf16[4,96,128]{2,1,0:T(8,128)(2,1)S(1)} collective-permute-done((bf16[4,96,128]{2,1,0:T(8,128)(2,1)S(1)}, bf16[4,96,128]{2,1,0:T(8,128)(2,1)S(1)}, u32[]{:S(2)}, u32[]{:S(2)}) %collective-permute-start.5) | collective-permute-done | bytes 98336 | tf_op jit(solution)/shard_map/ppermute | solution.py:268
  52.9 0.7 mend.3
  53.7 1.9 %collective-permute-start.8 = (bf16[8,2,96,128]{3,2,1,0:T(8,128)(2,1)S(1)}, bf16[8,2,96,128]{3,2,1,0:T(8,128)(2,1)S(1)}, u32[]{:S(2)}, u32[]{:S(2)}) collective-permute-start(bf16[8,2,96,128]{3,2,1,0:T(8,128)(2,1)S(1)} %bitcast.21), channel_id=1, source_target_pairs={{8,0},{16,8},{24,16},{32,24},{40,32},{48,40},{56,48},{9,1},{17,9},... | collective-permute-start | bytes 1179656 | tf_op jit(solution)/shard_map/ppermute | solution.py:261
  55.6 2.4 %collective-permute-start.7 = (bf16[8,2,96,128]{3,2,1,0:T(8,128)(2,1)S(1)}, bf16[8,2,96,128]{3,2,1,0:T(8,128)(2,1)S(1)}, u32[]{:S(2)}, u32[]{:S(2)}) collective-permute-start(bf16[8,2,96,128]{3,2,1,0:T(8,128)(2,1)S(1)} %bitcast.22), channel_id=1, source_target_pairs={{0,8},{8,16},{16,24},{24,32},{32,40},{40,48},{48,56},{1,9},{9,17},... | collective-permute-start | bytes 1179656 | tf_op jit(solution)/shard_map/ppermute | solution.py:261
  58.1 2.4 %collective-permute-start.9 = (bf16[4,2,96,128]{3,2,1,0:T(8,128)(2,1)S(1)}, bf16[4,2,96,128]{3,2,1,0:T(8,128)(2,1)S(1)}, u32[]{:S(2)}, u32[]{:S(2)}) collective-permute-start(bf16[4,2,96,128]{3,2,1,0:T(8,128)(2,1)S(1)} %bitcast.24), channel_id=1, source_target_pairs={{16,0},{24,8},{32,16},{40,24},{48,32},{56,40},{17,1},{25,9},{33,17... | collective-permute-start | bytes 589832 | tf_op jit(solution)/shard_map/ppermute | solution.py:261
  60.5 3.6 %collective-permute-start.6 = (bf16[4,2,96,128]{3,2,1,0:T(8,128)(2,1)S(1)}, bf16[4,2,96,128]{3,2,1,0:T(8,128)(2,1)S(1)}, u32[]{:S(2)}, u32[]{:S(2)}) collective-permute-start(bf16[4,2,96,128]{3,2,1,0:T(8,128)(2,1)S(1)} %bitcast.25), channel_id=1, source_target_pairs={{0,16},{8,24},{16,32},{24,40},{32,48},{40,56},{1,17},{9,25},{17,33... | collective-permute-start | bytes 589832 | tf_op jit(solution)/shard_map/ppermute | solution.py:261
  64.1 0.7 and_convert_fusion.inside
  64.8 2.0 %collective-permute-done.9.c4 = bf16[4,2,96,128]{3,2,1,0:T(8,128)(2,1)S(1)} collective-permute-done((bf16[4,2,96,128]{3,2,1,0:T(8,128)(2,1)S(1)}, bf16[4,2,96,128]{3,2,1,0:T(8,128)(2,1)S(1)}, u32[]{:S(2)}, u32[]{:S(2)}) %collective-permute-start.9) | collective-permute-done | bytes 196640 | tf_op jit(solution)/shard_map/ppermute | solution.py:261
  66.8 3.3 %collective-permute-done.6.c0 = bf16[4,2,96,128]{3,2,1,0:T(8,128)(2,1)S(1)} collective-permute-done((bf16[4,2,96,128]{3,2,1,0:T(8,128)(2,1)S(1)}, bf16[4,2,96,128]{3,2,1,0:T(8,128)(2,1)S(1)}, u32[]{:S(2)}, u32[]{:S(2)}) %collective-permute-start.6) | collective-permute-done | bytes 196640 | tf_op jit(solution)/shard_map/ppermute | solution.py:261
  70.2 0.6 copy-done.12
  70.7 0.2 copy-done.5
  71.0 36.9 %blocks.1 = bf16[8,6,96,128]{3,2,1,0:T(8,128)(2,1)} custom-call(bf16[3,4,96,128]{3,2,1,0:T(8,128)(2,1)} %copy-done.8, bf16[3,4,96,128]{3,2,1,0:T(8,128)(2,1)} %copy-done.10, bf16[3,4,96,128]{3,2,1,0:T(8,128)(2,1)} %bitcast.18, bf16[3,4,96,128]{3,2,1,0:T(8,128)(2,1)} %copy-done.9, bf16[3,4,96,128]{3,2,1,0:T(8,128)(2,1)} %copy-done.7, ...), custom_call_target="tpu_custom_call" | custom-call | flops 17999998976 | bytes 8000000 | tf_op jit(solution)/shard_map/blocks/pallas_call | solution.py:341
  107.9 36.6 %all_to_all.10.parts = bf16[8,6,96,128]{3,2,1,0:T(8,128)(2,1)S(1)} all-to-all(bf16[8,6,96,128]{3,2,1,0:T(8,128)(2,1)} %blocks.1), channel_id=1, replica_groups=mesh['section'=8,'x'=4,'core'=2,'col'=8] {'section'}, dimensions={0} | all-to-all | bytes 2359296 | tf_op jit(solution)/shard_map/all_to_all | solution.py:361
  144.5 2.9 %join.1 = bf16[12,4,96,128]{3,2,1,0:T(8,128)(2,1)} custom-call(bf16[8,6,96,128]{3,2,1,0:T(8,128)(2,1)S(1)} %all_to_all.10.parts), custom_call_target="tpu_custom_call" | custom-call | tf_op jit(solution)/shard_map/join/pallas_call | solution.py:362
  (34 shorter events, 0.4 us)
Async XLA Ops:
  6.5 3.8 %copy-start = (bf16[12,4,96,128]{3,2,1,0:T(8,128)(2,1)S(1)}, bf16[12,4,96,128]{3,2,1,0:T(8,128)(2,1)}, u32[]{:S(2)}) copy-start(bf16[12,4,96,128]{3,2,1,0:T(8,128)(2,1)} %features.1) | copy-start | bytes 3538948
  6.5 63.6 %all-gather.3.cloned.1.call-start = ((), (), s32[]{:S(2)}) async-start(), calls=%async_computation.2 | async-start | bytes 4386816 | tf_op jit(solution)/shard_map/all_gather | solution.py:302
  7.5 1.1 copy-start.1
  10.3 0.9 copy-start.3
  13.5 31.1 %all-to-all-start = ((bf16[8,2,96,128]{3,2,1,0:T(8,128)(2,1)}), bf16[8,2,96,128]{3,2,1,0:T(8,128)(2,1)S(1)}, u32[]{:S(2)}, u32[]{:S(2)}) async-start(bf16[8,2,96,128]{3,2,1,0:T(8,128)(2,1)} %get-tuple-element.15), calls=%async_computation | async-start | bytes 786432 | tf_op jit(solution)/shard_map/all_to_all | solution.py:316
  20.6 7.4 %collective-permute-start = (bf16[3,96,128]{2,1,0:T(8,128)(2,1)S(1)}, bf16[3,96,128]{2,1,0:T(8,128)(2,1)S(1)}, u32[]{:S(2)}, u32[]{:S(2)}) collective-permute-start(bf16[3,96,128]{2,1,0:T(8,128)(2,1)S(1)} %get-tuple-element.17), channel_id=1, source_target_pairs={{0,1},{1,2},{2,3},{3,4},{4,5},{5,6},{6,7},{449,448},{450,449},{451... | collective-permute-start | bytes 221192 | tf_op jit(solution)/shard_map/ppermute | solution.py:268
  28.7 41.4 %copy-start.2 = (bf16[12,96,128]{2,1,0:T(8,128)(2,1)}, bf16[12,96,128]{2,1,0:T(8,128)(2,1)S(1)}, u32[]{:S(2)}) copy-start(bf16[12,96,128]{2,1,0:T(8,128)(2,1)S(1)} %mend.2) | copy-start | bytes 884740
  28.7 10.2 %collective-permute-start.4 = (bf16[3,4,96,128]{3,2,1,0:T(8,128)(2,1)S(1)}, bf16[3,4,96,128]{3,2,1,0:T(8,128)(2,1)S(1)}, u32[]{:S(2)}, u32[]{:S(2)}) collective-permute-start(bf16[3,4,96,128]{3,2,1,0:T(8,128)(2,1)S(1)} %bitcast.14), channel_id=1, source_target_pairs={{16,0},{24,8},{32,16},{40,24},{48,32},{56,40},{17,1},{25,9},{33,17... | collective-permute-start | bytes 884744 | tf_op jit(solution)/shard_map/ppermute | solution.py:261
  31.2 9.2 %collective-permute-start.3 = (bf16[3,4,96,128]{3,2,1,0:T(8,128)(2,1)S(1)}, bf16[3,4,96,128]{3,2,1,0:T(8,128)(2,1)S(1)}, u32[]{:S(2)}, u32[]{:S(2)}) collective-permute-start(bf16[3,4,96,128]{3,2,1,0:T(8,128)(2,1)S(1)} %bitcast.15), channel_id=1, source_target_pairs={{0,16},{8,24},{16,32},{24,40},{32,48},{40,56},{1,17},{9,25},{17,33... | collective-permute-start | bytes 884744 | tf_op jit(solution)/shard_map/ppermute | solution.py:261
  34.6 6.1 %collective-permute-start.2 = (bf16[3,4,96,128]{3,2,1,0:T(8,128)(2,1)S(1)}, bf16[3,4,96,128]{3,2,1,0:T(8,128)(2,1)S(1)}, u32[]{:S(2)}, u32[]{:S(2)}) collective-permute-start(bf16[3,4,96,128]{3,2,1,0:T(8,128)(2,1)S(1)} %bitcast.16), channel_id=1, source_target_pairs={{8,0},{16,8},{24,16},{32,24},{40,32},{48,40},{56,48},{9,1},{17,9},... | collective-permute-start | bytes 884744 | tf_op jit(solution)/shard_map/ppermute | solution.py:261
  36.5 8.0 %collective-permute-start.1 = (bf16[3,4,96,128]{3,2,1,0:T(8,128)(2,1)S(1)}, bf16[3,4,96,128]{3,2,1,0:T(8,128)(2,1)S(1)}, u32[]{:S(2)}, u32[]{:S(2)}) collective-permute-start(bf16[3,4,96,128]{3,2,1,0:T(8,128)(2,1)S(1)} %bitcast.17), channel_id=1, source_target_pairs={{0,8},{8,16},{16,24},{24,32},{32,40},{40,48},{48,56},{1,9},{9,17},... | collective-permute-start | bytes 884744 | tf_op jit(solution)/shard_map/ppermute | solution.py:261
  38.9 31.2 %copy-start.7 = (bf16[3,4,96,128]{3,2,1,0:T(8,128)(2,1)}, bf16[3,4,96,128]{3,2,1,0:T(8,128)(2,1)S(1)}, u32[]{:S(2)}) copy-start(bf16[3,4,96,128]{3,2,1,0:T(8,128)(2,1)S(1)} %collective-permute-done.4.f4) | copy-start | bytes 884740
  40.4 29.7 %copy-start.8 = (bf16[3,4,96,128]{3,2,1,0:T(8,128)(2,1)}, bf16[3,4,96,128]{3,2,1,0:T(8,128)(2,1)S(1)}, u32[]{:S(2)}) copy-start(bf16[3,4,96,128]{3,2,1,0:T(8,128)(2,1)S(1)} %collective-permute-done.3.f0) | copy-start | bytes 884740
  40.7 29.4 %copy-start.9 = (bf16[3,4,96,128]{3,2,1,0:T(8,128)(2,1)}, bf16[3,4,96,128]{3,2,1,0:T(8,128)(2,1)S(1)}, u32[]{:S(2)}) copy-start(bf16[3,4,96,128]{3,2,1,0:T(8,128)(2,1)S(1)} %collective-permute-done.2.f3) | copy-start | bytes 884740
  44.6 25.6 %copy-start.10 = (bf16[3,4,96,128]{3,2,1,0:T(8,128)(2,1)}, bf16[3,4,96,128]{3,2,1,0:T(8,128)(2,1)S(1)}, u32[]{:S(2)}) copy-start(bf16[3,4,96,128]{3,2,1,0:T(8,128)(2,1)S(1)} %collective-permute-done.1.f1) | copy-start | bytes 884740
  45.3 7.7 %collective-permute-start.5 = (bf16[4,96,128]{2,1,0:T(8,128)(2,1)S(1)}, bf16[4,96,128]{2,1,0:T(8,128)(2,1)S(1)}, u32[]{:S(2)}, u32[]{:S(2)}) collective-permute-start(bf16[4,96,128]{2,1,0:T(8,128)(2,1)S(1)} %ends.1), channel_id=1, source_target_pairs={{0,1},{1,2},{2,3},{3,4},{4,5},{5,6},{6,7},{449,448},{450,449},{451... | collective-permute-start | bytes 294920 | tf_op jit(solution)/shard_map/ppermute | solution.py:268
  53.7 16.5 %copy-start.4 = (bf16[16,96,128]{2,1,0:T(8,128)(2,1)}, bf16[16,96,128]{2,1,0:T(8,128)(2,1)S(1)}, u32[]{:S(2)}) copy-start(bf16[16,96,128]{2,1,0:T(8,128)(2,1)S(1)} %get-tuple-element.24) | copy-start | bytes 1179652
  53.7 16.4 %collective-permute-start.8 = (bf16[8,2,96,128]{3,2,1,0:T(8,128)(2,1)S(1)}, bf16[8,2,96,128]{3,2,1,0:T(8,128)(2,1)S(1)}, u32[]{:S(2)}, u32[]{:S(2)}) collective-permute-start(bf16[8,2,96,128]{3,2,1,0:T(8,128)(2,1)S(1)} %bitcast.21), channel_id=1, source_target_pairs={{8,0},{16,8},{24,16},{32,24},{40,32},{48,40},{56,48},{9,1},{17,9},... | collective-permute-start | bytes 1179656 | tf_op jit(solution)/shard_map/ppermute | solution.py:261
  55.6 14.4 %collective-permute-start.7 = (bf16[8,2,96,128]{3,2,1,0:T(8,128)(2,1)S(1)}, bf16[8,2,96,128]{3,2,1,0:T(8,128)(2,1)S(1)}, u32[]{:S(2)}, u32[]{:S(2)}) collective-permute-start(bf16[8,2,96,128]{3,2,1,0:T(8,128)(2,1)S(1)} %bitcast.22), channel_id=1, source_target_pairs={{0,8},{8,16},{16,24},{24,32},{32,40},{40,48},{48,56},{1,9},{9,17},... | collective-permute-start | bytes 1179656 | tf_op jit(solution)/shard_map/ppermute | solution.py:261
  58.1 8.7 %collective-permute-start.9 = (bf16[4,2,96,128]{3,2,1,0:T(8,128)(2,1)S(1)}, bf16[4,2,96,128]{3,2,1,0:T(8,128)(2,1)S(1)}, u32[]{:S(2)}, u32[]{:S(2)}) collective-permute-start(bf16[4,2,96,128]{3,2,1,0:T(8,128)(2,1)S(1)} %bitcast.24), channel_id=1, source_target_pairs={{16,0},{24,8},{32,16},{40,24},{48,32},{56,40},{17,1},{25,9},{33,17... | collective-permute-start | bytes 589832 | tf_op jit(solution)/shard_map/ppermute | solution.py:261
  60.5 9.5 %collective-permute-start.6 = (bf16[4,2,96,128]{3,2,1,0:T(8,128)(2,1)S(1)}, bf16[4,2,96,128]{3,2,1,0:T(8,128)(2,1)S(1)}, u32[]{:S(2)}, u32[]{:S(2)}) collective-permute-start(bf16[4,2,96,128]{3,2,1,0:T(8,128)(2,1)S(1)} %bitcast.25), channel_id=1, source_target_pairs={{0,16},{8,24},{16,32},{24,40},{32,48},{40,56},{1,17},{9,25},{17,33... | collective-permute-start | bytes 589832 | tf_op jit(solution)/shard_map/ppermute | solution.py:261
  66.8 3.4 %copy-start.11 = (bf16[4,2,96,128]{3,2,1,0:T(8,128)(2,1)}, bf16[4,2,96,128]{3,2,1,0:T(8,128)(2,1)S(1)}, u32[]{:S(2)}) copy-start(bf16[4,2,96,128]{3,2,1,0:T(8,128)(2,1)S(1)} %collective-permute-done.9.c4) | copy-start | bytes 589828
  70.0 0.7 copy-start.12
  70.0 0.9 copy-start.5
  70.1 1.0 copy-start.6
Sparse Core Ops, SparseCore 0:
  10.5 49.2 all-gather.2

commit v5 on v4

--- a/solution.py
+++ b/solution.py
@@ -317,8 +317,8 @@
     (own,) = mended(place, own, ends)
     steps = (1, -1, 2, -2)
     f = [along(own, ("x", "core"), d) for d in steps]
-    stored, *f = lax.optimization_barrier((stored, *f))
-    f = [f[2], f[0], own, f[1], f[3]]
+    stored, *near = lax.optimization_barrier((stored, *f[:2]))
+    f = [f[2], near[0], own, near[1], f[3]]
     ends = pl.pallas_call(
         ends_kernel,
         in_specs=[SMEM, VMEM],

time: 155 us -> 154 us (level)
  the two profiles are of different devices: /device:TPU:196 before, /device:TPU:199 now
where the time goes in v5:
time: 154 us
  Pallas kernels  45.7 us (30%)
  starting transfers between devices  40.2 us (26%)
  blocking collectives  36.1 us (23%)
  between operations  13.7 us (9%)
  waiting for transfers between devices  13.4 us (9%)
  local copies, waits for them, and re-layouts  2.99 us (2%)
  other arithmetic  1.61 us (1%)
    pallas_call x1, Pallas kernels, body(): pl.pallas_call(blocks_kernel, in_specs=[VMEM] * 11 + [pl.BlockSpec(memory...  36.8 us
    all_to_all x1, blocking collectives, body(): parts = lax.all_to_all(packed, 'section', 0, 0, tiled=True)  36.1 us
    ppermute x8, starting transfers between devices, along(): return lax.ppermute(block, axes, route)  22.2 us
    ppermute x8, waiting for transfers between devices, along(): return lax.ppermute(block, axes, route)  11.8 us
    ppermute x2, starting transfers between devices, mended(): beyond = lax.ppermute(ends, ('section', 'col'), route)  11.1 us
    all_to_all x1, starting transfers between devices, body(): stored = lax.all_to_all(spread, 'section', 0, 0, tiled=True)  6.83 us
  transfers between devices with their start and end apart: 12, of which 5 were waited for; matrix products, arithmetic and copies ran while one was open for 0% of the time, Pallas kernels for 3%

profile of v5, /device:TPU:199, one launch (start us, length us, event | category | flops | bytes accessed | tf_op | source)
XLA Modules:
  0.0 153.6 jit_solution(17961825390148028651)
XLA Ops:
  6.6 0.1 pad.2.clone
  6.7 0.8 maximum_maximum_fusion.small
  7.5 1.1 copy-done.1
  8.6 1.7 %weights.1 = bf16[144,896]{1,0:T(8,128)(2,1)} custom-call(s32[2]{0:T(128)S(1)} %pad_add_fusion.place, bf16[3,864,96]{2,1,0:T(8,128)(2,1)S(1)} %bitcast.13, f32[8,96]{1,0:T(8,128)S(1)} %maximum_maximum_fusion.small), custom_call_target="tpu_custom_call" | custom-call | tf_op jit(solution)/shard_map/weights/pallas_call | solution.py:293
  10.4 0.9 copy-done.3
  11.3 2.2 %windows.1 = (bf16[3,4,96,128]{3,2,1,0:T(8,128)(2,1)S(1)}, bf16[8,2,96,128]{3,2,1,0:T(8,128)(2,1)}, bf16[3,96,128]{2,1,0:T(8,128)(2,1)S(1)}) custom-call(s32[2]{0:T(128)S(1)} %pad_add_fusion.place, bf16[12,4,96,128]{3,2,1,0:T(8,128)(2,1)S(1)} %copy-done, bf16[2,4,96,128]{3,2,1,0:T(8,128)(2,1)S(1)} %bitcast.20), custom_call_target="tpu_custom_call" | custom-call | tf_op jit(solution)/shard_map/windows/pallas_call | solution.py:304
  13.5 6.8 %all-to-all-start = ((bf16[8,2,96,128]{3,2,1,0:T(8,128)(2,1)}), bf16[8,2,96,128]{3,2,1,0:T(8,128)(2,1)S(1)}, u32[]{:S(2)}, u32[]{:S(2)}) async-start(bf16[8,2,96,128]{3,2,1,0:T(8,128)(2,1)} %get-tuple-element.15), calls=%async_computation | async-start | bytes 786432 | tf_op jit(solution)/shard_map/all_to_all | solution.py:316
  20.3 5.2 %collective-permute-start = (bf16[3,96,128]{2,1,0:T(8,128)(2,1)S(1)}, bf16[3,96,128]{2,1,0:T(8,128)(2,1)S(1)}, u32[]{:S(2)}, u32[]{:S(2)}) collective-permute-start(bf16[3,96,128]{2,1,0:T(8,128)(2,1)S(1)} %get-tuple-element.14), channel_id=1, source_target_pairs={{0,1},{1,2},{2,3},{3,4},{4,5},{5,6},{6,7},{449,448},{450,449},{451... | collective-permute-start | bytes 221192 | tf_op jit(solution)/shard_map/ppermute | solution.py:268
  25.5 1.4 collective-permute-done.beyond
  26.9 0.7 mend.2
  27.6 3.7 %collective-permute-start.3 = (bf16[3,4,96,128]{3,2,1,0:T(8,128)(2,1)S(1)}, bf16[3,4,96,128]{3,2,1,0:T(8,128)(2,1)S(1)}, u32[]{:S(2)}, u32[]{:S(2)}) collective-permute-start(bf16[3,4,96,128]{3,2,1,0:T(8,128)(2,1)S(1)} %bitcast.14), channel_id=1, source_target_pairs={{8,0},{16,8},{24,16},{32,24},{40,32},{48,40},{56,48},{9,1},{17,9},... | collective-permute-start | bytes 884744 | tf_op jit(solution)/shard_map/ppermute | solution.py:261
  31.3 1.3 collective-permute-start.2
  32.6 2.2 %collective-permute-done.2.f1 = bf16[3,4,96,128]{3,2,1,0:T(8,128)(2,1)S(1)} collective-permute-done((bf16[3,4,96,128]{3,2,1,0:T(8,128)(2,1)S(1)}, bf16[3,4,96,128]{3,2,1,0:T(8,128)(2,1)S(1)}, u32[]{:S(2)}, u32[]{:S(2)}) %collective-permute-start.2) | collective-permute-done | bytes 294944 | tf_op jit(solution)/shard_map/ppermute | solution.py:261
  34.8 0.2 all-to-all-done
  35.0 0.7 ends.1
  35.7 5.9 %collective-permute-start.5 = (bf16[4,96,128]{2,1,0:T(8,128)(2,1)S(1)}, bf16[4,96,128]{2,1,0:T(8,128)(2,1)S(1)}, u32[]{:S(2)}, u32[]{:S(2)}) collective-permute-start(bf16[4,96,128]{2,1,0:T(8,128)(2,1)S(1)} %ends.1), channel_id=1, source_target_pairs={{0,1},{1,2},{2,3},{3,4},{4,5},{5,6},{6,7},{449,448},{450,449},{451... | collective-permute-start | bytes 294920 | tf_op jit(solution)/shard_map/ppermute | solution.py:268
  41.6 4.5 %collective-permute-start.4 = (bf16[3,4,96,128]{3,2,1,0:T(8,128)(2,1)S(1)}, bf16[3,4,96,128]{3,2,1,0:T(8,128)(2,1)S(1)}, u32[]{:S(2)}, u32[]{:S(2)}) collective-permute-start(bf16[3,4,96,128]{3,2,1,0:T(8,128)(2,1)S(1)} %bitcast.16), channel_id=1, source_target_pairs={{16,0},{24,8},{32,16},{40,24},{48,32},{56,40},{17,1},{25,9},{33,17... | collective-permute-start | bytes 884744 | tf_op jit(solution)/shard_map/ppermute | solution.py:261
  46.1 0.7 mend.3
  46.8 4.2 %collective-permute-start.8 = (bf16[8,2,96,128]{3,2,1,0:T(8,128)(2,1)S(1)}, bf16[8,2,96,128]{3,2,1,0:T(8,128)(2,1)S(1)}, u32[]{:S(2)}, u32[]{:S(2)}) collective-permute-start(bf16[8,2,96,128]{3,2,1,0:T(8,128)(2,1)S(1)} %bitcast.21), channel_id=1, source_target_pairs={{8,0},{16,8},{24,16},{32,24},{40,32},{48,40},{56,48},{9,1},{17,9},... | collective-permute-start | bytes 1179656 | tf_op jit(solution)/shard_map/ppermute | solution.py:261
  51.0 1.3 collective-permute-start.7
  52.3 1.3 collective-permute-start.1
  53.7 4.5 %collective-permute-start.9 = (bf16[4,2,96,128]{3,2,1,0:T(8,128)(2,1)S(1)}, bf16[4,2,96,128]{3,2,1,0:T(8,128)(2,1)S(1)}, u32[]{:S(2)}, u32[]{:S(2)}) collective-permute-start(bf16[4,2,96,128]{3,2,1,0:T(8,128)(2,1)S(1)} %bitcast.24), channel_id=1, source_target_pairs={{16,0},{24,8},{32,16},{40,24},{48,32},{56,40},{17,1},{25,9},{33,17... | collective-permute-start | bytes 589832 | tf_op jit(solution)/shard_map/ppermute | solution.py:261
  58.2 1.5 collective-permute-start.6
  59.7 0.7 and_convert_fusion.inside
  60.4 6.8 %collective-permute-done.1.f0 = bf16[3,4,96,128]{3,2,1,0:T(8,128)(2,1)S(1)} collective-permute-done((bf16[3,4,96,128]{3,2,1,0:T(8,128)(2,1)S(1)}, bf16[3,4,96,128]{3,2,1,0:T(8,128)(2,1)S(1)}, u32[]{:S(2)}, u32[]{:S(2)}) %collective-permute-start.1) | collective-permute-done | bytes 294944 | tf_op jit(solution)/shard_map/ppermute | solution.py:261
  67.2 2.8 %collective-permute-done.6.c0 = bf16[4,2,96,128]{3,2,1,0:T(8,128)(2,1)S(1)} collective-permute-done((bf16[4,2,96,128]{3,2,1,0:T(8,128)(2,1)S(1)}, bf16[4,2,96,128]{3,2,1,0:T(8,128)(2,1)S(1)}, u32[]{:S(2)}, u32[]{:S(2)}) %collective-permute-start.6) | collective-permute-done | bytes 196640 | tf_op jit(solution)/shard_map/ppermute | solution.py:261
  70.1 0.6 copy-done.12
  70.6 0.2 copy-done.5
  70.8 0.1 copy-done.6
  70.9 36.8 %blocks.1 = bf16[8,6,96,128]{3,2,1,0:T(8,128)(2,1)} custom-call(bf16[3,4,96,128]{3,2,1,0:T(8,128)(2,1)} %copy-done.10, bf16[3,4,96,128]{3,2,1,0:T(8,128)(2,1)} %copy-done.8, bf16[3,4,96,128]{3,2,1,0:T(8,128)(2,1)} %bitcast.18, bf16[3,4,96,128]{3,2,1,0:T(8,128)(2,1)} %copy-done.7, bf16[3,4,96,128]{3,2,1,0:T(8,128)(2,1)} %copy-done.9, ...), custom_call_target="tpu_custom_call" | custom-call | flops 17999998976 | bytes 8000000 | tf_op jit(solution)/shard_map/blocks/pallas_call | solution.py:341
  107.8 36.1 %all_to_all.10.parts = bf16[8,6,96,128]{3,2,1,0:T(8,128)(2,1)S(1)} all-to-all(bf16[8,6,96,128]{3,2,1,0:T(8,128)(2,1)} %blocks.1), channel_id=1, replica_groups=mesh['section'=8,'x'=4,'core'=2,'col'=8] {'section'}, dimensions={0} | all-to-all | bytes 2359296 | tf_op jit(solution)/shard_map/all_to_all | solution.py:361
  143.9 2.9 %join.1 = bf16[12,4,96,128]{3,2,1,0:T(8,128)(2,1)} custom-call(bf16[8,6,96,128]{3,2,1,0:T(8,128)(2,1)S(1)} %all_to_all.10.parts), custom_call_target="tpu_custom_call" | custom-call | tf_op jit(solution)/shard_map/join/pallas_call | solution.py:362
  (34 shorter events, 0.2 us)
Async XLA Ops:
  6.5 3.8 %copy-start = (bf16[12,4,96,128]{3,2,1,0:T(8,128)(2,1)S(1)}, bf16[12,4,96,128]{3,2,1,0:T(8,128)(2,1)}, u32[]{:S(2)}) copy-start(bf16[12,4,96,128]{3,2,1,0:T(8,128)(2,1)} %features.1) | copy-start | bytes 3538948
  6.5 63.5 %all-gather.3.cloned.1.call-start = ((), (), s32[]{:S(2)}) async-start(), calls=%async_computation.2 | async-start | bytes 4386816 | tf_op jit(solution)/shard_map/all_gather | solution.py:302
  7.5 1.1 copy-start.1
  10.3 0.9 copy-start.3
  13.5 21.5 %all-to-all-start = ((bf16[8,2,96,128]{3,2,1,0:T(8,128)(2,1)}), bf16[8,2,96,128]{3,2,1,0:T(8,128)(2,1)S(1)}, u32[]{:S(2)}, u32[]{:S(2)}) async-start(bf16[8,2,96,128]{3,2,1,0:T(8,128)(2,1)} %get-tuple-element.15), calls=%async_computation | async-start | bytes 786432 | tf_op jit(solution)/shard_map/all_to_all | solution.py:316
  20.3 6.6 %collective-permute-start = (bf16[3,96,128]{2,1,0:T(8,128)(2,1)S(1)}, bf16[3,96,128]{2,1,0:T(8,128)(2,1)S(1)}, u32[]{:S(2)}, u32[]{:S(2)}) collective-permute-start(bf16[3,96,128]{2,1,0:T(8,128)(2,1)S(1)} %get-tuple-element.14), channel_id=1, source_target_pairs={{0,1},{1,2},{2,3},{3,4},{4,5},{5,6},{6,7},{449,448},{450,449},{451... | collective-permute-start | bytes 221192 | tf_op jit(solution)/shard_map/ppermute | solution.py:268
  27.6 42.4 %copy-start.2 = (bf16[12,96,128]{2,1,0:T(8,128)(2,1)}, bf16[12,96,128]{2,1,0:T(8,128)(2,1)S(1)}, u32[]{:S(2)}) copy-start(bf16[12,96,128]{2,1,0:T(8,128)(2,1)S(1)} %mend.2) | copy-start | bytes 884740
  27.6 5.0 %collective-permute-start.3 = (bf16[3,4,96,128]{3,2,1,0:T(8,128)(2,1)S(1)}, bf16[3,4,96,128]{3,2,1,0:T(8,128)(2,1)S(1)}, u32[]{:S(2)}, u32[]{:S(2)}) collective-permute-start(bf16[3,4,96,128]{3,2,1,0:T(8,128)(2,1)S(1)} %bitcast.14), channel_id=1, source_target_pairs={{8,0},{16,8},{24,16},{32,24},{40,32},{48,40},{56,48},{9,1},{17,9},... | collective-permute-start | bytes 884744 | tf_op jit(solution)/shard_map/ppermute | solution.py:261
  31.3 3.5 %collective-permute-start.2 = (bf16[3,4,96,128]{3,2,1,0:T(8,128)(2,1)S(1)}, bf16[3,4,96,128]{3,2,1,0:T(8,128)(2,1)S(1)}, u32[]{:S(2)}, u32[]{:S(2)}) collective-permute-start(bf16[3,4,96,128]{3,2,1,0:T(8,128)(2,1)S(1)} %bitcast.15), channel_id=1, source_target_pairs={{0,8},{8,16},{16,24},{24,32},{32,40},{40,48},{48,56},{1,9},{9,17},... | collective-permute-start | bytes 884744 | tf_op jit(solution)/shard_map/ppermute | solution.py:261
  32.6 37.4 %copy-start.7 = (bf16[3,4,96,128]{3,2,1,0:T(8,128)(2,1)}, bf16[3,4,96,128]{3,2,1,0:T(8,128)(2,1)S(1)}, u32[]{:S(2)}) copy-start(bf16[3,4,96,128]{3,2,1,0:T(8,128)(2,1)S(1)} %collective-permute-done.3.f3) | copy-start | bytes 884740
  34.8 35.2 %copy-start.8 = (bf16[3,4,96,128]{3,2,1,0:T(8,128)(2,1)}, bf16[3,4,96,128]{3,2,1,0:T(8,128)(2,1)S(1)}, u32[]{:S(2)}) copy-start(bf16[3,4,96,128]{3,2,1,0:T(8,128)(2,1)S(1)} %collective-permute-done.2.f1) | copy-start | bytes 884740
  35.7 10.4 %collective-permute-start.5 = (bf16[4,96,128]{2,1,0:T(8,128)(2,1)S(1)}, bf16[4,96,128]{2,1,0:T(8,128)(2,1)S(1)}, u32[]{:S(2)}, u32[]{:S(2)}) collective-permute-start(bf16[4,96,128]{2,1,0:T(8,128)(2,1)S(1)} %ends.1), channel_id=1, source_target_pairs={{0,1},{1,2},{2,3},{3,4},{4,5},{5,6},{6,7},{449,448},{450,449},{451... | collective-permute-start | bytes 294920 | tf_op jit(solution)/shard_map/ppermute | solution.py:268
  41.6 16.6 %collective-permute-start.4 = (bf16[3,4,96,128]{3,2,1,0:T(8,128)(2,1)S(1)}, bf16[3,4,96,128]{3,2,1,0:T(8,128)(2,1)S(1)}, u32[]{:S(2)}, u32[]{:S(2)}) collective-permute-start(bf16[3,4,96,128]{3,2,1,0:T(8,128)(2,1)S(1)} %bitcast.16), channel_id=1, source_target_pairs={{16,0},{24,8},{32,16},{40,24},{48,32},{56,40},{17,1},{25,9},{33,17... | collective-permute-start | bytes 884744 | tf_op jit(solution)/shard_map/ppermute | solution.py:261
  46.8 23.2 %copy-start.4 = (bf16[16,96,128]{2,1,0:T(8,128)(2,1)}, bf16[16,96,128]{2,1,0:T(8,128)(2,1)S(1)}, u32[]{:S(2)}) copy-start(bf16[16,96,128]{2,1,0:T(8,128)(2,1)S(1)} %get-tuple-element.20) | copy-start | bytes 1179652
  46.8 23.1 %collective-permute-start.8 = (bf16[8,2,96,128]{3,2,1,0:T(8,128)(2,1)S(1)}, bf16[8,2,96,128]{3,2,1,0:T(8,128)(2,1)S(1)}, u32[]{:S(2)}, u32[]{:S(2)}) collective-permute-start(bf16[8,2,96,128]{3,2,1,0:T(8,128)(2,1)S(1)} %bitcast.21), channel_id=1, source_target_pairs={{8,0},{16,8},{24,16},{32,24},{40,32},{48,40},{56,48},{9,1},{17,9},... | collective-permute-start | bytes 1179656 | tf_op jit(solution)/shard_map/ppermute | solution.py:261
  51.0 18.9 %collective-permute-start.7 = (bf16[8,2,96,128]{3,2,1,0:T(8,128)(2,1)S(1)}, bf16[8,2,96,128]{3,2,1,0:T(8,128)(2,1)S(1)}, u32[]{:S(2)}, u32[]{:S(2)}) collective-permute-start(bf16[8,2,96,128]{3,2,1,0:T(8,128)(2,1)S(1)} %bitcast.22), channel_id=1, source_target_pairs={{0,8},{8,16},{16,24},{24,32},{32,40},{40,48},{48,56},{1,9},{9,17},... | collective-permute-start | bytes 1179656 | tf_op jit(solution)/shard_map/ppermute | solution.py:261
  52.3 14.8 %collective-permute-start.1 = (bf16[3,4,96,128]{3,2,1,0:T(8,128)(2,1)S(1)}, bf16[3,4,96,128]{3,2,1,0:T(8,128)(2,1)S(1)}, u32[]{:S(2)}, u32[]{:S(2)}) collective-permute-start(bf16[3,4,96,128]{3,2,1,0:T(8,128)(2,1)S(1)} %bitcast.17), channel_id=1, source_target_pairs={{0,16},{8,24},{16,32},{24,40},{32,48},{40,56},{1,17},{9,25},{17,33... | collective-permute-start | bytes 884744 | tf_op jit(solution)/shard_map/ppermute | solution.py:261
  53.7 13.5 %collective-permute-start.9 = (bf16[4,2,96,128]{3,2,1,0:T(8,128)(2,1)S(1)}, bf16[4,2,96,128]{3,2,1,0:T(8,128)(2,1)S(1)}, u32[]{:S(2)}, u32[]{:S(2)}) collective-permute-start(bf16[4,2,96,128]{3,2,1,0:T(8,128)(2,1)S(1)} %bitcast.24), channel_id=1, source_target_pairs={{16,0},{24,8},{32,16},{40,24},{48,32},{56,40},{17,1},{25,9},{33,17... | collective-permute-start | bytes 589832 | tf_op jit(solution)/shard_map/ppermute | solution.py:261
  58.2 11.9 %copy-start.9 = (bf16[3,4,96,128]{3,2,1,0:T(8,128)(2,1)}, bf16[3,4,96,128]{3,2,1,0:T(8,128)(2,1)S(1)}, u32[]{:S(2)}) copy-start(bf16[3,4,96,128]{3,2,1,0:T(8,128)(2,1)S(1)} %collective-permute-done.4.f4) | copy-start | bytes 884740
  58.2 11.8 %collective-permute-start.6 = (bf16[4,2,96,128]{3,2,1,0:T(8,128)(2,1)S(1)}, bf16[4,2,96,128]{3,2,1,0:T(8,128)(2,1)S(1)}, u32[]{:S(2)}, u32[]{:S(2)}) collective-permute-start(bf16[4,2,96,128]{3,2,1,0:T(8,128)(2,1)S(1)} %bitcast.25), channel_id=1, source_target_pairs={{0,16},{8,24},{16,32},{24,40},{32,48},{40,56},{1,17},{9,25},{17,33... | collective-permute-start | bytes 589832 | tf_op jit(solution)/shard_map/ppermute | solution.py:261
  67.2 2.9 %copy-start.10 = (bf16[3,4,96,128]{3,2,1,0:T(8,128)(2,1)}, bf16[3,4,96,128]{3,2,1,0:T(8,128)(2,1)S(1)}, u32[]{:S(2)}) copy-start(bf16[3,4,96,128]{3,2,1,0:T(8,128)(2,1)S(1)} %collective-permute-done.1.f0) | copy-start | bytes 884740
  67.2 2.9 %copy-start.11 = (bf16[4,2,96,128]{3,2,1,0:T(8,128)(2,1)}, bf16[4,2,96,128]{3,2,1,0:T(8,128)(2,1)S(1)}, u32[]{:S(2)}) copy-start(bf16[4,2,96,128]{3,2,1,0:T(8,128)(2,1)S(1)} %collective-permute-done.9.c4) | copy-start | bytes 589828
  70.0 0.7 copy-start.12
  70.0 0.9 copy-start.5
  70.0 1.0 copy-start.6
Sparse Core Ops, SparseCore 0:
  10.5 49.1 all-gather.2
